TPU v7x, 256 devices: a whole 4x4x8 slice. The times are simulated.
256 devices in a mesh: lat: 16 (over y, x), tm: 16 (over z, core).
Axes of the slice: x: 4, y: 4, z: 8, core: 2. Of those that a mesh axis runs over, the one named last changes fastest.
Arguments:
- light_field: float32 [2, 1024, 4096], P(None, 'lat', 'tm'), may hold values from -6 to 6
- lateral_phase: float32 [1024], replicated, may hold values from -3.140625 to 3.140625
- spectral_phase: float32 [4096], replicated, may hold values from -3.140625 to 3.140625
- occupation: float32 [128, 1024], P(None, 'lat'), may hold values from -0.5 to 1
- bin_decay: float32 [32], replicated, may hold values from 2e-05 to 0.05
- bin_detune: float32 [32], replicated, may hold values from -0.3 to 0.3
- group_bin: int32 [128], replicated, may hold values from 0 to 31
Outputs:
- output_field: float32 [2, 1024, 4096], P(None, 'lat', 'tm')
All inputs are finite; a program needn't handle non-finite values.
Results may differ from a plain program's by a relative error of at most 0.0003.
Values sent between devices are 32-bit elements; how exact they have to be, the bound alone decides.
No kernel may reach another device: no remote copies, remote signals or barrier semaphores. Data moves between devices by JAX's collectives and lax.ppermute only.
A program may use at most 128 MiB of HBM per device.

v0:
```python
import math

import jax
import jax.numpy as jnp
from jax import lax
from jax.sharding import PartitionSpec as P

STRETCH = 128
STEPS = 2


GAIN_SCALE = 0.5


def carried_in(value, axis, join, neutral):
    count, mine = (lax.axis_size(axis), lax.axis_index(axis))
    pieces = jax.tree.map(lambda part: lax.all_gather(part, axis), value)
    so_far = jax.tree.map(
        lambda part, zero: jnp.full_like(part, 0) + jnp.asarray(zero, part.dtype), value, neutral
    )

    def lap(position, so_far):
        longer = join(so_far, jax.tree.map(lambda part: part[position], pieces))
        return jax.tree.map(lambda new, old: jnp.where(position < mine, new, old), longer, so_far)

    return lax.fori_loop(0, count - 1, lap, so_far)


def complex_einsum(form, left, right):
    exact = lax.Precision.HIGHEST
    real_part = jnp.einsum(form, left[0], right[0], precision=exact) - jnp.einsum(
        form, left[1], right[1], precision=exact
    )
    imag_part = jnp.einsum(form, left[0], right[1], precision=exact) + jnp.einsum(
        form, left[1], right[0], precision=exact
    )
    return (real_part, imag_part)


def complex_times(left, right):
    return (left[0] * right[0] - left[1] * right[1], left[0] * right[1] + left[1] * right[0])


def angle_table(height, breadth, modulus, sign):
    first = jnp.arange(height, dtype=jnp.int32)[:, None]
    second = jnp.arange(breadth, dtype=jnp.int32)[None, :]
    turns = (first * second % modulus).astype(jnp.float32) * (2.0 * math.pi / modulus)
    return (jnp.cos(turns), sign * jnp.sin(turns))


def time_forward(grid, small_table, twiddle, long_table):
    mixed = complex_einsum("ka,rab->rkb", small_table, grid)
    mixed = complex_times(mixed, twiddle)
    return complex_einsum("rkb,bq->rkq", mixed, long_table)


def time_inverse(spectrum, small_table, twiddle, long_table, length):
    mixed = complex_einsum("rkq,qb->rkb", spectrum, long_table)
    mixed = complex_times(mixed, twiddle)
    result = complex_einsum("ak,rkb->rab", small_table, mixed)
    return (result[0] / length, result[1] / length)


def powers(decay_rate, detuning, exponent):
    magnitude = jnp.exp(-decay_rate * exponent)
    phase_angle = detuning * exponent
    return (magnitude * jnp.cos(phase_angle), -magnitude * jnp.sin(phase_angle))


def on_device(
    light_field, lateral_phase, spectral_phase, occupation, bin_decay, bin_detune, group_bin
):
    lat_count = lax.axis_size("lat")
    time_count = lax.axis_size("tm")
    height = light_field.shape[1]
    span = light_field.shape[2]
    lateral_total = height * lat_count
    time_total = span * time_count
    groups = occupation.shape[0]
    slab = height // time_count
    narrow = span // lat_count
    exact = lax.Precision.HIGHEST
    lat_forward = angle_table(lateral_total, lateral_total, lateral_total, -1.0)
    lat_backward = angle_table(lateral_total, lateral_total, lateral_total, 1.0)
    lateral_turn = (jnp.cos(lateral_phase)[:, None], jnp.sin(lateral_phase)[:, None])
    small_back = angle_table(time_count, time_count, time_count, 1.0)
    twiddle_back = angle_table(time_count, span, time_total, 1.0)
    long_back = angle_table(span, span, span, 1.0)
    spectral_grid = spectral_phase.reshape(span, time_count).T
    spectral_turn = (jnp.cos(spectral_grid), jnp.sin(spectral_grid))
    bins = jnp.arange(bin_decay.shape[0], dtype=jnp.int32)
    onehot = (group_bin[:, None] == bins[None, :]).astype(jnp.float32)
    decay_rate = jnp.dot(onehot, bin_decay, precision=exact)
    detuning = jnp.dot(onehot, bin_detune, precision=exact)
    coupling = jnp.sqrt(-jnp.expm1(-2.0 * decay_rate))[:, None] * occupation
    lags = jnp.arange(STRETCH + 1, dtype=jnp.float32)[:, None]
    lag_powers = powers(decay_rate, detuning, lags)
    lag_grid = (
        jnp.arange(STRETCH, dtype=jnp.int32)[:, None]
        - jnp.arange(STRETCH, dtype=jnp.int32)[None, :]
    )
    inside = (lag_grid >= 0)[None]
    clipped = jnp.maximum(lag_grid, 0)
    leading = (lag_powers[0][1:].T, lag_powers[1][1:].T)
    trailing = (lag_powers[0][:STRETCH][::-1], lag_powers[1][:STRETCH][::-1])
    stretch_step = (lag_powers[0][STRETCH][:, None], lag_powers[1][STRETCH][:, None])
    device_step = powers(decay_rate, detuning, jnp.float32(span))
    weight = GAIN_SCALE / math.sqrt(groups)
    small_forward = angle_table(time_count, time_count, time_count, -1.0)
    twiddle_forward = angle_table(time_count, span, time_total, -1.0)
    long_forward = angle_table(span, span, span, -1.0)
    current = light_field
    block_toeplitz = (
        jnp.where(
            inside,
            jnp.take(
                jnp.dot(coupling.T, lag_powers[0][:STRETCH].T, precision=exact), clipped, axis=1
            ),
            0.0,
        ),
        jnp.where(
            inside,
            jnp.take(
                jnp.dot(coupling.T, lag_powers[1][:STRETCH].T, precision=exact), clipped, axis=1
            ),
            0.0,
        ),
    )
    for repeat in range(STEPS):
        diffract_stacked = current.reshape(2, height, lat_count, narrow)
        lateral_block = lax.all_to_all(
            diffract_stacked, "lat", split_axis=2, concat_axis=1, tiled=True
        )
        piece = (lateral_block[0, :, 0, :], lateral_block[1, :, 0, :])
        lateral_spectrum = complex_einsum("kx,xn->kn", lat_forward, piece)
        lateral_spectrum = complex_times(lateral_spectrum, lateral_turn)
        lateral_result = complex_einsum("xk,kn->xn", lat_backward, lateral_spectrum)
        lateral_joined = (
            jnp.stack([lateral_result[0], lateral_result[1]])[:, :, None, :] / lateral_total
        )
        diffract_turned = lax.all_to_all(
            lateral_joined, "lat", split_axis=1, concat_axis=2, tiled=True
        )
        stacked = diffract_turned.reshape(2, height, span).reshape(2, time_count, slab, span)
        rows = lax.all_to_all(stacked, "tm", split_axis=1, concat_axis=3, tiled=True)[:, 0]
        rows_here = rows.shape[1]
        grid = (
            rows[0].reshape(rows_here, time_count, span),
            rows[1].reshape(rows_here, time_count, span),
        )
        spectrum = time_forward(grid, small_forward, twiddle_forward, long_forward)
        spectrum = complex_times(spectrum, spectral_turn)
        result = time_inverse(spectrum, small_back, twiddle_back, long_back, time_total)
        joined = jnp.stack(
            [result[0].reshape(rows_here, time_total), result[1].reshape(rows_here, time_total)]
        )[:, None]
        turned = lax.all_to_all(joined, "tm", split_axis=3, concat_axis=1, tiled=True)
        current = turned.reshape(2, height, span)
        amplify_rows_here = current.shape[1]
        length = current.shape[2]
        count = length // STRETCH
        amplify_grid = (
            current[0].reshape(amplify_rows_here, count, STRETCH),
            current[1].reshape(amplify_rows_here, count, STRETCH),
        )
        direct = complex_einsum("xji,xci->xcj", block_toeplitz, amplify_grid)
        projected = complex_einsum("xci,ig->cgx", amplify_grid, trailing)
        stretch_ends = (coupling[None] * projected[0], coupling[None] * projected[1])

        def chain_step(running, ends):
            moved = complex_times(stretch_step, running)
            return ((moved[0] + ends[0], moved[1] + ends[1]), running)

        zero_state = jnp.zeros((groups, amplify_rows_here), jnp.float32)
        running, chain = lax.scan(chain_step, (zero_state, zero_state), stretch_ends)

        def combine(earlier, later):
            joint = complex_times((earlier[0], earlier[1]), (later[0], later[1]))
            carried = complex_times(
                (later[0][:, None], later[1][:, None]), (earlier[2], earlier[3])
            )
            return (joint[0], joint[1], carried[0] + later[2], carried[1] + later[3])

        identity = (
            jnp.ones((groups,), jnp.float32),
            jnp.zeros((groups,), jnp.float32),
            jnp.zeros_like(running[0]),
            jnp.zeros_like(running[1]),
        )
        prefix = carried_in(
            (device_step[0], device_step[1], running[0], running[1]), "tm", combine, identity
        )
        starts = powers(
            decay_rate, detuning, (jnp.arange(count, dtype=jnp.float32) * STRETCH)[:, None]
        )
        before = complex_times(
            (starts[0][:, :, None], starts[1][:, :, None]), (prefix[2][None], prefix[3][None])
        )
        states = (before[0] + chain[0], before[1] + chain[1])
        delayed = complex_einsum("cgx,gj->xcj", states, leading)
        summed_re = (direct[0] + delayed[0]).reshape(amplify_rows_here, length)
        summed_im = (direct[1] + delayed[1]).reshape(amplify_rows_here, length)
        current = jnp.stack([current[0] - weight * summed_im, current[1] + weight * summed_re])
    return current


def solution(mesh):
    return jax.shard_map(
        on_device,
        mesh=mesh,
        in_specs=(P(None, "lat", "tm"), P(), P(), P(None, "lat"), P(), P(), P()),
        out_specs=P(None, "lat", "tm"),
        check_vma=False,
    )
```

profile of v0, /device:TPU:1, one launch (start us, length us, event | category | flops | bytes accessed | tf_op | source)
XLA Modules:
  0.0 869.8 jit_solution(7139973736807869454)
XLA Ops:
  1.9 7.6 all-to-all-start
  14.2 2.1 all-to-all-done
  18.0 21.2 %fusion.20 = f32[1024,16]{0,1:T(8,128)S(1)} fusion(f32[1024,16]{0,1:T(8,128)S(1)} %squeeze.80), kind=kOutput, calls=%fused_computation.47 | convolution fusion | flops 217055232 | bytes 131072 | tf_op jit(solution)/shard_map/kx,xn->kn/dot_general | solution.py:31
  39.4 21.2 %fusion.18 = f32[1024,16]{0,1:T(8,128)S(1)} fusion(f32[1024,16]{0,1:T(8,128)S(1)} %squeeze.79), kind=kOutput, calls=%fused_computation.45 | convolution fusion | flops 217055232 | bytes 131072 | tf_op jit(solution)/shard_map/kx,xn->kn/dot_general | solution.py:34
  60.7 21.0 %fusion.140 = f32[1024,16]{0,1:T(8,128)S(1)} fusion(f32[1024,16]{0,1:T(8,128)S(1)} %fusion.20, f32[1024,16]{0,1:T(8,128)S(1)} %squeeze.79), kind=kOutput, calls=%fused_computation.155 | convolution fusion | flops 216023040 | bytes 196608 | tf_op jit(solution)/shard_map/kx,xn->kn/dot_general | solution.py:31
  81.7 21.0 %fusion.143 = f32[1024,16]{0,1:T(8,128)S(1)} fusion(f32[1024,16]{0,1:T(8,128)S(1)} %fusion.18, f32[1024,16]{0,1:T(8,128)S(1)} %squeeze.80), kind=kOutput, calls=%fused_computation.156 | convolution fusion | flops 216023040 | bytes 196608 | tf_op jit(solution)/shard_map/kx,xn->kn/dot_general | solution.py:34
  102.8 19.4 %fusion.62 = f32[1024,16]{0,1:T(8,128)S(1)} fusion(f32[1024,16]{0,1:T(8,128)S(1)} %fusion.143, f32[1024,16]{0,1:T(8,128)S(1)} %fusion.140, f32[1024]{0:T(1024)S(1)} %get-tuple-element.741, f32[1024]{0:T(1024)S(1)} %get-tuple-element.740), kind=kOutput, calls=%fused_computation.84 | convolution fusion | flops 216055808 | bytes 204800 | tf_op jit(solution)/shard_map/xk,kn->xn/dot_general | solution.py:31
  122.2 19.8 %fusion.60 = f32[1024,16]{0,1:T(8,128)S(1)} fusion(f32[1024,16]{0,1:T(8,128)S(1)} %fusion.143, f32[1024,16]{0,1:T(8,128)S(1)} %fusion.140, f32[1024]{0:T(1024)S(1)} %get-tuple-element.741, f32[1024]{0:T(1024)S(1)} %get-tuple-element.740), kind=kOutput, calls=%fused_computation.83 | convolution fusion | flops 216055808 | bytes 204800 | tf_op jit(solution)/shard_map/xk,kn->xn/dot_general | solution.py:34
  142.0 19.5 %fusion.119 = f32[1,1024,1,16]{1,3,2,0:T(8,128)S(1)} fusion(f32[1024,16]{0,1:T(8,128)S(1)} %fusion.62, f32[1024,16]{0,1:T(8,128)S(1)} %fusion.143, f32[1024,16]{0,1:T(8,128)S(1)} %fusion.140, f32[1024]{0:T(1024)S(1)} %get-tuple-element.741, f32[1024]{0:T(1024)S(1)} %get-tuple-element.740), kind=kOutput, calls=%fused_computation.148 | convolution fusion | flops 216072192 | bytes 270336 | tf_op jit(solution)/shard_map/xk,kn->xn/dot_general | solution.py:31
  161.6 19.7 %fusion.125 = f32[1,1024,1,16]{1,3,2,0:T(8,128)S(1)} fusion(f32[1024,16]{0,1:T(8,128)S(1)} %fusion.60, f32[1024,16]{0,1:T(8,128)S(1)} %fusion.143, f32[1024,16]{0,1:T(8,128)S(1)} %fusion.140, f32[1024]{0:T(1024)S(1)} %get-tuple-element.741, f32[1024]{0:T(1024)S(1)} %get-tuple-element.740), kind=kOutput, calls=%fused_computation.150 | convolution fusion | flops 216072192 | bytes 270336 | tf_op jit(solution)/shard_map/xk,kn->xn/dot_general | solution.py:34
  182.0 4.4 reduce.1
  186.3 2.1 reshape.461
  188.5 4.5 all-to-all-start.1
  193.2 6.6 all-to-all-done.1
  200.7 1.9 reshape.462
  204.3 11.6 %all-to-all-start.2 = ((f32[2,16,4,256]{3,2,0,1:T(4,128)}), f32[2,16,4,256]{3,2,0,1:T(4,128)S(1)}, u32[]{:S(2)}, u32[]{:S(2)}) async-start(f32[2,16,4,256]{3,2,0,1:T(4,128)} %copy.330), calls=%async_computation.2 | async-start | bytes 262144 | tf_op jit(solution)/shard_map/all_to_all | solution.py:145
  216.6 8.4 all-to-all-done.2
  237.3 4.4 copy.334
  241.7 4.7 bitcast_bitcast_fusion.1
  246.5 8.7 %reshape.463 = f32[16,1,2048]{2,1,0:T(1,128)} reshape(f32[4096,1,2,4]{3,2,1,0:T(2,128)} %bitcast_bitcast_fusion.1) | data formatting | bytes 262144
  255.2 3.4 all-to-all-start.3
  258.8 54.5 %gather_fusion = f32[16384,64]{1,0:T(8,128)} fusion(f32[64,128]{0,1:T(8,128)S(1)} %fusion.543, s32[16384]{0:T(1024)S(1)} %bitcast_clamp_fusion), kind=kCustom, calls=%fused_computation.clone | custom fusion | bytes 8454144 | tf_op jit(solution)/shard_map/jit(_take)/gather | solution.py:116
  313.2 7.4 copy.337
  320.6 54.4 %gather_fusion.1 = f32[16384,64]{1,0:T(8,128)} fusion(f32[64,128]{0,1:T(8,128)S(1)} %fusion.541, s32[16384]{0:T(1024)S(1)} %bitcast_clamp_fusion), kind=kCustom, calls=%fused_computation.1.clone | custom fusion | bytes 8454144 | tf_op jit(solution)/shard_map/jit(_take)/gather | solution.py:123
  375.1 7.4 copy.339
  382.4 16.7 %all-gather.6 = f32[16,1,128]{2,1,0:T(1,128)S(1)} all-gather(f32[1,1,128]{2,1,0:T(1,128)S(1)} %get-tuple-element.745), channel_id=2, replica_groups=mesh['lat'=16,'tm'=16] {'tm'}, dimensions={0}, use_global_device_ids=true | all-gather | bytes 8704 | tf_op jit(solution)/shard_map/all_gather | solution.py:17
  399.1 15.1 %all-gather.7 = f32[16,1,128]{2,1,0:T(1,128)S(1)} all-gather(f32[1,1,128]{2,1,0:T(1,128)S(1)} %get-tuple-element.744), channel_id=3, replica_groups=mesh['lat'=16,'tm'=16] {'tm'}, dimensions={0}, use_global_device_ids=true | all-gather | bytes 8704 | tf_op jit(solution)/shard_map/all_gather | solution.py:17
  415.1 7.8 reshape.464
  422.9 5.2 copy.335
  430.2 18.0 %all-gather.2 = f32[2048,64]{1,0:T(8,128)S(1)} all-gather(f32[128,64]{1,0:T(8,128)S(1)} %get-tuple-element.386), channel_id=4, replica_groups=mesh['lat'=16,'tm'=16] {'tm'}, dimensions={0}, use_global_device_ids=true | all-gather | bytes 557056 | tf_op jit(solution)/shard_map/all_gather | solution.py:17
  448.2 19.7 %all-gather.3 = f32[2048,64]{1,0:T(8,128)} all-gather(f32[128,64]{1,0:T(8,128)S(1)} %get-tuple-element.387), channel_id=5, replica_groups=mesh['lat'=16,'tm'=16] {'tm'}, dimensions={0}, use_global_device_ids=true | all-gather | bytes 557056 | tf_op jit(solution)/shard_map/all_gather | solution.py:17
  467.8 15.2 %while.67 = (s32[]{:T(128)}, f32[128,64]{1,0:T(8,128)S(1)}, f32[128,64]{1,0:T(8,128)S(1)}, s32[]{:T(128)}, f32[16,128]{1,0:T(8,128)S(1)}, /*index=5*/f32[16,128]...) while((s32[]{:T(128)}, f32[128,64]{1,0:T(8,128)S(1)}, ...), condition=%wide.region_3.5_spmd.clone, body=%wide.region_2.4_spmd.clone.sunk | while | flops 98308 | bytes 199809 | solution.py:26
  484.4 9.1 %fusion.25 = f32[64,2,128]{2,1,0:T(2,128)S(1)} fusion(f32[64,2,128]{2,1,0:T(2,128)S(1)} %reshape_squeeze.26, f32[128,128,64]{1,0,2:T(8,128)} %copy.337, pred[128,128]{1,0:T(8,128)(4,1)S(1)} %get-tuple-element.755, pred[128,128]{1,0:T(8,128)(4,1)S(1)} %get-tuple-element.754), kind=kOutput, calls=%fused_computation.52 | convolution fusion | flops 27262976 | bytes 4358144 | tf_op jit(solution)/shard_map/xji,xci->xcj/dot_general | solution.py:34
  493.6 6.6 fusion.24
  500.2 6.6 fusion.29
  506.8 6.8 fusion.28
  515.6 9.6 %all_to_all.120 = f32[16,1,2048]{2,1,0:T(1,128)S(1)} all-to-all(f32[16,1,2048]{2,1,0:T(1,128)S(1)} %reshape.465), channel_id=1, replica_groups=mesh['lat'=16,'tm'=16] {'lat'}, dimensions={0} | all-to-all | bytes 262144 | tf_op jit(solution)/shard_map/all_to_all | solution.py:131
  526.4 21.2 %fusion.16 = f32[1024,16]{0,1:T(8,128)S(1)} fusion(f32[1024,16]{0,1:T(8,128)S(1)} %squeeze.84), kind=kOutput, calls=%fused_computation.43 | convolution fusion | flops 217055232 | bytes 131072 | tf_op jit(solution)/shard_map/kx,xn->kn/dot_general | solution.py:31
  547.8 21.2 %fusion.14 = f32[1024,16]{0,1:T(8,128)S(1)} fusion(f32[1024,16]{0,1:T(8,128)S(1)} %squeeze.83), kind=kOutput, calls=%fused_computation.41 | convolution fusion | flops 217055232 | bytes 131072 | tf_op jit(solution)/shard_map/kx,xn->kn/dot_general | solution.py:34
  569.1 21.0 %fusion.146 = f32[1024,16]{0,1:T(8,128)S(1)} fusion(f32[1024,16]{0,1:T(8,128)S(1)} %fusion.16, f32[1024,16]{0,1:T(8,128)S(1)} %squeeze.83), kind=kOutput, calls=%fused_computation.157 | convolution fusion | flops 216023040 | bytes 196608 | tf_op jit(solution)/shard_map/kx,xn->kn/dot_general | solution.py:31
  590.1 21.0 %fusion.149 = f32[1024,16]{0,1:T(8,128)S(1)} fusion(f32[1024,16]{0,1:T(8,128)S(1)} %fusion.14, f32[1024,16]{0,1:T(8,128)S(1)} %squeeze.84), kind=kOutput, calls=%fused_computation.158 | convolution fusion | flops 216023040 | bytes 196608 | tf_op jit(solution)/shard_map/kx,xn->kn/dot_general | solution.py:34
  611.2 19.4 %fusion.54 = f32[1024,16]{0,1:T(8,128)S(1)} fusion(f32[1024,16]{0,1:T(8,128)S(1)} %fusion.149, f32[1024,16]{0,1:T(8,128)S(1)} %fusion.146, f32[1024]{0:T(1024)S(1)} %copy-done.22, f32[1024]{0:T(1024)S(1)} %copy-done.20), kind=kOutput, calls=%fused_computation.80 | convolution fusion | flops 216055808 | bytes 204800 | tf_op jit(solution)/shard_map/xk,kn->xn/dot_general | solution.py:31
  630.6 19.8 %fusion.52 = f32[1024,16]{0,1:T(8,128)S(1)} fusion(f32[1024,16]{0,1:T(8,128)S(1)} %fusion.149, f32[1024,16]{0,1:T(8,128)S(1)} %fusion.146, f32[1024]{0:T(1024)S(1)} %copy-done.22, f32[1024]{0:T(1024)S(1)} %copy-done.20), kind=kOutput, calls=%fused_computation.79 | convolution fusion | flops 216055808 | bytes 204800 | tf_op jit(solution)/shard_map/xk,kn->xn/dot_general | solution.py:34
  650.4 19.5 %fusion.131 = f32[1,1024,1,16]{1,3,2,0:T(8,128)S(1)} fusion(f32[1024,16]{0,1:T(8,128)S(1)} %fusion.54, f32[1024,16]{0,1:T(8,128)S(1)} %fusion.149, f32[1024,16]{0,1:T(8,128)S(1)} %fusion.146, f32[1024]{0:T(1024)S(1)} %copy-done.22, f32[1024]{0:T(1024)S(1)} %copy-done.20), kind=kOutput, calls=%fused_computation.152 | convolution fusion | flops 216072192 | bytes 270336 | tf_op jit(solution)/shard_map/xk,kn->xn/dot_general | solution.py:31
  669.9 19.7 %fusion.137 = f32[1,1024,1,16]{1,3,2,0:T(8,128)S(1)} fusion(f32[1024,16]{0,1:T(8,128)S(1)} %fusion.52, f32[1024,16]{0,1:T(8,128)S(1)} %fusion.149, f32[1024,16]{0,1:T(8,128)S(1)} %fusion.146, f32[1024]{0:T(1024)S(1)} %copy-done.22, f32[1024]{0:T(1024)S(1)} %copy-done.20), kind=kOutput, calls=%fused_computation.154 | convolution fusion | flops 216072192 | bytes 270336 | tf_op jit(solution)/shard_map/xk,kn->xn/dot_general | solution.py:34
  690.3 4.4 reduce.5
  694.7 1.5 reshape.467
  696.1 9.9 %all_to_all.121 = f32[16,1,2048]{2,1,0:T(1,128)S(1)} all-to-all(f32[16,1,2048]{2,1,0:T(1,128)S(1)} %reshape.467), channel_id=1, replica_groups=mesh['lat'=16,'tm'=16] {'lat'}, dimensions={0} | all-to-all | bytes 262144 | tf_op jit(solution)/shard_map/all_to_all | solution.py:141
  706.9 1.9 reshape.468
  709.9 16.7 %all_to_all.122 = f32[2,16,4,256]{3,2,0,1:T(4,128)S(1)} all-to-all(f32[2,16,4,256]{3,2,0,1:T(4,128)S(1)} %copy.363), channel_id=1, replica_groups=mesh['lat'=16,'tm'=16] {'tm'}, dimensions={1} | all-to-all | bytes 262144 | tf_op jit(solution)/shard_map/all_to_all | solution.py:145
  739.0 4.4 copy.365
  743.4 4.7 bitcast_bitcast_fusion
  748.1 8.9 %reshape.469 = f32[16,1,2048]{2,1,0:T(1,128)} reshape(f32[4096,1,2,4]{3,2,1,0:T(2,128)} %bitcast_bitcast_fusion) | data formatting | bytes 262144
  757.1 3.4 all-to-all-start.7
  760.5 8.4 all-to-all-done.7
  769.8 7.8 reshape.470
  777.7 5.2 copy.366
  783.0 8.4 fusion.27
  792.5 9.0 %fusion.23 = f32[64,2,128]{2,1,0:T(2,128)} fusion(f32[64,2,128]{2,1,0:T(2,128)S(1)} %reshape_squeeze.30, f32[128,128,64]{1,0,2:T(8,128)} %copy.337, pred[128,128]{1,0:T(8,128)(4,1)S(1)} %get-tuple-element.755, pred[128,128]{1,0:T(8,128)(4,1)S(1)} %get-tuple-element.754), kind=kOutput, calls=%fused_computation.50 | convolution fusion | flops 27262976 | bytes 4358144 | tf_op jit(solution)/shard_map/xji,xci->xcj/dot_general | solution.py:34
  802.8 17.7 %all-gather.4 = f32[2048,64]{1,0:T(8,128)S(1)} all-gather(f32[128,64]{1,0:T(8,128)S(1)} %get-tuple-element.392), channel_id=6, replica_groups=mesh['lat'=16,'tm'=16] {'tm'}, dimensions={0}, use_global_device_ids=true | all-gather | bytes 557056 | tf_op jit(solution)/shard_map/all_gather | solution.py:17
  820.5 18.6 %all-gather.5 = f32[2048,64]{1,0:T(8,128)S(1)} all-gather(f32[128,64]{1,0:T(8,128)S(1)} %get-tuple-element.393), channel_id=7, replica_groups=mesh['lat'=16,'tm'=16] {'tm'}, dimensions={0}, use_global_device_ids=true | all-gather | bytes 557056 | tf_op jit(solution)/shard_map/all_gather | solution.py:17
  839.0 12.8 %while.69 = (s32[]{:T(128)}, f32[128,64]{1,0:T(8,128)S(1)}, f32[128,64]{1,0:T(8,128)S(1)}, s32[]{:T(128)}, f32[16,128]{1,0:T(8,128)}, /*index=5*/f32[16,128]{1,0...) while((s32[]{:T(128)}, f32[128,64]{1,0:T(8,128)S(1)}, ...), condition=%wide.region_7.9_spmd.clone, body=%wide.region_6.8_spmd.clone.sunk | while | flops 98308 | bytes 199809 | solution.py:26
  853.3 8.7 fusion.22
  861.9 6.6 fusion.26
  (290 shorter events, 80.8 us)
Async XLA Ops:
  0.0 11.2 %copy-start = (f32[32]{0:T(128)S(1)}, f32[32]{0:T(128)}, u32[]{:S(2)}) copy-start(f32[32]{0:T(128)} %param.21) | copy-start | bytes 388
  1.9 14.5 %all-to-all-start = ((f32[16,1,2048]{2,1,0:T(1,128)}), f32[16,1,2048]{2,1,0:T(1,128)S(1)}, u32[]{:S(2)}, u32[]{:S(2)}) async-start(f32[16,1,2048]{2,1,0:T(1,128)} %reshape.459), calls=%async_computation | async-start | bytes 262144 | tf_op jit(solution)/shard_map/all_to_all | solution.py:131
  14.2 147.3 %copy-start.19 = (f32[1024]{0:T(1024)}, f32[1024]{0:T(1024)S(1)}, u32[]{:S(2)}) copy-start(f32[1024]{0:T(1024)S(1)} %get-tuple-element.740) | copy-start | bytes 12292
  14.2 147.3 %copy-start.21 = (f32[1024]{0:T(1024)}, f32[1024]{0:T(1024)S(1)}, u32[]{:S(2)}) copy-start(f32[1024]{0:T(1024)S(1)} %get-tuple-element.741) | copy-start | bytes 12292
  188.5 11.4 %all-to-all-start.1 = ((f32[16,1,2048]{2,1,0:T(1,128)}), f32[16,1,2048]{2,1,0:T(1,128)S(1)}, u32[]{:S(2)}, u32[]{:S(2)}) async-start(f32[16,1,2048]{2,1,0:T(1,128)} %reshape.461), calls=%async_computation.1 | async-start | bytes 262144 | tf_op jit(solution)/shard_map/all_to_all | solution.py:141
  193.1 289.9 %copy-start.15 = (f32[2,128]{1,0:T(2,128)}, f32[2,128]{1,0:T(2,128)S(1)}, u32[]{:S(2)}) copy-start(f32[2,128]{1,0:T(2,128)S(1)} %get-tuple-element.742) | copy-start | bytes 3076
  193.1 289.9 %copy-start.17 = (f32[2,128]{1,0:T(2,128)}, f32[2,128]{1,0:T(2,128)S(1)}, u32[]{:S(2)}) copy-start(f32[2,128]{1,0:T(2,128)S(1)} %get-tuple-element.743) | copy-start | bytes 3076
  193.2 36.7 %copy-start.13 = (f32[16,256]{1,0:T(8,128)}, f32[16,256]{1,0:T(8,128)S(1)}, u32[]{:S(2)}) copy-start(f32[16,256]{1,0:T(8,128)S(1)} %get-tuple-element.750) | copy-start | bytes 49156
  204.3 20.7 %all-to-all-start.2 = ((f32[2,16,4,256]{3,2,0,1:T(4,128)}), f32[2,16,4,256]{3,2,0,1:T(4,128)S(1)}, u32[]{:S(2)}, u32[]{:S(2)}) async-start(f32[2,16,4,256]{3,2,0,1:T(4,128)} %copy.330), calls=%async_computation.2 | async-start | bytes 262144 | tf_op jit(solution)/shard_map/all_to_all | solution.py:145
  216.2 18.7 %copy-start.9 = (f32[16,256]{1,0:T(8,128)}, f32[16,256]{1,0:T(8,128)S(1)}, u32[]{:S(2)}) copy-start(f32[16,256]{1,0:T(8,128)S(1)} %copy.332) | copy-start | bytes 49156
  216.4 18.5 %copy-start.11 = (f32[16,256]{1,0:T(8,128)}, f32[16,256]{1,0:T(8,128)S(1)}, u32[]{:S(2)}) copy-start(f32[16,256]{1,0:T(8,128)S(1)} %copy.333) | copy-start | bytes 49156
  255.2 159.0 %all-to-all-start.3 = ((f32[16,1,2048]{2,1,0:T(1,128)}), f32[16,1,2048]{2,1,0:T(1,128)S(1)}, u32[]{:S(2)}, u32[]{:S(2)}) async-start(f32[16,1,2048]{2,1,0:T(1,128)} %reshape.463), calls=%async_computation.3 | async-start | bytes 262144 | tf_op jit(solution)/shard_map/all_to_all | solution.py:157
  483.0 17.2 %copy-start.7 = (f32[16,128]{1,0:T(8,128)}, f32[16,128]{1,0:T(8,128)S(1)}, u32[]{:S(2)}) copy-start(f32[16,128]{1,0:T(8,128)S(1)} %get-tuple-element.1137) | copy-start | bytes 24580
  483.0 17.2 %copy-start.8 = (f32[16,128]{1,0:T(8,128)}, f32[16,128]{1,0:T(8,128)S(1)}, u32[]{:S(2)}) copy-start(f32[16,128]{1,0:T(8,128)S(1)} %get-tuple-element.1138) | copy-start | bytes 24580
  483.9 9.7 %copy-start.2 = (f32[128,128,64]{1,0,2:T(8,128)S(1)}, f32[128,128,64]{1,0,2:T(8,128)}, u32[]{:S(2)}) copy-start(f32[128,128,64]{1,0,2:T(8,128)} %copy.337) | copy-start | bytes 12582916
  484.4 15.7 %copy-start.3 = (f32[128,128,64]{1,0,2:T(8,128)S(1)}, f32[128,128,64]{1,0,2:T(8,128)}, u32[]{:S(2)}) copy-start(f32[128,128,64]{1,0,2:T(8,128)} %copy.339) | copy-start | bytes 12582916
  590.1 21.1 %copy-start.20 = (f32[1024]{0:T(1024)S(1)}, f32[1024]{0:T(1024)}, u32[]{:S(2)}) copy-start(f32[1024]{0:T(1024)} %copy-done.19) | copy-start | bytes 12292
  590.1 21.1 %copy-start.22 = (f32[1024]{0:T(1024)S(1)}, f32[1024]{0:T(1024)}, u32[]{:S(2)}) copy-start(f32[1024]{0:T(1024)} %copy-done.21) | copy-start | bytes 12292
  694.7 33.1 %copy-start.14 = (f32[16,256]{1,0:T(8,128)S(1)}, f32[16,256]{1,0:T(8,128)}, u32[]{:S(2)}) copy-start(f32[16,256]{1,0:T(8,128)} %copy-done.13) | copy-start | bytes 49156
  708.8 23.9 %copy-start.10 = (f32[16,256]{1,0:T(8,128)S(1)}, f32[16,256]{1,0:T(8,128)}, u32[]{:S(2)}) copy-start(f32[16,256]{1,0:T(8,128)} %copy-done.9) | copy-start | bytes 49156
  708.8 23.9 %copy-start.12 = (f32[16,256]{1,0:T(8,128)S(1)}, f32[16,256]{1,0:T(8,128)}, u32[]{:S(2)}) copy-start(f32[16,256]{1,0:T(8,128)} %copy-done.11) | copy-start | bytes 49156
  757.1 11.9 %all-to-all-start.7 = ((f32[16,1,2048]{2,1,0:T(1,128)}), f32[16,1,2048]{2,1,0:T(1,128)S(1)}, u32[]{:S(2)}, u32[]{:S(2)}) async-start(f32[16,1,2048]{2,1,0:T(1,128)} %reshape.469), calls=%async_computation.7 | async-start | bytes 262144 | tf_op jit(solution)/shard_map/all_to_all | solution.py:157
  802.0 49.9 %copy-start.16 = (f32[2,128]{1,0:T(2,128)S(1)}, f32[2,128]{1,0:T(2,128)}, u32[]{:S(2)}) copy-start(f32[2,128]{1,0:T(2,128)} %copy-done.15) | copy-start | bytes 3076
  802.0 49.9 %copy-start.18 = (f32[2,128]{1,0:T(2,128)S(1)}, f32[2,128]{1,0:T(2,128)}, u32[]{:S(2)}) copy-start(f32[2,128]{1,0:T(2,128)} %copy-done.17) | copy-start | bytes 3076
  852.7 9.2 %copy-start.4 = (f32[128,128,64]{1,0,2:T(8,128)S(1)}, f32[128,128,64]{1,0,2:T(8,128)}, u32[]{:S(2)}) copy-start(f32[128,128,64]{1,0,2:T(8,128)} %copy.339) | copy-start | bytes 12582916
  853.2 15.4 %copy-start.5 = (f32[64,2,128]{2,1,0:T(2,128)S(1)}, f32[64,2,128]{2,1,0:T(2,128)}, u32[]{:S(2)}) copy-start(f32[64,2,128]{2,1,0:T(2,128)} %fusion.23) | copy-start | bytes 196612
  853.2 15.7 %copy-start.6 = (f32[1,64,256]{2,1,0:T(8,128)S(1)}, f32[1,64,256]{2,1,0:T(8,128)}, u32[]{:S(2)}) copy-start(f32[1,64,256]{2,1,0:T(8,128)} %squeeze.85) | copy-start | bytes 196612
  853.3 16.4 %copy-start.1 = (f32[32]{0:T(128)S(1)}, f32[32]{0:T(128)}, u32[]{:S(2)}) copy-start(f32[32]{0:T(128)} %param.21) | copy-start | bytes 388
where the time goes:
time: 881 us; the launch traced here: 870 us
  matrix products  418 us (47%)
  local copies, waits for them, and re-layouts  218 us (25%)
  blocking collectives  142 us (16%)
  other arithmetic  33.5 us (4%)
  starting transfers between devices  30.6 us (3%)
  waiting for transfers between devices  25.6 us (3%)
    dot_general x16, matrix products, complex_einsum(): jnp.einsum(form, left[0], right[1], precision=exact)  106 us
    all_gather x6, blocking collectives, carried_in(): pieces = jax.tree.map(lambda part: lax.all_gather(part, axis), value)  106 us
    dot_general x16, matrix products, complex_einsum(): jnp.einsum(form, left[1], right[0], precision=exact)  103 us
    dot_general x16, matrix products, complex_einsum(): jnp.einsum(form, left[0], right[0], precision=exact)  103 us
    dot_general x16, matrix products, complex_einsum(): jnp.einsum(form, left[1], right[1], precision=exact)  101 us
    gather x2, local copies, waits for them, and re-layouts, on_device(): jnp.take(jnp.dot(coupling.T, lag_powers[0][:STRETCH].T, precision=exact),...  61.9 us
    gather x2, local copies, waits for them, and re-layouts, on_device(): jnp.take(jnp.dot(coupling.T, lag_powers[1][:STRETCH].T, precision=exact),...  61.8 us
    unnamed x61, local copies, waits for them, and re-layouts  52.6 us
  transfers between devices with their start and end apart: 5, of which 4 were waited for; matrix products, arithmetic and copies ran while one was open for 15% of the time, Pallas kernels for 0%

commit v1 on v0

v1 whole, which is shorter than its diff:
```python
import math

import jax
import jax.numpy as jnp
import numpy as np
from jax import lax
from jax.experimental import pallas as pl
from jax.experimental.pallas import tpu as pltpu
from jax.sharding import PartitionSpec as P

NX, NT, BINS, GROUPS = 1024, 4096, 32, 128
WEIGHT = 0.5 / math.sqrt(GROUPS)
F32, BF16 = jnp.float32, jnp.bfloat16
BOTH = ("lat", "tm")


def split_table(table):
    high = table.astype(np.float32).astype(jnp.bfloat16)
    low = (table - high.astype(np.float64)).astype(jnp.bfloat16)
    return high, low


def build_tables():
    grid = np.arange
    angle = 2 * np.pi * (grid(256)[:, None] * grid(256)[None, :] % 256) / 256
    wide = np.concatenate([np.cos(angle), np.sin(angle)], 1)
    tall = np.concatenate([np.cos(angle), np.sin(angle)], 0)
    lane = grid(128)
    c, q, col = lane // 64, lane // 16 % 4, lane % 16
    row = grid(128)
    rm, rc, rq = row // 8, row // 4 % 2, row % 4
    turn = 2 * np.pi * (col[:, None] * rm[None, :] % 16) / 16
    same = c[:, None] == rc[None, :]
    sign = np.where(c[:, None] == 0, 1.0, -1.0)
    small = np.where(same, np.cos(turn), sign * np.sin(turn)) * (q[:, None] == rq[None, :])
    short = 2 * np.pi * (col[:64, None] * grid(256)[None, :]) / NT
    index = 16 * grid(256)[:, None] + grid(16)[None, :]
    index = np.where(index > NT // 2, index - NT, index)
    omega = 2 * np.pi * index / NT
    omega_high = omega.astype(np.float32)
    omega_low = (omega - omega_high).astype(np.float32)
    omega_lanes = np.tile(omega, (1, 8))
    eight = lane // 16
    twiddle_a = np.zeros((8, 256, 128))
    twiddle_b = np.zeros((8, 256, 128))
    for r in range(8):
        source = (eight + r) % 8
        sc, sq = source // 4, source % 4
        theta = -2 * np.pi * ((sq - q)[None, :] * grid(256)[:, None]) / NX
        re, im = np.cos(theta), np.sin(theta)
        same_part = (sc == c)[None, :]
        flip = np.where(c == 0, -1.0, 1.0)[None, :]
        twiddle_a[r] = np.where(same_part, re, flip * im) / NX
        twiddle_b[r] = np.where(same_part, -im, flip * re) / NX
    t = {}
    t["wide"] = np.concatenate(split_table(wide), 0)
    t["tall"] = np.concatenate(split_table(tall), 1)
    t["small"] = np.concatenate(split_table(small), 0)
    t["small_back"] = np.concatenate(split_table(small.T), 0)
    t["tc"] = np.cos(short).astype(np.float32)
    t["ts"] = np.sin(short).astype(np.float32)
    t["omega_rows"] = np.stack([omega_high.T, omega_low.T])
    t["omega_lanes"] = np.stack([np.tile(omega_high, (1, 8)), np.tile(omega_low, (1, 8))])
    t["back_re"] = (np.cos(omega_lanes) / NT).astype(np.float32)
    t["back_im"] = (-np.sin(omega_lanes) / NT).astype(np.float32)
    t["twiddle_a"] = twiddle_a.astype(np.float32)
    t["twiddle_b"] = twiddle_b.astype(np.float32)
    return t


TABLES = build_tables()


def iota(shape, dim):
    return lax.broadcasted_iota(jnp.int32, shape, dim)


def halves(value):
    high = value.astype(BF16)
    return high, (value - high.astype(F32)).astype(BF16)


def thirds(value):
    high = value.astype(BF16)
    rest = value - high.astype(F32)
    middle = rest.astype(BF16)
    return high, middle, (rest - middle.astype(F32)).astype(BF16)


def dot(left, right):
    return lax.dot_general(left, right, (((1,), (0,)), ((), ())), preferred_element_type=F32)


def dot_nt(left, right):
    return lax.dot_general(left, right, (((1,), (1,)), ((), ())), preferred_element_type=F32)


def quadrants(product, rows, cols):
    return product[:rows, :cols] + (product[:rows, cols:] + product[rows:, :cols])


def table_times(table, value):
    product = dot(table, jnp.concatenate(halves(value), 1))
    return quadrants(product, table.shape[0] // 2, value.shape[1])


def times_table(value, table):
    product = dot(jnp.concatenate(halves(value), 0), table)
    return quadrants(product, value.shape[0], table.shape[1] // 2)


def sine_cosine_half(angle):
    x = angle * 0.5
    z = x * x
    s = jnp.full_like(z, 1.0 / 6227020800.0)
    for k in (-1.0 / 39916800.0, 1.0 / 362880.0, -1.0 / 5040.0, 1.0 / 120.0, -1.0 / 6.0):
        s = s * z + k
    c = jnp.full_like(z, -1.0 / 87178291200.0)
    for k in (1.0 / 479001600.0, -1.0 / 3628800.0, 1.0 / 40320.0, -1.0 / 720.0, 1.0 / 24.0, -0.5):
        c = c * z + k
    return x + x * (z * s), 1.0 + z * c


def resonance(detune, keep, lost, high, low):
    s, c = sine_cosine_half((detune + high) + low)
    re = lost + (2.0 * keep) * (s * s)
    im = (2.0 * keep) * (s * c)
    scale = 1.0 / (re * re + im * im)
    return re * scale, -(im * scale)


def prepare(params, group_bin, occupation, spectral, lateral, omega_rows, omega_row, phase_row,
            back_re, back_im, twiddle_a, twiddle_b, quad):
    detune, keep, lost, drive = (params[:, k : k + 1] for k in range(4))
    real, imag = [], []
    for w1 in range(16):
        g_re, g_im = resonance(
            detune, keep, lost, omega_rows[0, w1 : w1 + 1, :], omega_rows[1, w1 : w1 + 1, :]
        )
        real.append(g_re)
        imag.append(g_im)
    resonances = jnp.concatenate(halves(jnp.concatenate(real + imag, 0)), 0)
    member = (iota((BINS, GROUPS), 0) == group_bin).astype(BF16)
    per_bin = dot(member, jnp.concatenate(thirds(occupation), 1))
    width = occupation.shape[1]
    per_bin = (per_bin[:, :width] + per_bin[:, width : 2 * width]) + per_bin[:, 2 * width :]
    per_bin = per_bin * drive
    parts = thirds(per_bin)
    pick = (iota((128, 128), 0) == 4 * quad + iota((128, 128), 1) // 16 % 4).astype(BF16)
    chosen = (dot(parts[0], pick) + dot(parts[1], pick)) + dot(parts[2], pick)
    lane = iota((BINS, 128), 1)
    couple_row = jnp.sum(
        jnp.where(iota((BINS, 128), 0) == lane // 64 * 16 + lane % 16, chosen, 0.0),
        axis=0, keepdims=True,
    )
    pick_rows = (iota((64, 128), 1) == 4 * quad + iota((64, 128), 0) // 16).astype(BF16)
    spread = sum(dot_nt(pick_rows, jnp.concatenate([part] * 16, 0)) for part in parts)
    couple_grid = jnp.where(
        iota((64, 512), 1) // 32 == iota((64, 512), 0) % 16, spread, 0.0
    )
    gain_high, gain_low = halves(couple_grid * WEIGHT)
    gain = dot(jnp.concatenate([gain_high, gain_low], 0),
               jnp.concatenate([resonances[:512], resonances[512:1024]], 1))
    gain_rest = dot(gain_high, jnp.concatenate([resonances[1024:1536], resonances[1536:]], 1))
    gain = (gain[:64] + gain[64:]) + gain_rest
    gain = jnp.concatenate([-gain[:, 256:], gain[:, :256]], 0)
    s, c = sine_cosine_half(spectral)
    cos, sin = 1.0 - 2.0 * (s * s), 2.0 * (s * c)
    side = jnp.where(iota((256, 128), 1) < 64, -1.0, 1.0)
    wrap_a = cos * back_re - sin * back_im
    wrap_b = (cos * back_im + sin * back_re) * side
    s, c = sine_cosine_half(lateral)
    cos, sin = 1.0 - 2.0 * (s * s), 2.0 * (s * c)
    r = [cos[:, k : k + 1] for k in range(4)]
    i = [sin[:, k : k + 1] for k in range(4)]
    blocks_re = [
        (r[0] + r[2]) + (r[1] + r[3]),
        (r[0] - r[2]) + (i[1] - i[3]),
        (r[0] + r[2]) - (r[1] + r[3]),
        (r[0] - r[2]) - (i[1] - i[3]),
    ]
    blocks_im = [
        (i[0] + i[2]) + (i[1] + i[3]),
        (i[0] - i[2]) - (r[1] - r[3]),
        (i[0] + i[2]) - (i[1] + i[3]),
        (i[0] - i[2]) + (r[1] - r[3]),
    ]
    mixing = [
        twiddle_a[k] * blocks_re[k % 4] + twiddle_b[k] * blocks_im[k % 4] for k in range(8)
    ]
    rows = jnp.concatenate([params[:16]] * 4 + [params[16:]] * 4, 0)
    g_re, g_im = resonance(
        rows[:, 0:1], rows[:, 1:2], rows[:, 2:3], omega_row[0:1, :], omega_row[1:2, :]
    )
    s, c = sine_cosine_half(phase_row)
    once_re, once_im = 1.0 - 2.0 * (s * s), 2.0 * (s * c)
    twice_re = once_re * once_re - once_im * once_im
    twice_im = 2.0 * once_re * once_im
    inside = iota((128, 128), 0) // 16 % 4 == iota((128, 128), 1) // 16 % 4
    left = iota((128, 128), 1) < 64
    f_re, f_im = -WEIGHT * twice_im, WEIGHT * twice_re
    b_re = jnp.where(inside, g_re * f_re - g_im * f_im, 0.0)
    b_im = jnp.where(inside, g_re * f_im + g_im * f_re, 0.0)
    gain_here = jnp.concatenate([b_re, jnp.where(left, -b_im, b_im)], 1)
    gain_here = jnp.concatenate(halves(gain_here), 1)
    side_row = side[0:1]
    twice = jnp.concatenate([twice_re, twice_im * side_row], 1)
    k_re, k_im = rows[:, 4:5], rows[:, 5:6]
    f_re = once_re * k_re - once_im * k_im
    f_im = once_re * k_im + once_im * k_re
    h_re = jnp.where(inside, g_re * f_re - g_im * f_im, 0.0)
    h_im = jnp.where(inside, g_re * f_im + g_im * f_re, 0.0)
    top, bottom = jnp.where(left, h_re, h_im), jnp.where(left, -h_im, h_re)
    wrap_here = jnp.concatenate([top[:64], bottom[:64], top[64:], bottom[64:]], 0)
    wrap_here = jnp.concatenate(halves(wrap_here), 1)
    return (resonances, couple_row, couple_grid, gain, wrap_a, wrap_b, mixing, gain_here,
            twice, wrap_here)


def half_sign(shape):
    return jnp.where(iota(shape, 1) < 64, -1.0, 1.0)


def wrap_state(resonances, weighted, roll):
    product = dot(resonances, jnp.concatenate(halves(weighted), 1))
    product = quadrants(product, 1024, 128)
    lane = iota((BINS, 128), 1) % 16
    sums = []
    for part in range(2):
        total = jnp.zeros((BINS, 128), F32)
        for w1 in range(16):
            start = (part * 16 + w1) * BINS
            total = total + jnp.where(lane == w1, product[start : start + BINS], 0.0)
        sums.append(total)
    return sums[0] + half_sign((BINS, 128)) * roll(sums[1], 64)


def to_rows(field, couple_row, resonances, wrap_a, wrap_b, wide, small, tc, ts, roll):
    mixed = table_times(small, field)
    re, im = mixed[:64], mixed[64:]
    re, im = re * tc + im * ts, im * tc - re * ts
    both = jnp.concatenate(
        [jnp.concatenate([re, im], 1), jnp.concatenate([im, -re], 1)], 0
    )
    product = dot_nt(wide, jnp.concatenate(halves(both), 0))
    spectrum = quadrants(product, 256, 128)
    weighted = wrap_a * spectrum + wrap_b * roll(spectrum, 64)
    state = wrap_state(resonances, weighted, roll)
    place = (iota((128, 256), 0) // 16 == iota((128, 256), 1) % 128 // 16).astype(BF16)
    parts = dot(jnp.concatenate(thirds(state), 0), place)
    parts = (parts[:BINS] + parts[BINS : 2 * BINS]) + parts[2 * BINS :]
    lane = iota((BINS, 256), 1)
    chosen = iota((BINS, 256), 0) == lane // 128 * 16 + lane % 16
    state_row = jnp.sum(jnp.where(chosen, parts, 0.0), axis=0, keepdims=True)
    tail = jnp.concatenate([state_row, couple_row], 1)
    return jnp.concatenate([spectrum, jnp.broadcast_to(tail, (256, 384))], 1)


def diffract(blocks, wide, mixing, roll):
    sign = half_sign((256, 128))

    def transform(parts, direction):
        columns = []
        for part in parts:
            turned = roll(part, 64) * (sign * (-direction))
            columns += list(halves(jnp.concatenate([part, turned], 0)))
        product = dot(wide, jnp.concatenate(columns, 1))
        return [
            quadrants(product[:, 256 * k : 256 * k + 256], 256, 128) for k in range(len(parts))
        ]

    spectra = transform(blocks, 1.0)
    mixed = []
    for part in spectra:
        total = mixing[0] * part
        for r in range(1, 8):
            total = total + mixing[r] * roll(part, 128 - 16 * r)
        mixed.append(total)
    return transform(mixed, -1.0)


def columns_step(message, wide, mixing, gain_here, twice, wrap_here, roll):
    field, state0, state1, couple = (message[:, 128 * k : 128 * k + 128] for k in range(4))
    field, state0, state1 = diffract([field, state0, state1], wide, mixing, roll)
    factor = times_table(couple, gain_here) + twice
    turned = roll(couple, 64)
    left = iota((256, 128), 1) < 64
    states = jnp.concatenate(
        [state0 * jnp.where(left, couple, turned), state1 * jnp.where(left, turned, couple)], 1
    )
    wrapped = times_table(states, wrap_here)
    field = factor[:, :128] * field + factor[:, 128:] * roll(field, 64) + wrapped
    return diffract([field], wide, mixing, roll)[0]


def to_blocks(spectrum, params, resonances, couple_grid, gain, back_re, back_im, tall,
              small_back, tc, ts, roll):
    sign = half_sign((256, 128))
    weighted = back_re * spectrum + (back_im * sign) * roll(spectrum, 64)
    state = wrap_state(resonances, weighted, roll)
    state = params[:, 4:5] * state + params[:, 5:6] * (
        half_sign((BINS, 128)) * roll(state, 64)
    )
    gather = (iota((128, 128), 0) // 16 == iota((128, 128), 1) // 16).astype(BF16)
    spread = sum(dot_nt(gather, jnp.concatenate([part] * 16, 0)) for part in thirds(state))
    k_re, k_im = couple_grid * spread[:64], couple_grid * spread[64:]
    left = jnp.concatenate(
        [jnp.concatenate([k_re, -k_im], 1), jnp.concatenate([k_im, k_re], 1)], 0
    )
    left_high, left_low = halves(left)
    wrapped = dot(jnp.concatenate([left_high, left_low], 0), resonances[:1024])
    wrapped = (wrapped[:128] + wrapped[128:]) + dot(left_high, resonances[1024:])
    turned = spectrum.T
    re, im = turned[:64], turned[64:]
    gain_re, gain_im = gain[:64], gain[64:]
    out_re = re + (re * gain_re - im * gain_im) + wrapped[:64]
    out_im = im + (re * gain_im + im * gain_re) + wrapped[64:]
    both = jnp.concatenate(
        [jnp.concatenate([out_re, -out_im], 1), jnp.concatenate([out_im, out_re], 1)], 0
    )
    mixed = times_table(both, tall)
    re, im = mixed[:64], mixed[64:]
    mixed = jnp.concatenate([re * tc - im * ts, im * tc + re * ts], 0)
    return table_times(small_back, mixed) * (1.0 / NT)


def lane_roll(value, shift):
    return pltpu.roll(value, shift, 1)


def call(kernel, out_shape, *operands, flops, smem=0):
    in_specs = [pl.BlockSpec(memory_space=pltpu.SMEM)] * smem + [
        pl.BlockSpec(memory_space=pltpu.VMEM)
    ] * (len(operands) - smem)
    several = isinstance(out_shape, tuple)
    out_spec = pl.BlockSpec(memory_space=pltpu.VMEM)
    moved = sum(x.size * x.dtype.itemsize for x in operands)
    return pl.pallas_call(
        kernel,
        out_shape=out_shape,
        in_specs=in_specs,
        out_specs=(out_spec,) * len(out_shape) if several else out_spec,
        compiler_params=pltpu.CompilerParams(vmem_limit_bytes=40 * 1024 * 1024),
        cost_estimate=pl.CostEstimate(flops=flops, bytes_accessed=moved, transcendentals=0),
    )(*operands)


def shape(*dims, dtype=F32):
    return jax.ShapeDtypeStruct(dims, dtype)


def prepare_kernel(place, params, group_bin, occupation, spectral, lateral, omega_rows,
                   omega_lanes, back_re, back_im, twiddle_a, twiddle_b, *outs):
    here, quad = place[0], place[1]
    omega_row = jnp.concatenate(
        [omega_lanes[0, pl.ds(here, 1), :], omega_lanes[1, pl.ds(here, 1), :]], 0
    )
    phase_row = spectral[pl.ds(here, 1), :]
    made = prepare(
        params[...], group_bin[...], occupation[...], spectral[...], lateral[...],
        omega_rows[...], omega_row, phase_row, back_re[...], back_im[...], twiddle_a, twiddle_b,
        quad,
    )
    for out, value in zip(outs, made):
        if isinstance(value, list):
            for k, part in enumerate(value):
                out[k] = part
        else:
            out[...] = value


def rows_kernel(field, couple_row, resonances, wrap_a, wrap_b, wide, small, tc, ts, out):
    out[...] = to_rows(
        field[...], couple_row[...], resonances[...], wrap_a[...], wrap_b[...], wide[...],
        small[...], tc[...], ts[...], lane_roll,
    )


def columns_kernel(message, wide, mixing, gain_here, twice, wrap_here, out):
    out[...] = columns_step(
        message[...], wide[...], mixing, gain_here[...], twice[...], wrap_here[...], lane_roll
    )


def blocks_kernel(spectrum, params, resonances, couple_grid, gain, back_re, back_im, tall,
                  small_back, tc, ts, out):
    out[...] = to_blocks(
        spectrum[...], params[...], resonances[...], couple_grid[...], gain[...], back_re[...],
        back_im[...], tall[...], small_back[...], tc[...], ts[...], lane_roll,
    )


def bin_params(bin_decay, bin_detune):
    keep = jnp.exp(-bin_decay)
    p_re, p_im = keep * jnp.cos(bin_detune), -keep * jnp.sin(bin_detune)
    whole = jnp.exp(-NT * bin_decay)
    r_re = 1.0 - whole * jnp.cos(NT * bin_detune)
    r_im = whole * jnp.sin(NT * bin_detune)
    k_re, k_im = p_re * r_re - p_im * r_im, p_re * r_im + p_im * r_re
    return jnp.stack(
        [
            bin_detune, keep, -jnp.expm1(-bin_decay), jnp.sqrt(-jnp.expm1(-2.0 * bin_decay)),
            WEIGHT * k_im, -WEIGHT * k_re, keep, keep,
        ],
        axis=1,
    )


def parameter_forms(lateral_phase, spectral_phase, occupation, bin_decay, bin_detune, group_bin):
    return (
        bin_params(bin_decay, bin_detune),
        group_bin[None, :],
        jnp.pad(occupation, ((0, 0), (0, 128 - occupation.shape[1]))),
        jnp.tile(spectral_phase.reshape(256, 16), (1, 8)),
        lateral_phase.reshape(4, 256).T,
    )


def on_device(
    light_field, lateral_phase, spectral_phase, occupation, bin_decay, bin_detune, group_bin
):
    t = {name: jnp.asarray(value) for name, value in TABLES.items()}
    lat, tm = lax.axis_index("lat"), lax.axis_index("tm")
    blocks = light_field.reshape(2, 16, 4, 256).transpose(1, 0, 2, 3).reshape(16, 8, 256)
    rows = lax.all_to_all(blocks, "tm", 0, 0, tiled=True).reshape(128, 256)
    forms = parameter_forms(
        lateral_phase, spectral_phase, occupation, bin_decay, bin_detune, group_bin
    )
    place = jnp.stack([lat * 16 + tm, tm]).astype(jnp.int32)
    (resonances, couple_row, couple_grid, gain, wrap_a, wrap_b, mixing, gain_here, twice,
     wrap_here) = call(
        prepare_kernel,
        (
            shape(2048, 256, dtype=BF16), shape(1, 128), shape(64, 512), shape(128, 256),
            shape(256, 128), shape(256, 128), shape(8, 256, 128), shape(128, 512, dtype=BF16),
            shape(1, 256), shape(256, 256, dtype=BF16),
        ),
        place, *forms, t["omega_rows"], t["omega_lanes"], t["back_re"], t["back_im"],
        t["twiddle_a"], t["twiddle_b"],
        flops=200_000_000, smem=1,
    )
    message = call(
        rows_kernel, shape(256, 512),
        rows, couple_row, resonances, wrap_a, wrap_b, t["wide"], t["small"], t["tc"], t["ts"],
        flops=500_000_000,
    )
    message = lax.all_to_all(message, BOTH, 0, 0, tiled=True)
    columns = call(
        columns_kernel, shape(256, 128),
        message, t["wide"], mixing, gain_here, twice, wrap_here,
        flops=1_000_000_000,
    )
    spectrum = lax.all_to_all(columns, BOTH, 0, 0, tiled=True)
    finished = call(
        blocks_kernel, shape(128, 256),
        spectrum, forms[0], resonances, couple_grid, gain, t["back_re"], t["back_im"],
        t["tall"], t["small_back"], t["tc"], t["ts"],
        flops=800_000_000,
    )
    turned = lax.all_to_all(finished.reshape(16, 8, 256), "tm", 0, 0, tiled=True)
    return turned.reshape(16, 2, 4, 256).transpose(1, 0, 2, 3).reshape(2, 64, 256)


def solution(mesh):
    return jax.shard_map(
        on_device,
        mesh=mesh,
        in_specs=(P(None, "lat", "tm"), P(), P(), P(None, "lat"), P(), P(), P()),
        out_specs=P(None, "lat", "tm"),
        check_vma=False,
    )
```

time: 881 us -> 108 us (0.12); the launches traced: 870 us -> 108 us
  matrix products: 418 us -> 0 us
  local copies, waits for them, and re-layouts: 218 us -> 23 us
  blocking collectives: 142 us -> 64.9 us
  other arithmetic: 33.5 us -> 0.8 us
  waiting for transfers between devices: 25.6 us -> 0.01 us
  starting transfers between devices: 30.6 us -> 9.98 us
    dot_general x68 -> x0, matrix products: 416 us -> none  [the longest x16 106 us: complex_einsum(): jnp.einsum(form, left[0], right[1], precision=exact)]
    gather x4 -> x0, local copies, waits for them, and re-layouts: 124 us -> none  [the longest x2 61.9 us: on_device(): jnp.take(jnp.dot(coupling.T, lag_powers[0][:STRETCH].T, precision=exact),...]
    all_gather x6 -> x0, blocking collectives: 106 us -> none  [carried_in(): pieces = jax.tree.map(lambda part: lax.all_gather(part, axis), value)]
    unnamed x61 -> x72, local copies, waits for them, and re-layouts: 52.6 us -> 17.3 us
    all_to_all x3, blocking collectives: 36.3 us -> 64.9 us  [the longest x1 34.1 us: on_device(): message = lax.all_to_all(message, BOTH, 0, 0, tiled=True)]
    all_to_all x5 -> x1, waiting for transfers between devices: 25.6 us -> 0.01 us  [on_device(): rows = lax.all_to_all(blocks, 'tm', 0, 0, tiled=True).reshape(128, 256)]
    all_to_all x5 -> x1, starting transfers between devices: 30.6 us -> 9.98 us  [on_device(): rows = lax.all_to_all(blocks, 'tm', 0, 0, tiled=True).reshape(128, 256)]
    select_n x30 -> x0, other arithmetic: 16.4 us -> none  [lap(): jnp.where(position < mine, new, old)]
  transfers between devices with their start and end apart: 5 -> 1, of which waited for: 4 -> 0; matrix products, arithmetic and copies ran while one was open for 15% -> 4% of each run, Pallas kernels for 0% -> 2%
where the time goes in v1:
time: 108 us
  blocking collectives  64.9 us (60%)
  local copies, waits for them, and re-layouts  23 us (21%)
  starting transfers between devices  9.98 us (9%)
  Pallas kernels  8.71 us (8%)
    all_to_all x1, blocking collectives, on_device(): message = lax.all_to_all(message, BOTH, 0, 0, tiled=True)  34.1 us
    all_to_all x1, blocking collectives, on_device(): spectrum = lax.all_to_all(columns, BOTH, 0, 0, tiled=True)  18.3 us
    unnamed x72, local copies, waits for them, and re-layouts  17.3 us
    all_to_all x1, blocking collectives, on_device(): lax.all_to_all(finished.reshape(16, 8, 256), 'tm', 0, 0, tiled=True)  12.5 us
    all_to_all x1, starting transfers between devices, on_device(): rows = lax.all_to_all(blocks, 'tm', 0, 0, tiled=True).reshape(128, 256)  9.98 us
    pallas_call x4, Pallas kernels, call(): pl.pallas_call(kernel, out_shape=out_shape, in_specs=in_specs, out_specs=...  8.71 us
  transfers between devices with their start and end apart: 1, of which 0 were waited for; matrix products, arithmetic and copies ran while one was open for 4% of the time, Pallas kernels for 2%

profile of v1, /device:TPU:1, one launch (start us, length us, event | category | flops | bytes accessed | tf_op | source)
XLA Modules:
  0.0 107.6 jit_solution(4495364451335703284)
XLA Ops:
  0.0 1.1 %reshape.29 = f32[2,16,4,256]{3,2,1,0:T(4,128)S(1)} reshape(f32[2,64,256]{2,1,0:T(8,128)} %param.19) | data formatting | bytes 262144 | tf_op jit(solution)/shard_map/reshape | solution.py:424
  1.1 0.7 reshape.30
  1.8 10.0 %all-to-all-start = ((f32[16,8,256]{2,1,0:T(8,128)}), f32[16,8,256]{2,1,0:T(8,128)S(1)}, u32[]{:S(2)}, u32[]{:S(2)}) async-start(f32[16,8,256]{2,1,0:T(8,128)} %reshape.30), calls=%async_computation | async-start | bytes 262144 | tf_op jit(solution)/shard_map/all_to_all | solution.py:425
  11.8 0.7 reshape.32
  12.5 0.7 multiply_bitcast_fusion
  13.2 0.7 stack.41
  13.9 0.1 copy.49.params
  14.0 0.8 copy.46
  14.8 0.1 copy.48
  15.0 0.8 tile.10
  15.8 0.1 copy.47
  15.9 0.1 copy.50.spectral
  16.0 0.0 copy-start.17
  16.0 0.1 pad_add_fusion.place
  16.1 0.0 copy-done
  16.1 0.0 copy-done.1
  16.1 0.6 copy-done.17
  16.7 0.0 copy-done.20
  16.8 0.9 copy-done.3
  17.7 0.9 copy-done.4
  18.6 0.9 copy-done.6
  19.5 2.3 %shard_map.181 = (bf16[2048,256]{1,0:T(8,128)(2,1)S(1)}, f32[1,128]{1,0:T(1,128)S(1)}, f32[64,512]{1,0:T(8,128)S(1)}, f32[128,256]{1,0:T(8,128)S(1)}, f32[256,12...) custom-call(s32[2]{0:T(128)S(1)} %pad_add_fusion.place, ...), custom_call_target="tpu_custom_call" | custom-call | flops 200000000 | bytes 2856456 | tf_op jit(solution)/shard_map/pallas_call | solution.py:338
  21.8 0.0 copy-start.8
  21.8 0.7 copy-done.8
  22.5 0.7 copy-done.10
  23.2 0.6 copy-done.18
  23.7 1.0 copy-done.21
  24.7 0.7 copy-done.23
  25.3 0.6 copy-done.25
  26.0 0.6 copy-done.27
  26.6 0.6 copy-done.29
  27.3 0.6 copy-done.31
  27.8 0.0 all-to-all-done
  27.8 0.7 copy-done.19
  28.5 1.0 copy-done.2
  29.5 0.9 copy-done.9
  30.4 0.9 copy-done.11
  31.4 0.8 copy-done.12
  32.2 0.8 copy-done.14
  33.0 0.8 copy-done.16
  33.9 1.4 %shard_map.182 = f32[256,512]{1,0:T(8,128)S(1)} custom-call(f32[128,256]{1,0:T(8,128)S(1)} %bitcast.31, f32[1,128]{1,0:T(1,128)S(1)} %copy-done.19, bf16[2048,256]{1,0:T(8,128)(2,1)S(1)} %get-tuple-element.16.resonances, f32[256,128]{1,0:T(8,128)S(1)} %copy-done.9, f32[256,128]{1,0:T(8,128)S(1)} %copy-done.11, bf16[512,512]{1,0:T(8,128)(2,1)S(1)} %copy-done.2, ...), custom_call_target="tpu_custom_call" | custom-call | flops 500000000 | bytes 2163200 | tf_op jit(solution)/shard_map/pallas_call | solution.py:338
  35.3 0.5 copy.51
  35.9 0.0 copy-start.22
  35.9 34.1 %all_to_all.32 = f32[256,1,512]{2,1,0:T(1,128)S(1)} all-to-all(f32[256,1,512]{2,1,0:T(1,128)S(1)} %copy.51), channel_id=1, replica_groups=mesh['lat'=16,'tm'=16] {'lat','tm'}, dimensions={0} | all-to-all | bytes 1048576 | tf_op jit(solution)/shard_map/all_to_all | solution.py:447
  70.0 0.0 copy-start.32
  70.1 0.0 copy-done.22
  70.1 0.8 copy-done.28
  70.9 0.1 copy-done.30
  71.0 0.0 copy-done.32
  71.0 0.0 copy-start.26
  71.0 0.0 copy-start.33
  71.0 0.0 copy-start.34
  71.0 2.8 %shard_map.183 = f32[256,128]{1,0:T(8,128)S(1)} custom-call(f32[256,512]{1,0:T(8,128)S(1)} %bitcast.33, bf16[512,512]{1,0:T(8,128)(2,1)S(1)} %copy-done.2, f32[8,256,128]{2,1,0:T(8,128)S(1)} %copy-done.22, bf16[128,512]{1,0:T(8,128)(2,1)S(1)} %copy-done.28, f32[1,256]{1,0:T(1,128)S(1)} %copy-done.32, bf16[256,256]{1,0:T(8,128)(2,1)S(1)} %copy-done.30), custom_call_target="tpu_custom_call" | custom-call | flops 1000000000 | bytes 2360320 | tf_op jit(solution)/shard_map/pallas_call | solution.py:338
  73.8 0.0 copy-start.5
  73.8 0.0 copy-start.7
  73.9 18.3 %all_to_all.33 = f32[256,1,128]{2,1,0:T(1,128)S(1)} all-to-all(f32[256,1,128]{2,1,0:T(1,128)S(1)} %bitcast.36), channel_id=1, replica_groups=mesh['lat'=16,'tm'=16] {'lat','tm'}, dimensions={0} | all-to-all | bytes 262144 | tf_op jit(solution)/shard_map/all_to_all | solution.py:453
  92.1 0.0 copy-done.13
  92.1 0.0 copy-done.15
  92.1 0.0 copy-done.24
  92.1 0.0 copy-done.26
  92.1 0.0 copy-done.33
  92.2 2.2 %shard_map.184 = f32[128,256]{1,0:T(8,128)S(1)} custom-call(f32[256,128]{1,0:T(8,128)S(1)} %bitcast.34, f32[32,8]{1,0:T(8,128)S(1)} %copy.49.params, bf16[2048,256]{1,0:T(8,128)(2,1)S(1)} %get-tuple-element.16.resonances, f32[64,512]{1,0:T(8,128)S(1)} %copy-done.24, f32[128,256]{1,0:T(8,128)S(1)} %copy-done.26, f32[256,128]{1,0:T(8,128)S(1)} %copy-done.7, ...), custom_call_target="tpu_custom_call" | custom-call | flops 800000000 | bytes 2425856 | tf_op jit(solution)/shard_map/pallas_call | solution.py:338
  94.4 12.5 %all_to_all.34 = f32[16,8,256]{2,1,0:T(8,128)S(1)} all-to-all(f32[16,8,256]{2,1,0:T(8,128)S(1)} %bitcast.35), channel_id=1, replica_groups=mesh['lat'=16,'tm'=16] {'tm'}, dimensions={0} | all-to-all | bytes 262144 | tf_op jit(solution)/shard_map/all_to_all | solution.py:460
  106.9 0.7 reshape.35
  (35 shorter events, 0.2 us)
Async XLA Ops:
  0.0 16.1 %copy-start = (f32[8,256,128]{2,1,0:T(8,128)S(1)}, f32[8,256,128]{2,1,0:T(8,128)}, u32[]{:S(2)}) copy-start(f32[8,256,128]{2,1,0:T(8,128)} %constant.59.clone.twiddle_b) | copy-start | bytes 3145732
  0.0 16.1 %copy-start.1 = (f32[8,256,128]{2,1,0:T(8,128)S(1)}, f32[8,256,128]{2,1,0:T(8,128)}, u32[]{:S(2)}) copy-start(f32[8,256,128]{2,1,0:T(8,128)} %constant.58.clone.twiddle_a) | copy-start | bytes 3145732
  1.8 26.0 %all-to-all-start = ((f32[16,8,256]{2,1,0:T(8,128)}), f32[16,8,256]{2,1,0:T(8,128)S(1)}, u32[]{:S(2)}, u32[]{:S(2)}) async-start(f32[16,8,256]{2,1,0:T(8,128)} %reshape.30), calls=%async_computation | async-start | bytes 262144 | tf_op jit(solution)/shard_map/all_to_all | solution.py:425
  16.0 0.8 copy-start.17
  16.1 0.7 copy-start.20
  16.8 0.9 copy-start.3
  17.7 0.9 copy-start.4
  18.6 0.9 copy-start.6
  21.8 0.7 copy-start.8
  22.5 0.7 copy-start.10
  23.2 0.6 copy-start.18
  23.7 1.0 copy-start.21
  24.7 0.7 copy-start.23
  25.3 0.6 copy-start.25
  26.0 0.6 copy-start.27
  26.6 0.6 copy-start.29
  27.3 0.6 copy-start.31
  27.8 0.7 copy-start.19
  28.5 1.0 copy-start.2
  29.5 0.9 copy-start.9
  30.4 0.9 copy-start.11
  31.3 0.8 copy-start.12
  32.2 0.8 copy-start.14
  33.0 0.8 copy-start.16
  35.9 34.2 %copy-start.22 = (f32[8,256,128]{2,1,0:T(8,128)S(1)}, f32[8,256,128]{2,1,0:T(8,128)}, u32[]{:S(2)}) copy-start(f32[8,256,128]{2,1,0:T(8,128)} %copy-done.21) | copy-start | bytes 3145732
  70.0 0.9 copy-start.28
  70.0 1.0 copy-start.30
  70.0 0.9 copy-start.32
  71.0 21.1 %copy-start.13 = (f32[64,256]{1,0:T(8,128)S(1)}, f32[64,256]{1,0:T(8,128)}, u32[]{:S(2)}) copy-start(f32[64,256]{1,0:T(8,128)} %constant.53.clone.ts) | copy-start | bytes 196612
  71.0 21.1 %copy-start.15 = (f32[64,256]{1,0:T(8,128)S(1)}, f32[64,256]{1,0:T(8,128)}, u32[]{:S(2)}) copy-start(f32[64,256]{1,0:T(8,128)} %constant.52.clone.tc) | copy-start | bytes 196612
  71.0 21.1 %copy-start.24 = (f32[64,512]{1,0:T(8,128)S(1)}, f32[64,512]{1,0:T(8,128)}, u32[]{:S(2)}) copy-start(f32[64,512]{1,0:T(8,128)} %copy-done.23) | copy-start | bytes 393220
  71.0 21.1 %copy-start.26 = (f32[128,256]{1,0:T(8,128)S(1)}, f32[128,256]{1,0:T(8,128)}, u32[]{:S(2)}) copy-start(f32[128,256]{1,0:T(8,128)} %copy-done.25) | copy-start | bytes 393220
  71.0 21.1 %copy-start.33 = (bf16[512,512]{1,0:T(8,128)(2,1)S(1)}, bf16[512,512]{1,0:T(8,128)(2,1)}, u32[]{:S(2)}) copy-start(bf16[512,512]{1,0:T(8,128)(2,1)} %constant.49.clone.tall) | copy-start | bytes 1572868
  71.0 21.1 %copy-start.34 = (bf16[256,128]{1,0:T(8,128)(2,1)S(1)}, bf16[256,128]{1,0:T(8,128)(2,1)}, u32[]{:S(2)}) copy-start(bf16[256,128]{1,0:T(8,128)(2,1)} %constant.51.clone.small_back) | copy-start | bytes 196612
  73.8 18.3 %copy-start.5 = (f32[256,128]{1,0:T(8,128)S(1)}, f32[256,128]{1,0:T(8,128)}, u32[]{:S(2)}) copy-start(f32[256,128]{1,0:T(8,128)} %constant.57.clone.back_im) | copy-start | bytes 393220
  73.8 18.3 %copy-start.7 = (f32[256,128]{1,0:T(8,128)S(1)}, f32[256,128]{1,0:T(8,128)}, u32[]{:S(2)}) copy-start(f32[256,128]{1,0:T(8,128)} %constant.56.clone.back_re) | copy-start | bytes 393220

commit v2 on v1

v2 whole, which is shorter than its diff:
```python
import math

import jax
import jax.numpy as jnp
import numpy as np
from jax import lax
from jax.experimental import pallas as pl
from jax.experimental.pallas import tpu as pltpu
from jax.sharding import PartitionSpec as P

NX, NT, BINS, GROUPS = 1024, 4096, 32, 128
WEIGHT = 0.5 / math.sqrt(GROUPS)
F32, BF16 = jnp.float32, jnp.bfloat16
BOTH = ("lat", "tm")


def split_table(table):
    high = table.astype(np.float32).astype(jnp.bfloat16)
    low = (table - high.astype(np.float64)).astype(jnp.bfloat16)
    return high, low


def build_tables():
    grid = np.arange
    angle = 2 * np.pi * (grid(256)[:, None] * grid(256)[None, :] % 256) / 256
    wide = np.concatenate([np.cos(angle), np.sin(angle)], 1)
    tall = np.concatenate([np.cos(angle), np.sin(angle)], 0)
    lane = grid(128)
    c, q, col = lane // 64, lane // 16 % 4, lane % 16
    to, row = grid(256), grid(256)
    th, tc, tq, tw = to // 128, to // 64 % 2, to // 16 % 4, to % 16
    rm, rc, rh, rq = row // 16, row // 8 % 2, row // 4 % 2, row % 4
    turn = 2 * np.pi * (tw[:, None] * rm[None, :] % 16) / 16
    sign = np.where(tc[:, None] == 0, 1.0, -1.0)
    small = np.where(tc[:, None] == rc[None, :], np.cos(turn), sign * np.sin(turn))
    small = small * (tq[:, None] == rq[None, :]) * (th[:, None] == rh[None, :])
    short = 2 * np.pi * (col[:64, None] * grid(256)[None, :]) / NT
    omega_lanes = np.tile(2 * np.pi * (16 * grid(256)[:, None] + grid(16)[None, :]) / NT, (1, 8))
    eight = lane // 16
    twiddle_a = np.zeros((8, 256, 128))
    twiddle_b = np.zeros((8, 256, 128))
    for r in range(8):
        source = (eight + r) % 8
        sc, sq = source // 4, source % 4
        theta = -2 * np.pi * ((sq - q)[None, :] * grid(256)[:, None]) / NX
        re, im = np.cos(theta), np.sin(theta)
        same_part = (sc == c)[None, :]
        flip = np.where(c == 0, -1.0, 1.0)[None, :]
        twiddle_a[r] = np.where(same_part, re, flip * im) / NX
        twiddle_b[r] = np.where(same_part, -im, flip * re) / NX
    t = {}
    t["wide"] = np.concatenate(split_table(wide), 0)
    t["small"] = np.concatenate(split_table(small), 0)
    t["back"] = np.concatenate(split_table(tall) + split_table(small.T), 0)
    t["twist"] = np.concatenate([np.cos(short), np.sin(short)], 0).astype(np.float32)
    omega_part = np.concatenate([np.cos(omega_lanes), -np.sin(omega_lanes)], 0)
    t["shift"] = (omega_part / NT).astype(np.float32)
    t["twiddle_a"] = twiddle_a.astype(np.float32)
    t["twiddle_b"] = twiddle_b.astype(np.float32)
    return t


STEP = 2 * math.pi / NT
STEP_HIGH = round(STEP * 2**22) / 2**22
STEP_LOW = STEP - STEP_HIGH
TURN = (6.28125, 2 * math.pi - 6.28125)
TABLES = build_tables()


def iota(shape, dim):
    return lax.broadcasted_iota(jnp.int32, shape, dim)


def halves(value):
    high = value.astype(BF16)
    return high, (value - high.astype(F32)).astype(BF16)


def thirds(value):
    high = value.astype(BF16)
    rest = value - high.astype(F32)
    middle = rest.astype(BF16)
    return high, middle, (rest - middle.astype(F32)).astype(BF16)


def dot(left, right):
    return lax.dot_general(left, right, (((1,), (0,)), ((), ())), preferred_element_type=F32)


def dot_nt(left, right):
    return lax.dot_general(left, right, (((1,), (1,)), ((), ())), preferred_element_type=F32)


def quadrants(product, rows, cols):
    return product[:rows, :cols] + (product[:rows, cols:] + product[rows:, :cols])


def table_times(table, value):
    product = dot(table, jnp.concatenate(halves(value), 1))
    return quadrants(product, table.shape[0] // 2, value.shape[1])


def times_table(value, table):
    product = dot(jnp.concatenate(halves(value), 0), table)
    return quadrants(product, value.shape[0], table.shape[1] // 2)


def sine_cosine_half(angle):
    x = angle * 0.5
    z = x * x
    s = jnp.full_like(z, 1.0 / 6227020800.0)
    for k in (-1.0 / 39916800.0, 1.0 / 362880.0, -1.0 / 5040.0, 1.0 / 120.0, -1.0 / 6.0):
        s = s * z + k
    c = jnp.full_like(z, -1.0 / 87178291200.0)
    for k in (1.0 / 479001600.0, -1.0 / 3628800.0, 1.0 / 40320.0, -1.0 / 720.0, 1.0 / 24.0, -0.5):
        c = c * z + k
    return x + x * (z * s), 1.0 + z * c


def resonance(detune, keep, lost, index):
    index = jnp.where(index > NT // 2, index - NT, index).astype(F32)
    s, c = sine_cosine_half((detune + index * STEP_HIGH) + index * STEP_LOW)
    re = lost + (2.0 * keep) * (s * s)
    im = (2.0 * keep) * (s * c)
    scale = 1.0 / (re * re + im * im)
    return re * scale, -(im * scale)


def cosine_sine(angle):
    s, c = sine_cosine_half(angle)
    return 1.0 - 2.0 * (s * s), 2.0 * (s * c)


def lost_by(rate):
    total = jnp.full_like(rate, 1.0 / 5040.0)
    for k in (-1.0 / 720.0, 1.0 / 120.0, -1.0 / 24.0, 1.0 / 6.0, -0.5, 1.0):
        total = k + rate * total
    return rate * total


def exact_dot(left, right):
    parts = thirds(left)
    return (dot(parts[0], right) + dot(parts[1], right)) + dot(parts[2], right)


def pick_dot(left, right):
    parts = thirds(right)
    return (dot(left, parts[0]) + dot(left, parts[1])) + dot(left, parts[2])


def pick_dot_nt(left, right):
    parts = thirds(right)
    return (dot_nt(left, parts[0]) + dot_nt(left, parts[1])) + dot_nt(left, parts[2])


def bin_columns(decay, detune):
    lost = lost_by(decay)
    keep = 1.0 - lost
    drive = jnp.sqrt(lost_by(2.0 * decay))
    cos, sin = cosine_sine(detune)
    p_re, p_im = keep * cos, -keep * sin
    whole = jnp.exp(-float(NT) * decay)
    far = float(NT) * detune
    turns = jnp.floor(far * (0.5 / math.pi) + 0.5)
    cos, sin = cosine_sine((far - turns * TURN[0]) - turns * TURN[1])
    r_re, r_im = 1.0 - whole * cos, whole * sin
    k_re, k_im = p_re * r_re - p_im * r_im, p_re * r_im + p_im * r_re
    rows = jnp.concatenate(
        [detune, keep, lost, drive, WEIGHT * k_im, -WEIGHT * k_re, keep, keep], 0
    )
    eye = (iota((BINS, BINS), 0) == iota((BINS, BINS), 1)).astype(BF16)
    return pick_dot_nt(eye, rows)


def prepare(decay, detune_row, group_bin, occupation, spectral, lateral, shift, twiddle_a,
            twiddle_b, here, quad):
    params = bin_columns(decay, detune_row)
    detune, keep, lost, drive = (params[:, k : k + 1] for k in range(4))
    real, imag = [], []
    for w1 in range(16):
        g_re, g_im = resonance(detune, keep, lost, 16 * iota((BINS, 256), 1) + w1)
        real.append(g_re)
        imag.append(g_im)
    resonances = jnp.concatenate(halves(jnp.concatenate(real + imag, 0)), 0)
    member = (iota((BINS, GROUPS), 0) == group_bin).astype(BF16)
    per_bin = pick_dot(member, occupation) * drive
    points = occupation.shape[1]
    pick = iota((points, 128), 0) == 4 * quad + iota((points, 128), 1) // 16 % 4
    chosen = exact_dot(per_bin, pick.astype(BF16))
    lane = iota((BINS, 128), 1)
    couple_row = jnp.sum(
        jnp.where(iota((BINS, 128), 0) == lane // 64 * 16 + lane % 16, chosen, 0.0),
        axis=0, keepdims=True,
    )
    pick_rows = iota((64, points), 1) == 4 * quad + iota((64, points), 0) // 16
    spread = pick_dot_nt(pick_rows.astype(BF16), jnp.concatenate([per_bin] * 16, 0))
    couple_grid = jnp.where(
        iota((64, 512), 1) // 32 == iota((64, 512), 0) % 16, spread, 0.0
    )
    gain_high, gain_low = halves(couple_grid * WEIGHT)
    gain = dot(jnp.concatenate([gain_high, gain_low], 0),
               jnp.concatenate([resonances[:512], resonances[512:1024]], 1))
    gain_rest = dot(gain_high, jnp.concatenate([resonances[1024:1536], resonances[1536:]], 1))
    gain = (gain[:64] + gain[64:]) + gain_rest
    gain = jnp.concatenate([-gain[:, 256:], gain[:, :256]], 0)
    cos, sin = cosine_sine(spectral)
    row_of = (iota((256, 32), 0) // 8 == iota((256, 32), 1)).astype(BF16)
    mine = iota((256, 128), 1) // 16 == iota((256, 128), 0) % 8
    lane_of = (iota((128, 128), 0) % 16 == iota((128, 128), 1) % 16).astype(BF16)
    cos = exact_dot(jnp.where(mine, pick_dot(row_of, cos), 0.0), lane_of)
    sin = exact_dot(jnp.where(mine, pick_dot(row_of, sin), 0.0), lane_of)
    side = jnp.where(iota((256, 128), 1) < 64, -1.0, 1.0)
    wrap_a = cos * shift[:256] - sin * shift[256:]
    wrap_b = (cos * shift[256:] + sin * shift[:256]) * side
    own = iota((256, 128), 0) == here
    once_re = jnp.sum(jnp.where(own, cos, 0.0), axis=0, keepdims=True)
    once_im = jnp.sum(jnp.where(own, sin, 0.0), axis=0, keepdims=True)
    eye = (iota((128, 128), 0) == iota((128, 128), 1)).astype(BF16)
    cos, sin = cosine_sine(lateral)
    cos, sin = pick_dot_nt(eye, cos), pick_dot_nt(eye, sin)
    r, i = (
        [
            jnp.concatenate([x[:, 2 * k : 2 * k + 1], x[:, 2 * k + 1 : 2 * k + 2]], 0)
            for k in range(4)
        ]
        for x in (cos, sin)
    )
    blocks_re = [
        (r[0] + r[2]) + (r[1] + r[3]),
        (r[0] - r[2]) + (i[1] - i[3]),
        (r[0] + r[2]) - (r[1] + r[3]),
        (r[0] - r[2]) - (i[1] - i[3]),
    ]
    blocks_im = [
        (i[0] + i[2]) + (i[1] + i[3]),
        (i[0] - i[2]) - (r[1] - r[3]),
        (i[0] + i[2]) - (i[1] + i[3]),
        (i[0] - i[2]) + (r[1] - r[3]),
    ]
    mixing = jnp.concatenate(
        [twiddle_a[k] * blocks_re[k % 4] + twiddle_b[k] * blocks_im[k % 4] for k in range(8)], 0
    )
    rows = jnp.concatenate([params[:16]] * 4 + [params[16:]] * 4, 0)
    g_re, g_im = resonance(
        rows[:, 0:1], rows[:, 1:2], rows[:, 2:3], 16 * here + iota((128, 128), 1) % 16
    )
    twice_re = once_re * once_re - once_im * once_im
    twice_im = 2.0 * once_re * once_im
    inside = iota((128, 128), 0) // 16 % 4 == iota((128, 128), 1) // 16 % 4
    left = iota((128, 128), 1) < 64
    f_re, f_im = -WEIGHT * twice_im, WEIGHT * twice_re
    b_re = jnp.where(inside, g_re * f_re - g_im * f_im, 0.0)
    b_im = jnp.where(inside, g_re * f_im + g_im * f_re, 0.0)
    gain_here = jnp.concatenate([b_re, jnp.where(left, -b_im, b_im)], 1)
    gain_here = jnp.concatenate(halves(gain_here), 0)
    side_row = side[0:1]
    twice = jnp.concatenate([twice_re] * 8 + [twice_im * side_row] * 8, 0)
    k_re, k_im = rows[:, 4:5], rows[:, 5:6]
    f_re = once_re * k_re - once_im * k_im
    f_im = once_re * k_im + once_im * k_re
    h_re = jnp.where(inside, g_re * f_re - g_im * f_im, 0.0)
    h_im = jnp.where(inside, g_re * f_im + g_im * f_re, 0.0)
    top, bottom = jnp.where(left, h_re, h_im), jnp.where(left, -h_im, h_re)
    wrap_here = jnp.concatenate([top[:64], bottom[:64], top[64:], bottom[64:]], 0)
    wrap_here = jnp.concatenate(halves(wrap_here), 1)
    first = jnp.concatenate([wrap_a, wrap_b, jnp.broadcast_to(couple_row, (8, 128))], 0)
    second = jnp.concatenate([twice, mixing], 0)
    second_tables = jnp.concatenate([gain_here, wrap_here], 0)
    turned = [jnp.broadcast_to(params[:, k : k + 1], (BINS, 128)) for k in (4, 5)]
    third = jnp.concatenate(
        [couple_grid[:, 128 * k : 128 * k + 128] for k in range(4)]
        + [gain[:, :128], gain[:, 128:]] + turned, 0,
    )
    return resonances, first, second, second_tables, third


def half_sign(shape):
    return jnp.where(iota(shape, 1) < 64, -1.0, 1.0)


def wrap_state(resonances, weighted, roll):
    product = dot(resonances, jnp.concatenate(halves(weighted), 1))
    product = quadrants(product, 1024, 128)
    lane = iota((BINS, 128), 1) % 16
    sums = []
    for part in range(2):
        total = jnp.zeros((BINS, 128), F32)
        for w1 in range(16):
            start = (part * 16 + w1) * BINS
            total = total + jnp.where(lane == w1, product[start : start + BINS], 0.0)
        sums.append(total)
    return sums[0] + half_sign((BINS, 128)) * roll(sums[1], 64)


def to_rows(field, first, resonances, wide, small, twist, roll):
    mixed = table_times(small[...], field)
    mixed = jnp.concatenate([mixed[:128], mixed[128:]], 1)
    re, im = mixed[:64], mixed[64:]
    tc, ts = twist[:64], twist[64:]
    re, im = re * tc + im * ts, im * tc - re * ts
    both = jnp.concatenate(
        [jnp.concatenate([re, im], 1), jnp.concatenate([im, -re], 1)], 0
    )
    product = dot_nt(wide[...], jnp.concatenate(halves(both), 0))
    spectrum = quadrants(product, 256, 128)
    weighted = first[:256] * spectrum + first[256:512] * roll(spectrum, 64)
    state = wrap_state(resonances[...], weighted, roll)
    place = (iota((128, 256), 0) // 16 == iota((128, 256), 1) % 128 // 16).astype(BF16)
    parts = exact_dot(state, place)
    lane = iota((BINS, 256), 1)
    chosen = iota((BINS, 256), 0) == lane // 128 * 16 + lane % 16
    state_row = jnp.sum(jnp.where(chosen, parts, 0.0), axis=0, keepdims=True)
    return spectrum, state_row[:, :128], state_row[:, 128:], first[512:513]


def diffract(blocks, wide, mixing, roll):
    sign = half_sign((256, 128))

    def transform(parts, direction):
        columns = []
        for part in parts:
            turned = roll(part, 64) * (sign * (-direction))
            columns += list(halves(jnp.concatenate([part, turned], 0)))
        product = dot(wide, jnp.concatenate(columns, 1))
        return [
            quadrants(product[:, 256 * k : 256 * k + 256], 256, 128) for k in range(len(parts))
        ]

    spectra = transform(blocks, 1.0)
    mixed = []
    for part in spectra:
        total = mixing[0] * part
        for r in range(1, 8):
            total = total + mixing[r] * roll(part, 128 - 16 * r)
        mixed.append(total)
    return transform(mixed, -1.0)


def columns_step(message, wide, second, second_tables, roll):
    field, state0, state1, couple = message
    mixing = [second[16 + 256 * k : 272 + 256 * k] for k in range(8)]
    field, state0, state1 = diffract([field, state0, state1], wide, mixing, roll)
    product = dot(jnp.concatenate(halves(couple), 0), second_tables[:128])
    rest = dot(couple.astype(BF16), second_tables[128:256])
    factor = (product[:256] + product[256:]) + rest
    turned = roll(couple, 64)
    left = iota((256, 128), 1) < 64
    states = jnp.concatenate(
        [state0 * jnp.where(left, couple, turned), state1 * jnp.where(left, turned, couple)], 1
    )
    wrapped = times_table(states, second_tables[256:])
    straight, crossed = factor[:, :128] + second[0:1], factor[:, 128:] + second[8:9]
    field = straight * field + crossed * roll(field, 64) + wrapped
    return diffract([field], wide, mixing, roll)[0]


def to_blocks(spectrum, resonances, third, back, twist, shift, roll):
    sign = half_sign((256, 128))
    weighted = shift[:256] * spectrum + (shift[256:] * sign) * roll(spectrum, 64)
    state = wrap_state(resonances[...], weighted, roll)
    state = third[512:544] * state + third[544:576] * (
        half_sign((BINS, 128)) * roll(state, 64)
    )
    gather = (iota((128, 128), 0) // 16 == iota((128, 128), 1) // 16).astype(BF16)
    spread = sum(dot_nt(gather, jnp.concatenate([part] * 16, 0)) for part in thirds(state))
    couple_grid = jnp.concatenate([third[64 * k : 64 * k + 64] for k in range(4)], 1)
    k_re, k_im = couple_grid * spread[:64], couple_grid * spread[64:]
    left = jnp.concatenate(
        [jnp.concatenate([k_re, -k_im], 1), jnp.concatenate([k_im, k_re], 1)], 0
    )
    left_high, left_low = halves(left)
    wrapped = dot(jnp.concatenate([left_high, left_low], 0), resonances[:1024])
    wrapped = (wrapped[:128] + wrapped[128:]) + dot(left_high, resonances[1024:])
    turned = spectrum.T
    re, im = turned[:64], turned[64:]
    gain = jnp.concatenate([third[256:384], third[384:512]], 1)
    gain_re, gain_im = gain[:64], gain[64:]
    out_re = re + (re * gain_re - im * gain_im) + wrapped[:64]
    out_im = im + (re * gain_im + im * gain_re) + wrapped[64:]
    both = jnp.concatenate(
        [jnp.concatenate([out_re, -out_im], 1), jnp.concatenate([out_im, out_re], 1)], 0
    )
    high, low = halves(both)
    mixed = dot(jnp.concatenate([high, low], 0), back[:512])
    mixed = (mixed[:128] + mixed[128:]) + dot(high, back[512:1024])
    re, im = mixed[:64], mixed[64:]
    tc, ts = twist[:64], twist[64:]
    re, im = re * tc - im * ts, im * tc + re * ts
    mixed = jnp.concatenate(
        [re[:, :128], im[:, :128], re[:, 128:], im[:, 128:]], 0
    ) * (1.0 / NT)
    return table_times(back[1024:], mixed)


def lane_roll(value, shift):
    return pltpu.roll(value, shift, 1)


def shape(*dims, dtype=F32):
    return jax.ShapeDtypeStruct(dims, dtype)


VMEM_SPEC = pl.BlockSpec(memory_space=pltpu.VMEM)
HBM_SPEC = pl.BlockSpec(memory_space=pltpu.HBM)


def call(kernel, out_shape, in_specs, out_specs, scratch, *operands, flops):
    moved = sum(x.size * x.dtype.itemsize for x in operands)
    return pl.pallas_call(
        kernel,
        out_shape=out_shape,
        in_specs=in_specs,
        out_specs=out_specs,
        scratch_shapes=scratch,
        compiler_params=pltpu.CompilerParams(vmem_limit_bytes=40 * 1024 * 1024),
        cost_estimate=pl.CostEstimate(flops=flops, bytes_accessed=moved, transcendentals=0),
    )(*operands)


def fetches(sources, targets, sems):
    copies = [
        pltpu.make_async_copy(source, target, sems.at[k])
        for k, (source, target) in enumerate(zip(sources, targets))
    ]
    for copy in copies:
        copy.start()
    return copies


def halves_of_tiles(upper, lower):
    low = iota((8, 128), 0) < 4
    return (
        jnp.where(low, upper, pltpu.roll(lower, 4, 0)),
        jnp.where(low, pltpu.roll(upper, 4, 0), lower),
    )


def cut_kernel(field, out, buffer, sems):
    copies = [
        pltpu.make_async_copy(field.at[c], buffer.at[c], sems.at[c]) for c in range(2)
    ]
    for copy in copies:
        copy.start()
    for c in range(2):
        copies[c].wait()
        for row in range(8):
            tile = buffer[c, 8 * row : 8 * row + 8, :]
            first, second = halves_of_tiles(tile[:, :128], tile[:, 128:])
            out[32 * row + 8 * c : 32 * row + 8 * c + 8, :] = first
            out[32 * row + 16 + 8 * c : 32 * row + 24 + 8 * c, :] = second


def join_kernel(rows, field, buffer, sems):
    copies = []
    for c in range(2):
        for row in range(8):
            first = rows[32 * row + 8 * c : 32 * row + 8 * c + 8, :]
            second = rows[32 * row + 16 + 8 * c : 32 * row + 24 + 8 * c, :]
            upper, lower = halves_of_tiles(first, second)
            buffer[c, 8 * row : 8 * row + 8, :128] = upper
            buffer[c, 8 * row : 8 * row + 8, 128:] = lower
        copies.append(pltpu.make_async_copy(buffer.at[c], field.at[c], sems.at[c]))
        copies[-1].start()
    for copy in copies:
        copy.wait()


PREPARED = (
    shape(2048, 256, dtype=BF16), shape(520, 128), shape(2064, 128), shape(512, 256, dtype=BF16),
    shape(576, 128),
)


def prepare_kernel(*refs):
    inputs, outs = refs[:9], refs[9:14]
    local, made, in_sems, out_sems = refs[14:23], refs[23:28], refs[28], refs[29]
    copies = fetches(inputs, local, in_sems)
    for copy in copies:
        copy.wait()
    decay, detune, group, occupation, spectral, lateral, shift, twiddle_a, twiddle_b = local
    quad = lax.axis_index("tm")
    here = lax.axis_index("lat") * 16 + quad
    values = prepare(
        decay[...], detune[...], group[...], occupation[...], spectral[...], lateral[...],
        shift[...], twiddle_a, twiddle_b, here, quad,
    )
    for ref, value in zip(made, values):
        ref[...] = value
    for copy in fetches(made, outs, out_sems):
        copy.wait()


class Late:
    def __init__(self, copy, ref):
        self.copy, self.ref = copy, ref

    def __getitem__(self, index):
        if self.copy is not None:
            self.copy.wait()
            self.copy = None
        return self.ref[index]


def rows_kernel(field, first, resonances, wide, small, twist, out, *scratch):
    local, sems = scratch[:5], scratch[5]
    sources = (small, twist, wide, first, resonances)
    copies = fetches(sources, local, sems)
    small, twist, wide, first, resonances = (Late(*pair) for pair in zip(copies, local))
    spectrum, *rest = to_rows(field[...], first, resonances, wide, small, twist, lane_roll)
    out[pl.ds(0, 256, stride=4), :] = spectrum
    for k, row in enumerate(rest):
        out[pl.ds(k + 1, 256, stride=4), :] = jnp.broadcast_to(row, (256, 128))


def columns_kernel(message, wide, second, second_tables, out):
    parts = [message[pl.ds(k, 256, stride=4), :] for k in range(4)]
    out[...] = columns_step(parts, wide[...], second, second_tables[...], lane_roll)


def blocks_kernel(spectrum, resonances, third, back, twist, shift, out):
    out[...] = to_blocks(
        spectrum[...], resonances[...], third[...], back[...], twist[...], shift[...], lane_roll
    )


def buffers(operands):
    return [pltpu.VMEM(x.shape, x.dtype) for x in operands]


def on_device(
    light_field, lateral_phase, spectral_phase, occupation, bin_decay, bin_detune, group_bin
):
    t = {name: jnp.asarray(value) for name, value in TABLES.items()}
    sems = pltpu.SemaphoreType.DMA
    rows = call(
        cut_kernel, shape(256, 128), [HBM_SPEC], VMEM_SPEC,
        [pltpu.VMEM((2, 64, 256), F32), sems((2,))], light_field, flops=1000,
    )
    rows = lax.all_to_all(rows.reshape(16, 16, 128), "tm", 0, 0, tiled=True)
    arguments = (
        bin_decay[None, :], bin_detune[None, :], group_bin[None, :], occupation,
        spectral_phase.reshape(32, 128), lateral_phase.reshape(8, 128), t["shift"],
        t["twiddle_a"], t["twiddle_b"],
    )
    resonances, first, second, second_tables, third = call(
        prepare_kernel, PREPARED, [HBM_SPEC] * 9, (HBM_SPEC,) * 5,
        buffers(arguments) + buffers(PREPARED) + [sems((9,)), sems((5,))],
        *arguments, flops=200_000_000,
    )
    operands = (first, resonances, t["wide"], t["small"], t["twist"])
    message = call(
        rows_kernel, shape(1024, 128), [VMEM_SPEC] + [HBM_SPEC] * 5, VMEM_SPEC,
        buffers((t["small"], t["twist"], t["wide"], first, resonances)) + [sems((5,))],
        rows.reshape(256, 128), *operands, flops=500_000_000,
    )
    message = lax.all_to_all(message.reshape(256, 4, 128), BOTH, 0, 0, tiled=True)
    columns = call(
        columns_kernel, shape(256, 128), [VMEM_SPEC] * 4, VMEM_SPEC, [],
        message.reshape(1024, 128), t["wide"], second, second_tables, flops=1_000_000_000,
    )
    spectrum = lax.all_to_all(columns, BOTH, 0, 0, tiled=True)
    finished = call(
        blocks_kernel, shape(256, 128), [VMEM_SPEC] * 6, VMEM_SPEC, [],
        spectrum, resonances, third, t["back"], t["twist"], t["shift"], flops=800_000_000,
    )
    turned = lax.all_to_all(finished.reshape(16, 16, 128), "tm", 0, 0, tiled=True)
    return call(
        join_kernel, shape(2, 64, 256), [VMEM_SPEC], HBM_SPEC,
        [pltpu.VMEM((2, 64, 256), F32), sems((2,))], turned.reshape(256, 128), flops=1000,
    )


def solution(mesh):
    return jax.shard_map(
        on_device,
        mesh=mesh,
        in_specs=(P(None, "lat", "tm"), P(), P(), P(None, "lat"), P(), P(), P()),
        out_specs=P(None, "lat", "tm"),
        check_vma=False,
    )
```

time: 108 us -> 96.9 us (0.90)
  local copies, waits for them, and re-layouts: 23 us -> 9.94 us
  Pallas kernels: 8.71 us -> 11.6 us
    unnamed x72 -> x37, local copies, waits for them, and re-layouts: 17.3 us -> 9.94 us
    reshape x7 -> x0, local copies, waits for them, and re-layouts: 3.37 us -> none  [the longest x2 1.79 us: on_device(): light_field.reshape(2, 16, 4, 256).transpose(1, 0, 2, 3).reshape(16, 8, 256)]
    pallas_call x4 -> x6, Pallas kernels: 8.71 us -> 11.6 us  [call(): pl.pallas_call(kernel, out_shape=out_shape, in_specs=in_specs, out_specs=...]
    another operation x6 -> x0, local copies, waits for them, and re-layouts: 1.74 us -> none  [the longest x4 0.98 us: parameter_forms(): jnp.tile(spectral_phase.reshape(256, 16), (1, 8))]
  transfers between devices with their start and end apart: 1 -> 1, of which waited for: 0 -> 0; matrix products, arithmetic and copies ran while one was open for 4% -> 1% of each run, Pallas kernels for 2% -> 3%
where the time goes in v2:
time: 96.9 us; the launch traced here: 96.4 us
  blocking collectives  64.8 us (67%)
  Pallas kernels  11.6 us (12%)
  starting transfers between devices  9.99 us (10%)
  local copies, waits for them, and re-layouts  9.94 us (10%)
    all_to_all x1, blocking collectives, on_device(): lax.all_to_all(message.reshape(256, 4, 128), BOTH, 0, 0, tiled=True)  34.1 us
    all_to_all x1, blocking collectives, on_device(): spectrum = lax.all_to_all(columns, BOTH, 0, 0, tiled=True)  18.1 us
    all_to_all x1, blocking collectives, on_device(): lax.all_to_all(finished.reshape(16, 16, 128), 'tm', 0, 0, tiled=True)  12.5 us
    pallas_call x6, Pallas kernels, call(): pl.pallas_call(kernel, out_shape=out_shape, in_specs=in_specs, out_specs=...  11.6 us
    all_to_all x1, starting transfers between devices, on_device(): rows = lax.all_to_all(rows.reshape(16, 16, 128), 'tm', 0, 0, tiled=True)  9.99 us
    unnamed x37, local copies, waits for them, and re-layouts  9.94 us
  transfers between devices with their start and end apart: 1, of which 0 were waited for; matrix products, arithmetic and copies ran while one was open for 1% of the time, Pallas kernels for 3%

profile of v2, /device:TPU:1, one launch (start us, length us, event | category | flops | bytes accessed | tf_op | source)
XLA Modules:
  0.0 96.4 jit_solution(17692259939188168591)
XLA Ops:
  0.0 0.0 copy-start.7
  0.0 0.9 copy-done.7
  0.9 0.8 shard_map.136
  1.7 10.0 %all-to-all-start = ((f32[16,16,128]{2,1,0:T(8,128)}), f32[16,16,128]{2,1,0:T(8,128)S(1)}, u32[]{:S(2)}, u32[]{:S(2)}) async-start(f32[16,16,128]{2,1,0:T(8,128)} %bitcast), calls=%async_computation | async-start | bytes 262144 | tf_op jit(solution)/shard_map/all_to_all | solution.py:539
  11.7 0.8 copy.16.refs_3_
  12.6 0.0 copy-start
  12.6 1.2 %copy-done = f32[8,256,128]{2,1,0:T(8,128)S(1)} copy-done((f32[8,256,128]{2,1,0:T(8,128)S(1)}, f32[8,256,128]{2,1,0:T(8,128)}, u32[]{:S(2)}) %copy-start) | copy-done | bytes 1048600
  13.8 0.0 copy-start.1
  13.8 1.2 %copy-done.1 = f32[8,256,128]{2,1,0:T(8,128)S(1)} copy-done((f32[8,256,128]{2,1,0:T(8,128)S(1)}, f32[8,256,128]{2,1,0:T(8,128)}, u32[]{:S(2)}) %copy-start.1) | copy-done | bytes 1048600
  15.0 0.0 copy-start.3
  15.0 0.9 copy-done.3
  16.0 0.0 copy-start.8
  16.0 0.7 copy-done.8
  16.7 0.0 copy-start.9
  16.7 0.7 copy-done.9
  17.4 0.0 copy-start.10
  17.4 0.7 copy-done.10
  18.1 0.0 copy-start.11
  18.1 0.7 copy-done.11
  18.7 0.0 copy-start.12
  18.7 0.7 copy-done.12
  19.4 0.0 copy-start.2
  19.4 0.0 copy-start.5
  19.4 0.0 copy-start.6
  19.4 3.0 %shard_map.137 = (bf16[2048,256]{1,0:T(8,128)(2,1)S(1)}, f32[520,128]{1,0:T(8,128)S(1)}, f32[2064,128]{1,0:T(8,128)S(1)}, bf16[512,256]{1,0:T(8,128)(2,1)S(1)}, f32[576,128]{1,0:T(8,128)S(1)}) custom-call(f32[1,32]{1,0:T(1,128)S(1)} %bitcast.24, f32[1,32]{1,0:T(1,128)S(1)} %bitcast.25, s32[1,128]{1,0:T(1,128)S(1)} %bitcast.26, f32[128,64]{1,0:T(8,128)S(1)} %copy.16.refs_3_, ...), custom_call_target="tpu_custom_call" | custom-call | flops 200000000 | bytes 2413312 | tf_op jit(solution)/shard_map/pallas_call | solution.py:409
  22.4 0.0 copy-start.13
  22.4 0.7 copy-done.13
  23.1 0.0 copy-start.15
  23.1 0.7 copy-done.15
  23.8 0.0 all-to-all-done
  23.8 0.0 copy-done.2
  23.8 0.0 copy-done.5
  23.8 0.0 copy-done.6
  23.8 0.0 copy-start.16
  23.9 2.0 %shard_map.138 = f32[1024,128]{1,0:T(8,128)S(1)} custom-call(f32[256,128]{1,0:T(8,128)S(1)} %bitcast.16, f32[520,128]{1,0:T(8,128)S(1)} %get-tuple-element.10.first, bf16[2048,256]{1,0:T(8,128)(2,1)S(1)} %get-tuple-element.11.resonances, bf16[512,512]{1,0:T(8,128)(2,1)S(1)} %copy-done.2, bf16[512,256]{1,0:T(8,128)(2,1)S(1)} %copy-done.5, ...), custom_call_target="tpu_custom_call" | custom-call | flops 500000000 | bytes 2363392 | tf_op jit(solution)/shard_map/pallas_call | solution.py:409
  25.8 34.1 %all_to_all.26 = f32[256,4,128]{2,1,0:T(4,128)S(1)} all-to-all(f32[256,4,128]{2,1,0:T(4,128)S(1)} %bitcast.15), channel_id=1, replica_groups=mesh['lat'=16,'tm'=16] {'lat','tm'}, dimensions={0} | all-to-all | bytes 1048576 | tf_op jit(solution)/shard_map/all_to_all | solution.py:556
  60.0 0.0 copy-done.16
  60.0 0.0 copy-start.4
  60.0 0.0 copy-start.14
  60.0 0.0 copy-start.17
  60.0 2.8 %shard_map.139 = f32[256,128]{1,0:T(8,128)S(1)} custom-call(f32[1024,128]{1,0:T(8,128)S(1)} %bitcast.17, bf16[512,512]{1,0:T(8,128)(2,1)S(1)} %copy-done.2, f32[2064,128]{1,0:T(8,128)S(1)} %get-tuple-element.12.second, bf16[512,256]{1,0:T(8,128)(2,1)S(1)} %copy-done.16), custom_call_target="tpu_custom_call" | custom-call | flops 1000000000 | bytes 2367488 | tf_op jit(solution)/shard_map/pallas_call | solution.py:409
  62.8 18.1 %all_to_all.27 = f32[256,1,128]{2,1,0:T(1,128)S(1)} all-to-all(f32[256,1,128]{2,1,0:T(1,128)S(1)} %bitcast.21), channel_id=1, replica_groups=mesh['lat'=16,'tm'=16] {'lat','tm'}, dimensions={0} | all-to-all | bytes 262144 | tf_op jit(solution)/shard_map/all_to_all | solution.py:561
  81.0 0.0 copy-done.4
  81.0 0.0 copy-done.14
  81.0 0.0 copy-done.17
  81.0 2.2 %shard_map.140 = f32[256,128]{1,0:T(8,128)S(1)} custom-call(f32[256,128]{1,0:T(8,128)S(1)} %bitcast.19, bf16[2048,256]{1,0:T(8,128)(2,1)S(1)} %get-tuple-element.11.resonances, f32[576,128]{1,0:T(8,128)S(1)} %copy-done.14, bf16[1536,256]{1,0:T(8,128)(2,1)S(1)} %copy-done.17, f32[128,256]{1,0:T(8,128)S(1)} %copy-done.6, f32[512,128]{1,0:T(8,128)S(1)} %copy-done.4), custom_call_target="tpu_custom_call" | custom-call | flops 800000000 | bytes 2654208 | tf_op jit(solution)/shard_map/pallas_call | solution.py:409
  83.2 12.5 %all_to_all.28 = f32[16,16,128]{2,1,0:T(8,128)S(1)} all-to-all(f32[16,16,128]{2,1,0:T(8,128)S(1)} %bitcast.20), channel_id=1, replica_groups=mesh['lat'=16,'tm'=16] {'tm'}, dimensions={0} | all-to-all | bytes 262144 | tf_op jit(solution)/shard_map/all_to_all | solution.py:566
  95.7 0.7 shard_map.141
Async XLA Ops:
  0.0 0.9 copy-start.7
  1.7 22.1 %all-to-all-start = ((f32[16,16,128]{2,1,0:T(8,128)}), f32[16,16,128]{2,1,0:T(8,128)S(1)}, u32[]{:S(2)}, u32[]{:S(2)}) async-start(f32[16,16,128]{2,1,0:T(8,128)} %bitcast), calls=%async_computation | async-start | bytes 262144 | tf_op jit(solution)/shard_map/all_to_all | solution.py:539
  12.6 1.2 %copy-start = (f32[8,256,128]{2,1,0:T(8,128)S(1)}, f32[8,256,128]{2,1,0:T(8,128)}, u32[]{:S(2)}) copy-start(f32[8,256,128]{2,1,0:T(8,128)} %constant.20.clone.refs_8_) | copy-start | bytes 3145732
  13.8 1.2 %copy-start.1 = (f32[8,256,128]{2,1,0:T(8,128)S(1)}, f32[8,256,128]{2,1,0:T(8,128)}, u32[]{:S(2)}) copy-start(f32[8,256,128]{2,1,0:T(8,128)} %constant.19.clone.refs_7_) | copy-start | bytes 3145732
  15.0 0.9 copy-start.3
  16.0 0.7 copy-start.8
  16.7 0.7 copy-start.9
  17.4 0.7 copy-start.10
  18.1 0.7 copy-start.11
  18.7 0.7 copy-start.12
  19.4 4.5 %copy-start.2 = (bf16[512,512]{1,0:T(8,128)(2,1)S(1)}, bf16[512,512]{1,0:T(8,128)(2,1)}, u32[]{:S(2)}) copy-start(bf16[512,512]{1,0:T(8,128)(2,1)} %constant.14.clone.wide) | copy-start | bytes 1572868
  19.4 4.5 %copy-start.5 = (bf16[512,256]{1,0:T(8,128)(2,1)S(1)}, bf16[512,256]{1,0:T(8,128)(2,1)}, u32[]{:S(2)}) copy-start(bf16[512,256]{1,0:T(8,128)(2,1)} %constant.15.clone.small) | copy-start | bytes 786436
  19.4 4.5 %copy-start.6 = (f32[128,256]{1,0:T(8,128)S(1)}, f32[128,256]{1,0:T(8,128)}, u32[]{:S(2)}) copy-start(f32[128,256]{1,0:T(8,128)} %constant.17.clone.twist) | copy-start | bytes 393220
  22.4 0.7 copy-start.13
  23.1 0.7 copy-start.15
  23.8 36.1 %copy-start.16 = (bf16[512,256]{1,0:T(8,128)(2,1)S(1)}, bf16[512,256]{1,0:T(8,128)(2,1)}, u32[]{:S(2)}) copy-start(bf16[512,256]{1,0:T(8,128)(2,1)} %copy-done.15) | copy-start | bytes 786436
  60.0 21.0 %copy-start.4 = (f32[512,128]{1,0:T(8,128)S(1)}, f32[512,128]{1,0:T(8,128)}, u32[]{:S(2)}) copy-start(f32[512,128]{1,0:T(8,128)} %constant.18.clone.refs_6_.shift) | copy-start | bytes 786436
  60.0 21.0 %copy-start.14 = (f32[576,128]{1,0:T(8,128)S(1)}, f32[576,128]{1,0:T(8,128)}, u32[]{:S(2)}) copy-start(f32[576,128]{1,0:T(8,128)} %copy-done.13) | copy-start | bytes 884740
  60.0 21.0 %copy-start.17 = (bf16[1536,256]{1,0:T(8,128)(2,1)S(1)}, bf16[1536,256]{1,0:T(8,128)(2,1)}, u32[]{:S(2)}) copy-start(bf16[1536,256]{1,0:T(8,128)(2,1)} %constant.16.clone.back) | copy-start | bytes 2359300

commit v3 on v2

--- a/solution.py
+++ b/solution.py
@@ -36,27 +36,20 @@
     small = small * (tq[:, None] == rq[None, :]) * (th[:, None] == rh[None, :])
     short = 2 * np.pi * (col[:64, None] * grid(256)[None, :]) / NT
     omega_lanes = np.tile(2 * np.pi * (16 * grid(256)[:, None] + grid(16)[None, :]) / NT, (1, 8))
-    eight = lane // 16
-    twiddle_a = np.zeros((8, 256, 128))
-    twiddle_b = np.zeros((8, 256, 128))
-    for r in range(8):
-        source = (eight + r) % 8
-        sc, sq = source // 4, source % 4
-        theta = -2 * np.pi * ((sq - q)[None, :] * grid(256)[:, None]) / NX
-        re, im = np.cos(theta), np.sin(theta)
-        same_part = (sc == c)[None, :]
-        flip = np.where(c == 0, -1.0, 1.0)[None, :]
-        twiddle_a[r] = np.where(same_part, re, flip * im) / NX
-        twiddle_b[r] = np.where(same_part, -im, flip * re) / NX
+    twiddle = []
+    for k in range(1, 4):
+        theta = -2 * np.pi * (((q + k) % 4 - q)[None, :] * grid(256)[:, None]) / NX
+        twiddle += [np.cos(theta), np.sin(theta)]
     t = {}
-    t["wide"] = np.concatenate(split_table(wide), 0)
-    t["small"] = np.concatenate(split_table(small), 0)
+    t["ahead"] = np.concatenate(
+        [np.concatenate(split_table(x), 0) for x in (wide, small)], 1
+    )
     t["back"] = np.concatenate(split_table(tall) + split_table(small.T), 0)
-    t["twist"] = np.concatenate([np.cos(short), np.sin(short)], 0).astype(np.float32)
+    twist = np.concatenate([np.cos(short), np.sin(short)], 0)
     omega_part = np.concatenate([np.cos(omega_lanes), -np.sin(omega_lanes)], 0)
-    t["shift"] = (omega_part / NT).astype(np.float32)
-    t["twiddle_a"] = twiddle_a.astype(np.float32)
-    t["twiddle_b"] = twiddle_b.astype(np.float32)
+    twist = [twist[:, :128], twist[:, 128:]]
+    t["shift"] = np.concatenate([omega_part / NT] + twist, 0).astype(np.float32)
+    t["twiddle"] = np.concatenate(twiddle + twist, 0).astype(np.float32)
     return t
 
 
@@ -172,8 +165,23 @@
     return pick_dot_nt(eye, rows)
 
 
-def prepare(decay, detune_row, group_bin, occupation, spectral, lateral, shift, twiddle_a,
-            twiddle_b, here, quad):
+def pack(decay, detune, group_bin, spectral, lateral):
+    row = [decay, detune, jnp.zeros((128 - 2 * BINS,), F32), group_bin.astype(F32)]
+    return jnp.concatenate(row + [spectral, lateral]).reshape(42, 128)
+
+
+def unpack(packed):
+    return (packed[0:1, :BINS], packed[0:1, BINS : 2 * BINS], packed[1:2], packed[2:34],
+            packed[34:42])
+
+
+def couplings(drive, group_bin, occupation):
+    member = (iota((BINS, GROUPS), 0).astype(F32) == group_bin).astype(BF16)
+    return pick_dot_nt(member, occupation) * drive
+
+
+def prepare_first(packed, occupation, quad):
+    decay, detune_row, group_bin, spectral, _ = unpack(packed)
     params = bin_columns(decay, detune_row)
     detune, keep, lost, drive = (params[:, k : k + 1] for k in range(4))
     real, imag = [], []
@@ -182,9 +190,8 @@
         real.append(g_re)
         imag.append(g_im)
     resonances = jnp.concatenate(halves(jnp.concatenate(real + imag, 0)), 0)
-    member = (iota((BINS, GROUPS), 0) == group_bin).astype(BF16)
-    per_bin = pick_dot(member, occupation) * drive
-    points = occupation.shape[1]
+    per_bin = couplings(drive, group_bin, occupation)
+    points = occupation.shape[0]
     pick = iota((points, 128), 0) == 4 * quad + iota((points, 128), 1) // 16 % 4
     chosen = exact_dot(per_bin, pick.astype(BF16))
     lane = iota((BINS, 128), 1)
@@ -192,6 +199,26 @@
         jnp.where(iota((BINS, 128), 0) == lane // 64 * 16 + lane % 16, chosen, 0.0),
         axis=0, keepdims=True,
     )
+    cos, sin = cosine_sine(spectral)
+    spectral_parts = cos, sin
+    row_of = (iota((256, 32), 0) // 8 == iota((256, 32), 1)).astype(BF16)
+    mine = iota((256, 128), 1) // 16 == iota((256, 128), 0) % 8
+    lane_of = (iota((128, 128), 0) % 16 == iota((128, 128), 1) % 16).astype(BF16)
+    cos = exact_dot(jnp.where(mine, pick_dot(row_of, cos), 0.0), lane_of)
+    sin = exact_dot(jnp.where(mine, pick_dot(row_of, sin), 0.0), lane_of)
+    side = jnp.where(iota((256, 128), 1) < 64, -1.0, 1.0)
+    index = 16 * iota((256, 128), 0) + iota((256, 128), 1) % 16
+    back_re, back_im = cosine_sine(jnp.where(index > NT // 2, NT - index, -index) * STEP)
+    wrap_a = (cos * back_re - sin * back_im) * (1.0 / NT)
+    wrap_b = (cos * back_im + sin * back_re) * (side * (1.0 / NT))
+    first = jnp.concatenate([wrap_a, wrap_b, jnp.broadcast_to(couple_row, (8, 128))], 0)
+    return resonances, first, params, per_bin, spectral_parts
+
+
+def prepare_rest(packed, twiddle, made, here, quad):
+    lateral = unpack(packed)[4]
+    resonances, _, params, per_bin, (cos, sin) = made
+    points = per_bin.shape[1]
     pick_rows = iota((64, points), 1) == 4 * quad + iota((64, points), 0) // 16
     spread = pick_dot_nt(pick_rows.astype(BF16), jnp.concatenate([per_bin] * 16, 0))
     couple_grid = jnp.where(
@@ -203,18 +230,11 @@
     gain_rest = dot(gain_high, jnp.concatenate([resonances[1024:1536], resonances[1536:]], 1))
     gain = (gain[:64] + gain[64:]) + gain_rest
     gain = jnp.concatenate([-gain[:, 256:], gain[:, :256]], 0)
-    cos, sin = cosine_sine(spectral)
-    row_of = (iota((256, 32), 0) // 8 == iota((256, 32), 1)).astype(BF16)
-    mine = iota((256, 128), 1) // 16 == iota((256, 128), 0) % 8
+    own = (iota((32, 128), 0) == here // 8) & (iota((32, 128), 1) // 16 == here % 8)
     lane_of = (iota((128, 128), 0) % 16 == iota((128, 128), 1) % 16).astype(BF16)
-    cos = exact_dot(jnp.where(mine, pick_dot(row_of, cos), 0.0), lane_of)
-    sin = exact_dot(jnp.where(mine, pick_dot(row_of, sin), 0.0), lane_of)
-    side = jnp.where(iota((256, 128), 1) < 64, -1.0, 1.0)
-    wrap_a = cos * shift[:256] - sin * shift[256:]
-    wrap_b = (cos * shift[256:] + sin * shift[:256]) * side
-    own = iota((256, 128), 0) == here
-    once_re = jnp.sum(jnp.where(own, cos, 0.0), axis=0, keepdims=True)
-    once_im = jnp.sum(jnp.where(own, sin, 0.0), axis=0, keepdims=True)
+    own_rows = [jnp.sum(jnp.where(own, x, 0.0), axis=0, keepdims=True) for x in (cos, sin)]
+    own_rows = exact_dot(jnp.concatenate(own_rows * 4, 0), lane_of)
+    once_re, once_im = own_rows[0:1], own_rows[1:2]
     eye = (iota((128, 128), 0) == iota((128, 128), 1)).astype(BF16)
     cos, sin = cosine_sine(lateral)
     cos, sin = pick_dot_nt(eye, cos), pick_dot_nt(eye, sin)
@@ -237,9 +257,19 @@
         (i[0] + i[2]) - (i[1] + i[3]),
         (i[0] - i[2]) + (r[1] - r[3]),
     ]
-    mixing = jnp.concatenate(
-        [twiddle_a[k] * blocks_re[k % 4] + twiddle_b[k] * blocks_im[k % 4] for k in range(8)], 0
-    )
+    eight = iota((256, 128), 1) // 16
+    flip = jnp.where(eight < 4, -1.0, 1.0)
+    mixing = [None] * 8
+    for k in range(4):
+        re, im = blocks_re[k] * (1.0 / NX), blocks_im[k] * (1.0 / NX)
+        if k == 0:
+            real, imag = re + jnp.zeros((256, 128), F32), im * flip
+        else:
+            cos, sin = twiddle[512 * k - 512 : 512 * k - 256], twiddle[512 * k - 256 : 512 * k]
+            real, imag = cos * re - sin * im, (cos * im + sin * re) * flip
+        for r in (k, k + 4):
+            mixing[r] = jnp.where((eight + r) % 8 // 4 == eight // 4, real, imag)
+    mixing = jnp.concatenate(mixing, 0)
     rows = jnp.concatenate([params[:16]] * 4 + [params[16:]] * 4, 0)
     g_re, g_im = resonance(
         rows[:, 0:1], rows[:, 1:2], rows[:, 2:3], 16 * here + iota((128, 128), 1) % 16
@@ -253,7 +283,7 @@
     b_im = jnp.where(inside, g_re * f_im + g_im * f_re, 0.0)
     gain_here = jnp.concatenate([b_re, jnp.where(left, -b_im, b_im)], 1)
     gain_here = jnp.concatenate(halves(gain_here), 0)
-    side_row = side[0:1]
+    side_row = jnp.where(iota((1, 128), 1) < 64, -1.0, 1.0)
     twice = jnp.concatenate([twice_re] * 8 + [twice_im * side_row] * 8, 0)
     k_re, k_im = rows[:, 4:5], rows[:, 5:6]
     f_re = once_re * k_re - once_im * k_im
@@ -263,7 +293,6 @@
     top, bottom = jnp.where(left, h_re, h_im), jnp.where(left, -h_im, h_re)
     wrap_here = jnp.concatenate([top[:64], bottom[:64], top[64:], bottom[64:]], 0)
     wrap_here = jnp.concatenate(halves(wrap_here), 1)
-    first = jnp.concatenate([wrap_a, wrap_b, jnp.broadcast_to(couple_row, (8, 128))], 0)
     second = jnp.concatenate([twice, mixing], 0)
     second_tables = jnp.concatenate([gain_here, wrap_here], 0)
     turned = [jnp.broadcast_to(params[:, k : k + 1], (BINS, 128)) for k in (4, 5)]
@@ -271,7 +300,7 @@
         [couple_grid[:, 128 * k : 128 * k + 128] for k in range(4)]
         + [gain[:, :128], gain[:, 128:]] + turned, 0,
     )
-    return resonances, first, second, second_tables, third
+    return second, second_tables, third
 
 
 def half_sign(shape):
@@ -292,25 +321,29 @@
     return sums[0] + half_sign((BINS, 128)) * roll(sums[1], 64)
 
 
-def to_rows(field, first, resonances, wide, small, twist, roll):
-    mixed = table_times(small[...], field)
+def untwist(pair):
+    return (jnp.concatenate([pair[k : k + 64], pair[128 + k : 192 + k]], 1) for k in (0, 64))
+
+
+def to_rows(field, first, resonances, ahead, roll):
+    mixed = table_times(ahead[:, 512:], field)
     mixed = jnp.concatenate([mixed[:128], mixed[128:]], 1)
     re, im = mixed[:64], mixed[64:]
-    tc, ts = twist[:64], twist[64:]
+    tc, ts = untwist(first)
     re, im = re * tc + im * ts, im * tc - re * ts
     both = jnp.concatenate(
         [jnp.concatenate([re, im], 1), jnp.concatenate([im, -re], 1)], 0
     )
-    product = dot_nt(wide[...], jnp.concatenate(halves(both), 0))
+    product = dot_nt(ahead[:, :512], jnp.concatenate(halves(both), 0))
     spectrum = quadrants(product, 256, 128)
-    weighted = first[:256] * spectrum + first[256:512] * roll(spectrum, 64)
+    weighted = first[256:512] * spectrum + first[512:768] * roll(spectrum, 64)
     state = wrap_state(resonances[...], weighted, roll)
     place = (iota((128, 256), 0) // 16 == iota((128, 256), 1) % 128 // 16).astype(BF16)
     parts = exact_dot(state, place)
     lane = iota((BINS, 256), 1)
     chosen = iota((BINS, 256), 0) == lane // 128 * 16 + lane % 16
     state_row = jnp.sum(jnp.where(chosen, parts, 0.0), axis=0, keepdims=True)
-    return spectrum, state_row[:, :128], state_row[:, 128:], first[512:513]
+    return spectrum, state_row[:, :128], state_row[:, 128:], first[768:769]
 
 
 def diffract(blocks, wide, mixing, roll):
@@ -354,9 +387,9 @@
     return diffract([field], wide, mixing, roll)[0]
 
 
-def to_blocks(spectrum, resonances, third, back, twist, shift, roll):
+def to_blocks(spectrum, resonances, third, back, shift, roll):
     sign = half_sign((256, 128))
-    weighted = shift[:256] * spectrum + (shift[256:] * sign) * roll(spectrum, 64)
+    weighted = shift[:256] * spectrum + (shift[256:512] * sign) * roll(spectrum, 64)
     state = wrap_state(resonances[...], weighted, roll)
     state = third[512:544] * state + third[544:576] * (
         half_sign((BINS, 128)) * roll(state, 64)
@@ -384,7 +417,7 @@
     mixed = dot(jnp.concatenate([high, low], 0), back[:512])
     mixed = (mixed[:128] + mixed[128:]) + dot(high, back[512:1024])
     re, im = mixed[:64], mixed[64:]
-    tc, ts = twist[:64], twist[64:]
+    tc, ts = untwist(shift[512:])
     re, im = re * tc - im * ts, im * tc + re * ts
     mixed = jnp.concatenate(
         [re[:, :128], im[:, :128], re[:, 128:], im[:, 128:]], 0
@@ -404,7 +437,7 @@
 HBM_SPEC = pl.BlockSpec(memory_space=pltpu.HBM)
 
 
-def call(kernel, out_shape, in_specs, out_specs, scratch, *operands, flops):
+def call(kernel, out_shape, in_specs, out_specs, scratch, *operands, flops, limit=40):
     moved = sum(x.size * x.dtype.itemsize for x in operands)
     return pl.pallas_call(
         kernel,
@@ -412,19 +445,9 @@
         in_specs=in_specs,
         out_specs=out_specs,
         scratch_shapes=scratch,
-        compiler_params=pltpu.CompilerParams(vmem_limit_bytes=40 * 1024 * 1024),
+        compiler_params=pltpu.CompilerParams(vmem_limit_bytes=limit * 1024 * 1024),
         cost_estimate=pl.CostEstimate(flops=flops, bytes_accessed=moved, transcendentals=0),
     )(*operands)
-
-
-def fetches(sources, targets, sems):
-    copies = [
-        pltpu.make_async_copy(source, target, sems.at[k])
-        for k, (source, target) in enumerate(zip(sources, targets))
-    ]
-    for copy in copies:
-        copy.start()
-    return copies
 
 
 def halves_of_tiles(upper, lower):
@@ -435,16 +458,10 @@
     )
 
 
-def cut_kernel(field, out, buffer, sems):
-    copies = [
-        pltpu.make_async_copy(field.at[c], buffer.at[c], sems.at[c]) for c in range(2)
-    ]
-    for copy in copies:
-        copy.start()
+def cut_kernel(field, out):
     for c in range(2):
-        copies[c].wait()
         for row in range(8):
-            tile = buffer[c, 8 * row : 8 * row + 8, :]
+            tile = field[c, 8 * row : 8 * row + 8, :]
             first, second = halves_of_tiles(tile[:, :128], tile[:, 128:])
             out[32 * row + 8 * c : 32 * row + 8 * c + 8, :] = first
             out[32 * row + 16 + 8 * c : 32 * row + 24 + 8 * c, :] = second
@@ -466,65 +483,38 @@
 
 
 PREPARED = (
-    shape(2048, 256, dtype=BF16), shape(520, 128), shape(2064, 128), shape(512, 256, dtype=BF16),
+    shape(2048, 256, dtype=BF16), shape(776, 128), shape(2064, 128), shape(512, 256, dtype=BF16),
     shape(576, 128),
 )
 
 
-def prepare_kernel(*refs):
-    inputs, outs = refs[:9], refs[9:14]
-    local, made, in_sems, out_sems = refs[14:23], refs[23:28], refs[28], refs[29]
-    copies = fetches(inputs, local, in_sems)
-    for copy in copies:
-        copy.wait()
-    decay, detune, group, occupation, spectral, lateral, shift, twiddle_a, twiddle_b = local
+def prepare_kernel(packed, occupation, twiddle, *outs):
     quad = lax.axis_index("tm")
     here = lax.axis_index("lat") * 16 + quad
-    values = prepare(
-        decay[...], detune[...], group[...], occupation[...], spectral[...], lateral[...],
-        shift[...], twiddle_a, twiddle_b, here, quad,
-    )
-    for ref, value in zip(made, values):
+    packed = packed[...]
+    made = prepare_first(packed, occupation[...], quad)
+    first = jnp.concatenate([twiddle[1536:], made[1]], 0)
+    values = (made[0], first, *prepare_rest(packed, twiddle, made, here, quad))
+    for ref, value in zip(outs, values):
         ref[...] = value
-    for copy in fetches(made, outs, out_sems):
-        copy.wait()
-
-
-class Late:
-    def __init__(self, copy, ref):
-        self.copy, self.ref = copy, ref
-
-    def __getitem__(self, index):
-        if self.copy is not None:
-            self.copy.wait()
-            self.copy = None
-        return self.ref[index]
-
-
-def rows_kernel(field, first, resonances, wide, small, twist, out, *scratch):
-    local, sems = scratch[:5], scratch[5]
-    sources = (small, twist, wide, first, resonances)
-    copies = fetches(sources, local, sems)
-    small, twist, wide, first, resonances = (Late(*pair) for pair in zip(copies, local))
-    spectrum, *rest = to_rows(field[...], first, resonances, wide, small, twist, lane_roll)
+
+
+def rows_kernel(field, first, resonances, ahead, out):
+    spectrum, *rest = to_rows(field[...], first, resonances, ahead, lane_roll)
     out[pl.ds(0, 256, stride=4), :] = spectrum
     for k, row in enumerate(rest):
         out[pl.ds(k + 1, 256, stride=4), :] = jnp.broadcast_to(row, (256, 128))
 
 
-def columns_kernel(message, wide, second, second_tables, out):
+def columns_kernel(message, ahead, second, second_tables, out):
     parts = [message[pl.ds(k, 256, stride=4), :] for k in range(4)]
-    out[...] = columns_step(parts, wide[...], second, second_tables[...], lane_roll)
-
-
-def blocks_kernel(spectrum, resonances, third, back, twist, shift, out):
+    out[...] = columns_step(parts, ahead[:, :512], second, second_tables[...], lane_roll)
+
+
+def blocks_kernel(spectrum, resonances, third, back, shift, out):
     out[...] = to_blocks(
-        spectrum[...], resonances[...], third[...], back[...], twist[...], shift[...], lane_roll
-    )
-
-
-def buffers(operands):
-    return [pltpu.VMEM(x.shape, x.dtype) for x in operands]
+        spectrum[...], resonances[...], third[...], back[...], shift[...], lane_roll
+    )
 
 
 def on_device(
@@ -533,35 +523,28 @@
     t = {name: jnp.asarray(value) for name, value in TABLES.items()}
     sems = pltpu.SemaphoreType.DMA
     rows = call(
-        cut_kernel, shape(256, 128), [HBM_SPEC], VMEM_SPEC,
-        [pltpu.VMEM((2, 64, 256), F32), sems((2,))], light_field, flops=1000,
+        cut_kernel, shape(256, 128), [VMEM_SPEC], VMEM_SPEC, [], light_field, flops=1000
     )
     rows = lax.all_to_all(rows.reshape(16, 16, 128), "tm", 0, 0, tiled=True)
-    arguments = (
-        bin_decay[None, :], bin_detune[None, :], group_bin[None, :], occupation,
-        spectral_phase.reshape(32, 128), lateral_phase.reshape(8, 128), t["shift"],
-        t["twiddle_a"], t["twiddle_b"],
-    )
+    packed = pack(bin_decay, bin_detune, group_bin, spectral_phase, lateral_phase)
     resonances, first, second, second_tables, third = call(
-        prepare_kernel, PREPARED, [HBM_SPEC] * 9, (HBM_SPEC,) * 5,
-        buffers(arguments) + buffers(PREPARED) + [sems((9,)), sems((5,))],
-        *arguments, flops=200_000_000,
-    )
-    operands = (first, resonances, t["wide"], t["small"], t["twist"])
+        prepare_kernel, PREPARED, [VMEM_SPEC] * 3, (VMEM_SPEC,) * 5, [],
+        packed, occupation.T, t["twiddle"], flops=200_000_000,
+    )
     message = call(
-        rows_kernel, shape(1024, 128), [VMEM_SPEC] + [HBM_SPEC] * 5, VMEM_SPEC,
-        buffers((t["small"], t["twist"], t["wide"], first, resonances)) + [sems((5,))],
-        rows.reshape(256, 128), *operands, flops=500_000_000,
+        rows_kernel, shape(1024, 128), [VMEM_SPEC] * 4, VMEM_SPEC, [],
+        rows.reshape(256, 128), first, resonances, t["ahead"],
+        flops=500_000_000,
     )
     message = lax.all_to_all(message.reshape(256, 4, 128), BOTH, 0, 0, tiled=True)
     columns = call(
         columns_kernel, shape(256, 128), [VMEM_SPEC] * 4, VMEM_SPEC, [],
-        message.reshape(1024, 128), t["wide"], second, second_tables, flops=1_000_000_000,
+        message.reshape(1024, 128), t["ahead"], second, second_tables, flops=1_000_000_000,
     )
     spectrum = lax.all_to_all(columns, BOTH, 0, 0, tiled=True)
     finished = call(
-        blocks_kernel, shape(256, 128), [VMEM_SPEC] * 6, VMEM_SPEC, [],
-        spectrum, resonances, third, t["back"], t["twist"], t["shift"], flops=800_000_000,
+        blocks_kernel, shape(256, 128), [VMEM_SPEC] * 5, VMEM_SPEC, [],
+        spectrum, resonances, third, t["back"], t["shift"], flops=800_000_000,
     )
     turned = lax.all_to_all(finished.reshape(16, 16, 128), "tm", 0, 0, tiled=True)
     return call(

time: 96.9 us -> 91.4 us (0.943)
  local copies, waits for them, and re-layouts: 9.94 us -> 5.1 us
  blocking collectives: 64.8 us -> 62.9 us
  waiting for transfers between devices: 0.01 us -> 1.84 us
  Pallas kernels: 11.6 us -> 10.4 us
    unnamed x37 -> x20, local copies, waits for them, and re-layouts: 9.94 us -> 4.28 us
    all_to_all x1, blocking collectives: 34.1 us -> 32.3 us  [on_device(): lax.all_to_all(message.reshape(256, 4, 128), BOTH, 0, 0, tiled=True)]
    all_to_all x1, waiting for transfers between devices: 0.01 us -> 1.84 us  [on_device(): rows = lax.all_to_all(rows.reshape(16, 16, 128), 'tm', 0, 0, tiled=True)]
    pallas_call x6, Pallas kernels: 11.6 us -> 10.4 us  [call(): pl.pallas_call(kernel, out_shape=out_shape, in_specs=in_specs, out_specs=...]
  transfers between devices with their start and end apart: 1 -> 1, of which waited for: 0 -> 1; matrix products, arithmetic and copies ran while one was open for 1% -> 2% of each run, Pallas kernels for 3% -> 3%
where the time goes in v3:
time: 91.4 us; the launch traced here: 90.9 us
  blocking collectives  62.9 us (69%)
  Pallas kernels  10.4 us (11%)
  starting transfers between devices  9.98 us (11%)
  local copies, waits for them, and re-layouts  5.1 us (6%)
  waiting for transfers between devices  1.84 us (2%)
    all_to_all x1, blocking collectives, on_device(): lax.all_to_all(message.reshape(256, 4, 128), BOTH, 0, 0, tiled=True)  32.3 us
    all_to_all x1, blocking collectives, on_device(): spectrum = lax.all_to_all(columns, BOTH, 0, 0, tiled=True)  18.1 us
    all_to_all x1, blocking collectives, on_device(): lax.all_to_all(finished.reshape(16, 16, 128), 'tm', 0, 0, tiled=True)  12.5 us
    pallas_call x6, Pallas kernels, call(): pl.pallas_call(kernel, out_shape=out_shape, in_specs=in_specs, out_specs=...  10.4 us
    all_to_all x1, starting transfers between devices, on_device(): rows = lax.all_to_all(rows.reshape(16, 16, 128), 'tm', 0, 0, tiled=True)  9.98 us
    unnamed x20, local copies, waits for them, and re-layouts  4.28 us
    all_to_all x1, waiting for transfers between devices, on_device(): rows = lax.all_to_all(rows.reshape(16, 16, 128), 'tm', 0, 0, tiled=True)  1.84 us
  transfers between devices with their start and end apart: 1, of which 1 were waited for; matrix products, arithmetic and copies ran while one was open for 2% of the time, Pallas kernels for 3%

profile of v3, /device:TPU:1, one launch (start us, length us, event | category | flops | bytes accessed | tf_op | source)
XLA Modules:
  0.0 90.9 jit_solution(16072177766531597838)
XLA Ops:
  0.0 0.0 copy-start.2
  0.0 0.9 copy-done.2
  0.9 0.7 shard_map.109
  1.6 10.0 %all-to-all-start = ((f32[16,16,128]{2,1,0:T(8,128)}), f32[16,16,128]{2,1,0:T(8,128)S(1)}, u32[]{:S(2)}, u32[]{:S(2)}) async-start(f32[16,16,128]{2,1,0:T(8,128)} %bitcast), calls=%async_computation | async-start | bytes 262144 | tf_op jit(solution)/shard_map/all_to_all | solution.py:528
  11.6 0.7 convert_element_type.3
  12.2 0.8 concatenate.3
  13.0 0.0 copy-start
  13.0 1.2 %copy-done = f32[1792,128]{1,0:T(8,128)S(1)} copy-done((f32[1792,128]{1,0:T(8,128)S(1)}, f32[1792,128]{1,0:T(8,128)}, u32[]{:S(2)}) %copy-start) | copy-done | bytes 917528
  14.2 0.0 copy-start.3
  14.2 0.8 copy-done.3
  15.0 0.0 copy-start.1
  15.0 2.5 %shard_map.110 = (bf16[2048,256]{1,0:T(8,128)(2,1)S(1)}, f32[776,128]{1,0:T(8,128)S(1)}, f32[2064,128]{1,0:T(8,128)S(1)}, bf16[512,256]{1,0:T(8,128)(2,1)S(1)}, f32[576,128]{1,0:T(8,128)S(1)}) custom-call(f32[42,128]{1,0:T(8,128)S(1)} %bitcast.19, f32[64,128]{1,0:T(8,128)S(1)} %bitcast.20, f32[1792,128]{1,0:T(8,128)S(1)} %copy-done), custom_call_target="tpu_custom_call" | custom-call | flops 200000000 | bytes 971776 | tf_op jit(solution)/shard_map/pallas_call | solution.py:442
  17.5 0.0 copy-start.4
  17.5 0.7 copy-done.4
  18.2 0.0 copy-start.6
  18.2 0.7 copy-done.6
  18.9 1.8 %all-to-all-done = f32[16,16,128]{2,1,0:T(8,128)S(1)} async-done(((f32[16,16,128]{2,1,0:T(8,128)}), f32[16,16,128]{2,1,0:T(8,128)S(1)}, u32[]{:S(2)}, u32[]{:S(2)}) %all-to-all-start) | async-done | bytes 131104 | tf_op jit(solution)/shard_map/all_to_all | solution.py:528
  20.7 0.0 copy-done.1
  20.7 0.0 copy-start.7
  20.7 1.5 %shard_map.111 = f32[1024,128]{1,0:T(8,128)S(1)} custom-call(f32[256,128]{1,0:T(8,128)S(1)} %bitcast.13, f32[776,128]{1,0:T(8,128)S(1)} %get-tuple-element.10.first, bf16[2048,256]{1,0:T(8,128)(2,1)S(1)} %get-tuple-element.11.resonances, bf16[512,768]{1,0:T(8,128)(2,1)S(1)} %copy-done.1), custom_call_target="tpu_custom_call" | custom-call | flops 500000000 | bytes 2363392 | tf_op jit(solution)/shard_map/pallas_call | solution.py:442
  22.2 32.3 %all_to_all.26 = f32[256,4,128]{2,1,0:T(4,128)S(1)} all-to-all(f32[256,4,128]{2,1,0:T(4,128)S(1)} %bitcast.12), channel_id=1, replica_groups=mesh['lat'=16,'tm'=16] {'lat','tm'}, dimensions={0} | all-to-all | bytes 1048576 | tf_op jit(solution)/shard_map/all_to_all | solution.py:539
  54.5 0.0 copy-done.7
  54.5 0.0 copy-start.5
  54.5 0.0 copy-start.8
  54.5 0.0 copy-start.9
  54.5 2.8 %shard_map.112 = f32[256,128]{1,0:T(8,128)S(1)} custom-call(f32[1024,128]{1,0:T(8,128)S(1)} %bitcast.14, bf16[512,768]{1,0:T(8,128)(2,1)S(1)} %copy-done.1, f32[2064,128]{1,0:T(8,128)S(1)} %get-tuple-element.12.second, bf16[512,256]{1,0:T(8,128)(2,1)S(1)} %copy-done.7), custom_call_target="tpu_custom_call" | custom-call | flops 1000000000 | bytes 2629632 | tf_op jit(solution)/shard_map/pallas_call | solution.py:442
  57.4 18.1 %all_to_all.27 = f32[256,1,128]{2,1,0:T(1,128)S(1)} all-to-all(f32[256,1,128]{2,1,0:T(1,128)S(1)} %bitcast.18), channel_id=1, replica_groups=mesh['lat'=16,'tm'=16] {'lat','tm'}, dimensions={0} | all-to-all | bytes 262144 | tf_op jit(solution)/shard_map/all_to_all | solution.py:544
  75.5 0.0 copy-done.5
  75.5 0.0 copy-done.8
  75.5 0.0 copy-done.9
  75.5 2.2 %shard_map.113 = f32[256,128]{1,0:T(8,128)S(1)} custom-call(f32[256,128]{1,0:T(8,128)S(1)} %bitcast.16, bf16[2048,256]{1,0:T(8,128)(2,1)S(1)} %get-tuple-element.11.resonances, f32[576,128]{1,0:T(8,128)S(1)} %copy-done.5, bf16[1536,256]{1,0:T(8,128)(2,1)S(1)} %copy-done.8, f32[768,128]{1,0:T(8,128)S(1)} %copy-done.9), custom_call_target="tpu_custom_call" | custom-call | flops 800000000 | bytes 2654208 | tf_op jit(solution)/shard_map/pallas_call | solution.py:442
  77.8 12.5 %all_to_all.28 = f32[16,16,128]{2,1,0:T(8,128)S(1)} all-to-all(f32[16,16,128]{2,1,0:T(8,128)S(1)} %bitcast.17), channel_id=1, replica_groups=mesh['lat'=16,'tm'=16] {'tm'}, dimensions={0} | all-to-all | bytes 262144 | tf_op jit(solution)/shard_map/all_to_all | solution.py:549
  90.3 0.7 shard_map.114
  (1 shorter events, 0.0 us)
Async XLA Ops:
  0.0 0.9 copy-start.2
  1.6 19.1 %all-to-all-start = ((f32[16,16,128]{2,1,0:T(8,128)}), f32[16,16,128]{2,1,0:T(8,128)S(1)}, u32[]{:S(2)}, u32[]{:S(2)}) async-start(f32[16,16,128]{2,1,0:T(8,128)} %bitcast), calls=%async_computation | async-start | bytes 262144 | tf_op jit(solution)/shard_map/all_to_all | solution.py:528
  13.0 1.2 %copy-start = (f32[1792,128]{1,0:T(8,128)S(1)}, f32[1792,128]{1,0:T(8,128)}, u32[]{:S(2)}) copy-start(f32[1792,128]{1,0:T(8,128)} %constant.13.clone.twiddle) | copy-start | bytes 2752516
  14.2 0.8 copy-start.3
  15.0 5.7 %copy-start.1 = (bf16[512,768]{1,0:T(8,128)(2,1)S(1)}, bf16[512,768]{1,0:T(8,128)(2,1)}, u32[]{:S(2)}) copy-start(bf16[512,768]{1,0:T(8,128)(2,1)} %constant.10.clone.ahead) | copy-start | bytes 2359300
  17.5 0.7 copy-start.4
  18.2 0.7 copy-start.6
  20.7 33.8 %copy-start.7 = (bf16[512,256]{1,0:T(8,128)(2,1)S(1)}, bf16[512,256]{1,0:T(8,128)(2,1)}, u32[]{:S(2)}) copy-start(bf16[512,256]{1,0:T(8,128)(2,1)} %copy-done.6) | copy-start | bytes 786436
  54.5 21.0 %copy-start.5 = (f32[576,128]{1,0:T(8,128)S(1)}, f32[576,128]{1,0:T(8,128)}, u32[]{:S(2)}) copy-start(f32[576,128]{1,0:T(8,128)} %copy-done.4) | copy-start | bytes 884740
  54.5 21.0 %copy-start.8 = (bf16[1536,256]{1,0:T(8,128)(2,1)S(1)}, bf16[1536,256]{1,0:T(8,128)(2,1)}, u32[]{:S(2)}) copy-start(bf16[1536,256]{1,0:T(8,128)(2,1)} %constant.11.clone.back) | copy-start | bytes 2359300
  54.5 21.0 %copy-start.9 = (f32[768,128]{1,0:T(8,128)S(1)}, f32[768,128]{1,0:T(8,128)}, u32[]{:S(2)}) copy-start(f32[768,128]{1,0:T(8,128)} %constant.12.clone.shift) | copy-start | bytes 1179652

commit v4 on v3

--- a/solution.py
+++ b/solution.py
@@ -36,10 +36,6 @@
     small = small * (tq[:, None] == rq[None, :]) * (th[:, None] == rh[None, :])
     short = 2 * np.pi * (col[:64, None] * grid(256)[None, :]) / NT
     omega_lanes = np.tile(2 * np.pi * (16 * grid(256)[:, None] + grid(16)[None, :]) / NT, (1, 8))
-    twiddle = []
-    for k in range(1, 4):
-        theta = -2 * np.pi * (((q + k) % 4 - q)[None, :] * grid(256)[:, None]) / NX
-        twiddle += [np.cos(theta), np.sin(theta)]
     t = {}
     t["ahead"] = np.concatenate(
         [np.concatenate(split_table(x), 0) for x in (wide, small)], 1
@@ -49,7 +45,6 @@
     omega_part = np.concatenate([np.cos(omega_lanes), -np.sin(omega_lanes)], 0)
     twist = [twist[:, :128], twist[:, 128:]]
     t["shift"] = np.concatenate([omega_part / NT] + twist, 0).astype(np.float32)
-    t["twiddle"] = np.concatenate(twiddle + twist, 0).astype(np.float32)
     return t
 
 
@@ -165,14 +160,19 @@
     return pick_dot_nt(eye, rows)
 
 
-def pack(decay, detune, group_bin, spectral, lateral):
-    row = [decay, detune, jnp.zeros((128 - 2 * BINS,), F32), group_bin.astype(F32)]
-    return jnp.concatenate(row + [spectral, lateral]).reshape(42, 128)
+def pack(decay, detune, group_bin, spectral, lateral, occupation):
+    parts = [decay, detune, group_bin.astype(F32), spectral, lateral, occupation.T.reshape(-1)]
+    starts = [0, BINS, 128, 256, 256 + NT, 256 + NT + NX]
+    total = starts[-1] + parts[-1].size
+    padded = [
+        jnp.pad(part, (start, total - start - part.size)) for part, start in zip(parts, starts)
+    ]
+    return sum(padded[1:], padded[0]).reshape(total // 128, 128)
 
 
 def unpack(packed):
     return (packed[0:1, :BINS], packed[0:1, BINS : 2 * BINS], packed[1:2], packed[2:34],
-            packed[34:42])
+            packed[34:42], packed[42:])
 
 
 def couplings(drive, group_bin, occupation):
@@ -180,8 +180,8 @@
     return pick_dot_nt(member, occupation) * drive
 
 
-def prepare_first(packed, occupation, quad):
-    decay, detune_row, group_bin, spectral, _ = unpack(packed)
+def prepare_first(packed, quad):
+    decay, detune_row, group_bin, spectral, _, occupation = unpack(packed)
     params = bin_columns(decay, detune_row)
     detune, keep, lost, drive = (params[:, k : k + 1] for k in range(4))
     real, imag = [], []
@@ -211,11 +211,17 @@
     back_re, back_im = cosine_sine(jnp.where(index > NT // 2, NT - index, -index) * STEP)
     wrap_a = (cos * back_re - sin * back_im) * (1.0 / NT)
     wrap_b = (cos * back_im + sin * back_re) * (side * (1.0 / NT))
-    first = jnp.concatenate([wrap_a, wrap_b, jnp.broadcast_to(couple_row, (8, 128))], 0)
+    index = (iota((64, 256), 0) % 16) * iota((64, 256), 1)
+    tc, ts = cosine_sine(jnp.where(index > NT // 2, index - NT, index).astype(F32) * STEP)
+    first = jnp.concatenate(
+        [tc[:, :128], ts[:, :128], tc[:, 128:], ts[:, 128:], wrap_a, wrap_b,
+         jnp.broadcast_to(couple_row, (8, 128))],
+        0,
+    )
     return resonances, first, params, per_bin, spectral_parts
 
 
-def prepare_rest(packed, twiddle, made, here, quad):
+def prepare_rest(packed, made, here, quad):
     lateral = unpack(packed)[4]
     resonances, _, params, per_bin, (cos, sin) = made
     points = per_bin.shape[1]
@@ -259,13 +265,20 @@
     ]
     eight = iota((256, 128), 1) // 16
     flip = jnp.where(eight < 4, -1.0, 1.0)
+    index = iota((256, 128), 0)
+    cos1, sin1 = cosine_sine(index.astype(F32) * (-2.0 * math.pi / NX))
+    cos2, sin2 = cos1 * cos1 - sin1 * sin1, 2.0 * (cos1 * sin1)
+    cos3, sin3 = cos1 * cos2 - sin1 * sin2, cos1 * sin2 + sin1 * cos2
+    turns = [None, (cos1, sin1), (cos2, sin2), (cos3, sin3)]
     mixing = [None] * 8
     for k in range(4):
         re, im = blocks_re[k] * (1.0 / NX), blocks_im[k] * (1.0 / NX)
         if k == 0:
             real, imag = re + jnp.zeros((256, 128), F32), im * flip
         else:
-            cos, sin = twiddle[512 * k - 512 : 512 * k - 256], twiddle[512 * k - 256 : 512 * k]
+            near = eight % 4 + k < 4
+            cos = jnp.where(near, turns[k][0], turns[4 - k][0])
+            sin = jnp.where(near, turns[k][1], -turns[4 - k][1])
             real, imag = cos * re - sin * im, (cos * im + sin * re) * flip
         for r in (k, k + 4):
             mixing[r] = jnp.where((eight + r) % 8 // 4 == eight // 4, real, imag)
@@ -482,38 +495,39 @@
         copy.wait()
 
 
-PREPARED = (
-    shape(2048, 256, dtype=BF16), shape(776, 128), shape(2064, 128), shape(512, 256, dtype=BF16),
-    shape(576, 128),
-)
-
-
-def prepare_kernel(packed, occupation, twiddle, *outs):
+PREPARED = (shape(2560, 256, dtype=BF16), shape(3416, 128))
+
+
+def prepare_kernel(packed, ahead, tables, later):
     quad = lax.axis_index("tm")
     here = lax.axis_index("lat") * 16 + quad
     packed = packed[...]
-    made = prepare_first(packed, occupation[...], quad)
-    first = jnp.concatenate([twiddle[1536:], made[1]], 0)
-    values = (made[0], first, *prepare_rest(packed, twiddle, made, here, quad))
-    for ref, value in zip(outs, values):
-        ref[...] = value
-
-
-def rows_kernel(field, first, resonances, ahead, out):
-    spectrum, *rest = to_rows(field[...], first, resonances, ahead, lane_roll)
+    made = prepare_first(packed, quad)
+    second, second_tables, third = prepare_rest(packed, made, here, quad)
+    tables[:2048] = made[0]
+    tables[2048:] = second_tables
+    later[:2064] = second
+    later[2064:2640] = third
+    later[2640:] = made[1]
+
+
+def rows_kernel(field, tables, later, ahead, out):
+    spectrum, *rest = to_rows(
+        field[...], later[2640:], tables.at[:2048], ahead, lane_roll
+    )
     out[pl.ds(0, 256, stride=4), :] = spectrum
     for k, row in enumerate(rest):
         out[pl.ds(k + 1, 256, stride=4), :] = jnp.broadcast_to(row, (256, 128))
 
 
-def columns_kernel(message, ahead, second, second_tables, out):
+def columns_kernel(message, ahead, tables, later, out):
     parts = [message[pl.ds(k, 256, stride=4), :] for k in range(4)]
-    out[...] = columns_step(parts, ahead[:, :512], second, second_tables[...], lane_roll)
-
-
-def blocks_kernel(spectrum, resonances, third, back, shift, out):
+    out[...] = columns_step(parts, ahead[:, :512], later, tables[2048:], lane_roll)
+
+
+def blocks_kernel(spectrum, tables, later, back, shift, out):
     out[...] = to_blocks(
-        spectrum[...], resonances[...], third[...], back[...], shift[...], lane_roll
+        spectrum[...], tables[:2048], later[2064:2640], back[...], shift[...], lane_roll
     )
 
 
@@ -526,25 +540,27 @@
         cut_kernel, shape(256, 128), [VMEM_SPEC], VMEM_SPEC, [], light_field, flops=1000
     )
     rows = lax.all_to_all(rows.reshape(16, 16, 128), "tm", 0, 0, tiled=True)
-    packed = pack(bin_decay, bin_detune, group_bin, spectral_phase, lateral_phase)
-    resonances, first, second, second_tables, third = call(
-        prepare_kernel, PREPARED, [VMEM_SPEC] * 3, (VMEM_SPEC,) * 5, [],
-        packed, occupation.T, t["twiddle"], flops=200_000_000,
+    packed = pack(
+        bin_decay, bin_detune, group_bin, spectral_phase, lateral_phase, occupation
+    )
+    tables, later = call(
+        prepare_kernel, PREPARED, [VMEM_SPEC] * 2, (VMEM_SPEC,) * 2, [], packed, t["ahead"],
+        flops=200_000_000,
     )
     message = call(
         rows_kernel, shape(1024, 128), [VMEM_SPEC] * 4, VMEM_SPEC, [],
-        rows.reshape(256, 128), first, resonances, t["ahead"],
+        rows.reshape(256, 128), tables, later, t["ahead"],
         flops=500_000_000,
     )
     message = lax.all_to_all(message.reshape(256, 4, 128), BOTH, 0, 0, tiled=True)
     columns = call(
         columns_kernel, shape(256, 128), [VMEM_SPEC] * 4, VMEM_SPEC, [],
-        message.reshape(1024, 128), t["ahead"], second, second_tables, flops=1_000_000_000,
+        message.reshape(1024, 128), t["ahead"], tables, later, flops=1_000_000_000,
     )
     spectrum = lax.all_to_all(columns, BOTH, 0, 0, tiled=True)
     finished = call(
         blocks_kernel, shape(256, 128), [VMEM_SPEC] * 5, VMEM_SPEC, [],
-        spectrum, resonances, third, t["back"], t["shift"], flops=800_000_000,
+        spectrum, tables, later, t["back"], t["shift"], flops=800_000_000,
     )
     turned = lax.all_to_all(finished.reshape(16, 16, 128), "tm", 0, 0, tiled=True)
     return call(

time: 91.4 us -> 90.4 us (0.989)
  blocking collectives: 62.9 us -> 60.8 us
  waiting for transfers between devices: 1.84 us -> 3.93 us
  local copies, waits for them, and re-layouts: 5.1 us -> 3.18 us
    all_to_all x1, waiting for transfers between devices: 1.84 us -> 3.93 us  [on_device(): rows = lax.all_to_all(rows.reshape(16, 16, 128), 'tm', 0, 0, tiled=True)]
    all_to_all x1, blocking collectives: 32.3 us -> 30.2 us  [on_device(): lax.all_to_all(message.reshape(256, 4, 128), BOTH, 0, 0, tiled=True)]
    unnamed x20 -> x10, local copies, waits for them, and re-layouts: 4.28 us -> 3.18 us
where the time goes in v4:
time: 90.4 us; the launch traced here: 89.9 us
  blocking collectives  60.8 us (67%)
  Pallas kernels  10.5 us (12%)
  starting transfers between devices  9.98 us (11%)
  waiting for transfers between devices  3.93 us (4%)
  local copies, waits for them, and re-layouts  3.18 us (4%)
  other arithmetic  1.5 us (2%)
    all_to_all x1, blocking collectives, on_device(): lax.all_to_all(message.reshape(256, 4, 128), BOTH, 0, 0, tiled=True)  30.2 us
    all_to_all x1, blocking collectives, on_device(): spectrum = lax.all_to_all(columns, BOTH, 0, 0, tiled=True)  18.1 us
    all_to_all x1, blocking collectives, on_device(): lax.all_to_all(finished.reshape(16, 16, 128), 'tm', 0, 0, tiled=True)  12.5 us
    pallas_call x6, Pallas kernels, call(): pl.pallas_call(kernel, out_shape=out_shape, in_specs=in_specs, out_specs=...  10.5 us
    all_to_all x1, starting transfers between devices, on_device(): rows = lax.all_to_all(rows.reshape(16, 16, 128), 'tm', 0, 0, tiled=True)  9.98 us
    all_to_all x1, waiting for transfers between devices, on_device(): rows = lax.all_to_all(rows.reshape(16, 16, 128), 'tm', 0, 0, tiled=True)  3.93 us
    unnamed x10, local copies, waits for them, and re-layouts  3.18 us
  transfers between devices with their start and end apart: 1, of which 1 were waited for; matrix products, arithmetic and copies ran while one was open for 2% of the time, Pallas kernels for 3%

profile of v4, /device:TPU:1, one launch (start us, length us, event | category | flops | bytes accessed | tf_op | source)
XLA Modules:
  0.0 89.9 jit_solution(5896230349896254243)
XLA Ops:
  0.0 0.0 copy-start.4
  0.0 0.9 %copy-done.4 = f32[2,64,256]{2,1,0:T(8,128)S(1)} copy-done((f32[2,64,256]{2,1,0:T(8,128)S(1)}, f32[2,64,256]{2,1,0:T(8,128)}, u32[]{:S(2)}) %copy-start.4) | copy-done | bytes 131096
  0.9 0.7 shard_map.100
  1.6 10.0 %all-to-all-start = ((f32[16,16,128]{2,1,0:T(8,128)}), f32[16,16,128]{2,1,0:T(8,128)S(1)}, u32[]{:S(2)}, u32[]{:S(2)}) async-start(f32[16,16,128]{2,1,0:T(8,128)} %bitcast), calls=%async_computation | async-start | bytes 262144 | tf_op jit(solution)/shard_map/all_to_all | solution.py:542
  11.6 0.7 convert_element_type.15
  12.2 0.8 add_bitcast_fusion.packed
  13.1 0.0 copy-start
  13.1 1.1 %copy-done = bf16[512,768]{1,0:T(8,128)(2,1)S(1)} copy-done((bf16[512,768]{1,0:T(8,128)(2,1)S(1)}, bf16[512,768]{1,0:T(8,128)(2,1)}, u32[]{:S(2)}) %copy-start) | copy-done | bytes 786456
  14.2 2.6 %shard_map.101 = (bf16[2560,256]{1,0:T(8,128)(2,1)S(1)}, f32[3416,128]{1,0:T(8,128)S(1)}) custom-call(f32[106,128]{1,0:T(8,128)S(1)} %add_bitcast_fusion.packed, bf16[512,768]{1,0:T(8,128)(2,1)S(1)} %copy-done), custom_call_target="tpu_custom_call" | custom-call | flops 200000000 | bytes 840704 | tf_op jit(solution)/shard_map/pallas_call | solution.py:455
  16.8 3.9 %all-to-all-done = f32[16,16,128]{2,1,0:T(8,128)S(1)} async-done(((f32[16,16,128]{2,1,0:T(8,128)}), f32[16,16,128]{2,1,0:T(8,128)S(1)}, u32[]{:S(2)}, u32[]{:S(2)}) %all-to-all-start) | async-done | bytes 131104 | tf_op jit(solution)/shard_map/all_to_all | solution.py:542
  20.7 0.0 copy-start.1
  20.7 1.1 %copy-done.1 = bf16[512,768]{1,0:T(8,128)(2,1)S(1)} copy-done((bf16[512,768]{1,0:T(8,128)(2,1)S(1)}, bf16[512,768]{1,0:T(8,128)(2,1)}, u32[]{:S(2)}) %copy-start.1) | copy-done | bytes 786456
  21.9 1.5 %shard_map.102 = f32[1024,128]{1,0:T(8,128)S(1)} custom-call(f32[256,128]{1,0:T(8,128)S(1)} %bitcast.17, bf16[2560,256]{1,0:T(8,128)(2,1)S(1)} %get-tuple-element.7.tables, f32[3416,128]{1,0:T(8,128)S(1)} %get-tuple-element.8.later, bf16[512,768]{1,0:T(8,128)(2,1)S(1)} %copy-done.1), custom_call_target="tpu_custom_call" | custom-call | flops 500000000 | bytes 3977216 | tf_op jit(solution)/shard_map/pallas_call | solution.py:455
  23.4 30.2 %all_to_all.26 = f32[256,4,128]{2,1,0:T(4,128)S(1)} all-to-all(f32[256,4,128]{2,1,0:T(4,128)S(1)} %bitcast.16), channel_id=1, replica_groups=mesh['lat'=16,'tm'=16] {'lat','tm'}, dimensions={0} | all-to-all | bytes 1048576 | tf_op jit(solution)/shard_map/all_to_all | solution.py:555
  53.6 0.0 copy-start.2
  53.6 0.0 copy-start.3
  53.6 2.8 %shard_map.103 = f32[256,128]{1,0:T(8,128)S(1)} custom-call(f32[1024,128]{1,0:T(8,128)S(1)} %bitcast.15, bf16[512,768]{1,0:T(8,128)(2,1)S(1)} %copy-done.1, bf16[2560,256]{1,0:T(8,128)(2,1)S(1)} %get-tuple-element.7.tables, f32[3416,128]{1,0:T(8,128)S(1)} %get-tuple-element.8.later), custom_call_target="tpu_custom_call" | custom-call | flops 1000000000 | bytes 4370432 | tf_op jit(solution)/shard_map/pallas_call | solution.py:455
  56.4 18.1 %all_to_all.27 = f32[256,1,128]{2,1,0:T(1,128)S(1)} all-to-all(f32[256,1,128]{2,1,0:T(1,128)S(1)} %bitcast.20), channel_id=1, replica_groups=mesh['lat'=16,'tm'=16] {'lat','tm'}, dimensions={0} | all-to-all | bytes 262144 | tf_op jit(solution)/shard_map/all_to_all | solution.py:560
  74.5 0.0 copy-done.2
  74.5 0.0 copy-done.3
  74.5 2.2 %shard_map.104 = f32[256,128]{1,0:T(8,128)S(1)} custom-call(f32[256,128]{1,0:T(8,128)S(1)} %bitcast.18, bf16[2560,256]{1,0:T(8,128)(2,1)S(1)} %get-tuple-element.7.tables, f32[3416,128]{1,0:T(8,128)S(1)} %get-tuple-element.8.later, bf16[1536,256]{1,0:T(8,128)(2,1)S(1)} %copy-done.2, f32[768,128]{1,0:T(8,128)S(1)} %copy-done.3), custom_call_target="tpu_custom_call" | custom-call | flops 800000000 | bytes 4370432 | tf_op jit(solution)/shard_map/pallas_call | solution.py:455
  76.8 12.5 %all_to_all.28 = f32[16,16,128]{2,1,0:T(8,128)S(1)} all-to-all(f32[16,16,128]{2,1,0:T(8,128)S(1)} %bitcast.19), channel_id=1, replica_groups=mesh['lat'=16,'tm'=16] {'tm'}, dimensions={0} | all-to-all | bytes 262144 | tf_op jit(solution)/shard_map/all_to_all | solution.py:565
  89.3 0.7 shard_map.105
Async XLA Ops:
  0.0 0.9 %copy-start.4 = (f32[2,64,256]{2,1,0:T(8,128)S(1)}, f32[2,64,256]{2,1,0:T(8,128)}, u32[]{:S(2)}) copy-start(f32[2,64,256]{2,1,0:T(8,128)} %field.1) | copy-start | bytes 393220
  1.6 19.1 %all-to-all-start = ((f32[16,16,128]{2,1,0:T(8,128)}), f32[16,16,128]{2,1,0:T(8,128)S(1)}, u32[]{:S(2)}, u32[]{:S(2)}) async-start(f32[16,16,128]{2,1,0:T(8,128)} %bitcast), calls=%async_computation | async-start | bytes 262144 | tf_op jit(solution)/shard_map/all_to_all | solution.py:542
  13.1 1.1 %copy-start = (bf16[512,768]{1,0:T(8,128)(2,1)S(1)}, bf16[512,768]{1,0:T(8,128)(2,1)}, u32[]{:S(2)}) copy-start(bf16[512,768]{1,0:T(8,128)(2,1)} %constant.9.clone.ahead) | copy-start | bytes 2359300
  20.7 1.1 %copy-start.1 = (bf16[512,768]{1,0:T(8,128)(2,1)S(1)}, bf16[512,768]{1,0:T(8,128)(2,1)}, u32[]{:S(2)}) copy-start(bf16[512,768]{1,0:T(8,128)(2,1)} %constant.9.clone.ahead) | copy-start | bytes 2359300
  53.6 20.9 %copy-start.2 = (bf16[1536,256]{1,0:T(8,128)(2,1)S(1)}, bf16[1536,256]{1,0:T(8,128)(2,1)}, u32[]{:S(2)}) copy-start(bf16[1536,256]{1,0:T(8,128)(2,1)} %constant.10.clone.back) | copy-start | bytes 2359300
  53.6 20.9 %copy-start.3 = (f32[768,128]{1,0:T(8,128)S(1)}, f32[768,128]{1,0:T(8,128)}, u32[]{:S(2)}) copy-start(f32[768,128]{1,0:T(8,128)} %constant.11.clone.shift) | copy-start | bytes 1179652

commit v5 on v4

--- a/solution.py
+++ b/solution.py
@@ -161,11 +161,11 @@
 
 
 def pack(decay, detune, group_bin, spectral, lateral, occupation):
-    parts = [decay, detune, group_bin.astype(F32), spectral, lateral, occupation.T.reshape(-1)]
+    parts = [decay, detune, group_bin, spectral, lateral, occupation.T.reshape(-1)]
     starts = [0, BINS, 128, 256, 256 + NT, 256 + NT + NX]
     total = starts[-1] + parts[-1].size
     padded = [
-        jnp.pad(part, (start, total - start - part.size)) for part, start in zip(parts, starts)
+        jnp.pad(part, (start, total - start - part.size)).astype(F32) for part, start in zip(parts, starts)
     ]
     return sum(padded[1:], padded[0]).reshape(total // 128, 128)
 
@@ -206,15 +206,15 @@
     lane_of = (iota((128, 128), 0) % 16 == iota((128, 128), 1) % 16).astype(BF16)
     cos = exact_dot(jnp.where(mine, pick_dot(row_of, cos), 0.0), lane_of)
     sin = exact_dot(jnp.where(mine, pick_dot(row_of, sin), 0.0), lane_of)
-    side = jnp.where(iota((256, 128), 1) < 64, -1.0, 1.0)
     index = 16 * iota((256, 128), 0) + iota((256, 128), 1) % 16
     back_re, back_im = cosine_sine(jnp.where(index > NT // 2, NT - index, -index) * STEP)
     wrap_a = (cos * back_re - sin * back_im) * (1.0 / NT)
-    wrap_b = (cos * back_im + sin * back_re) * (side * (1.0 / NT))
+    wrap_b = (cos * back_im + sin * back_re) * (1.0 / NT)
     index = (iota((64, 256), 0) % 16) * iota((64, 256), 1)
     tc, ts = cosine_sine(jnp.where(index > NT // 2, index - NT, index).astype(F32) * STEP)
     first = jnp.concatenate(
-        [tc[:, :128], ts[:, :128], tc[:, 128:], ts[:, 128:], wrap_a, wrap_b,
+        [tc[:, :128], ts[:, :128], tc[:, 128:], ts[:, 128:],
+         jnp.where(iota((256, 128), 1) < 64, wrap_a, wrap_b),
          jnp.broadcast_to(couple_row, (8, 128))],
         0,
     )
@@ -264,24 +264,22 @@
         (i[0] - i[2]) + (r[1] - r[3]),
     ]
     eight = iota((256, 128), 1) // 16
-    flip = jnp.where(eight < 4, -1.0, 1.0)
     index = iota((256, 128), 0)
     cos1, sin1 = cosine_sine(index.astype(F32) * (-2.0 * math.pi / NX))
     cos2, sin2 = cos1 * cos1 - sin1 * sin1, 2.0 * (cos1 * sin1)
     cos3, sin3 = cos1 * cos2 - sin1 * sin2, cos1 * sin2 + sin1 * cos2
     turns = [None, (cos1, sin1), (cos2, sin2), (cos3, sin3)]
-    mixing = [None] * 8
+    mixing = []
     for k in range(4):
         re, im = blocks_re[k] * (1.0 / NX), blocks_im[k] * (1.0 / NX)
         if k == 0:
-            real, imag = re + jnp.zeros((256, 128), F32), im * flip
+            real, imag = re, im
         else:
             near = eight % 4 + k < 4
             cos = jnp.where(near, turns[k][0], turns[4 - k][0])
             sin = jnp.where(near, turns[k][1], -turns[4 - k][1])
-            real, imag = cos * re - sin * im, (cos * im + sin * re) * flip
-        for r in (k, k + 4):
-            mixing[r] = jnp.where((eight + r) % 8 // 4 == eight // 4, real, imag)
+            real, imag = cos * re - sin * im, cos * im + sin * re
+        mixing.append(jnp.where(eight < 4, real, imag))
     mixing = jnp.concatenate(mixing, 0)
     rows = jnp.concatenate([params[:16]] * 4 + [params[16:]] * 4, 0)
     g_re, g_im = resonance(
@@ -334,6 +332,12 @@
     return sums[0] + half_sign((BINS, 128)) * roll(sums[1], 64)
 
 
+def unfold(pair, roll):
+    turned = roll(pair, 64)
+    left = iota((256, 128), 1) < 64
+    return jnp.where(left, pair, turned), jnp.where(left, -turned, pair)
+
+
 def untwist(pair):
     return (jnp.concatenate([pair[k : k + 64], pair[128 + k : 192 + k]], 1) for k in (0, 64))
 
@@ -349,14 +353,15 @@
     )
     product = dot_nt(ahead[:, :512], jnp.concatenate(halves(both), 0))
     spectrum = quadrants(product, 256, 128)
-    weighted = first[256:512] * spectrum + first[512:768] * roll(spectrum, 64)
+    wrap_a, wrap_b = unfold(first[256:512], roll)
+    weighted = wrap_a * spectrum + wrap_b * roll(spectrum, 64)
     state = wrap_state(resonances[...], weighted, roll)
     place = (iota((128, 256), 0) // 16 == iota((128, 256), 1) % 128 // 16).astype(BF16)
     parts = exact_dot(state, place)
     lane = iota((BINS, 256), 1)
     chosen = iota((BINS, 256), 0) == lane // 128 * 16 + lane % 16
     state_row = jnp.sum(jnp.where(chosen, parts, 0.0), axis=0, keepdims=True)
-    return spectrum, state_row[:, :128], state_row[:, 128:], first[768:769]
+    return spectrum, state_row[:, :128], state_row[:, 128:], first[512:513]
 
 
 def diffract(blocks, wide, mixing, roll):
@@ -384,7 +389,12 @@
 
 def columns_step(message, wide, second, second_tables, roll):
     field, state0, state1, couple = message
-    mixing = [second[16 + 256 * k : 272 + 256 * k] for k in range(8)]
+    eight = iota((256, 128), 1) // 16
+    mixing = [None] * 8
+    for k in range(4):
+        real, imag = unfold(second[16 + 256 * k : 272 + 256 * k], roll)
+        for r in (k, k + 4):
+            mixing[r] = jnp.where((eight + r) % 8 // 4 == eight // 4, real, imag)
     field, state0, state1 = diffract([field, state0, state1], wide, mixing, roll)
     product = dot(jnp.concatenate(halves(couple), 0), second_tables[:128])
     rest = dot(couple.astype(BF16), second_tables[128:256])
@@ -495,10 +505,10 @@
         copy.wait()
 
 
-PREPARED = (shape(2560, 256, dtype=BF16), shape(3416, 128))
-
-
-def prepare_kernel(packed, ahead, tables, later):
+PREPARED = (shape(2560, 256, dtype=BF16), shape(2136, 128))
+
+
+def prepare_kernel(packed, tables, later):
     quad = lax.axis_index("tm")
     here = lax.axis_index("lat") * 16 + quad
     packed = packed[...]
@@ -506,14 +516,14 @@
     second, second_tables, third = prepare_rest(packed, made, here, quad)
     tables[:2048] = made[0]
     tables[2048:] = second_tables
-    later[:2064] = second
-    later[2064:2640] = third
-    later[2640:] = made[1]
+    later[:1040] = second
+    later[1040:1616] = third
+    later[1616:] = made[1]
 
 
 def rows_kernel(field, tables, later, ahead, out):
     spectrum, *rest = to_rows(
-        field[...], later[2640:], tables.at[:2048], ahead, lane_roll
+        field[...], later[1616:], tables.at[:2048], ahead, lane_roll
     )
     out[pl.ds(0, 256, stride=4), :] = spectrum
     for k, row in enumerate(rest):
@@ -527,7 +537,7 @@
 
 def blocks_kernel(spectrum, tables, later, back, shift, out):
     out[...] = to_blocks(
-        spectrum[...], tables[:2048], later[2064:2640], back[...], shift[...], lane_roll
+        spectrum[...], tables[:2048], later[1040:1616], back[...], shift[...], lane_roll
     )
 
 
@@ -544,23 +554,22 @@
         bin_decay, bin_detune, group_bin, spectral_phase, lateral_phase, occupation
     )
     tables, later = call(
-        prepare_kernel, PREPARED, [VMEM_SPEC] * 2, (VMEM_SPEC,) * 2, [], packed, t["ahead"],
-        flops=200_000_000,
+        prepare_kernel, PREPARED, [VMEM_SPEC], (VMEM_SPEC,) * 2, [], packed, flops=4_000_000_000
     )
     message = call(
         rows_kernel, shape(1024, 128), [VMEM_SPEC] * 4, VMEM_SPEC, [],
         rows.reshape(256, 128), tables, later, t["ahead"],
-        flops=500_000_000,
+        flops=1_500_000_000,
     )
     message = lax.all_to_all(message.reshape(256, 4, 128), BOTH, 0, 0, tiled=True)
     columns = call(
         columns_kernel, shape(256, 128), [VMEM_SPEC] * 4, VMEM_SPEC, [],
-        message.reshape(1024, 128), t["ahead"], tables, later, flops=1_000_000_000,
+        message.reshape(1024, 128), t["ahead"], tables, later, flops=3_000_000_000,
     )
     spectrum = lax.all_to_all(columns, BOTH, 0, 0, tiled=True)
     finished = call(
         blocks_kernel, shape(256, 128), [VMEM_SPEC] * 5, VMEM_SPEC, [],
-        spectrum, tables, later, t["back"], t["shift"], flops=800_000_000,
+        spectrum, tables, later, t["back"], t["shift"], flops=2_300_000_000,
     )
     turned = lax.all_to_all(finished.reshape(16, 16, 128), "tm", 0, 0, tiled=True)
     return call(

time: 90.4 us -> 88.5 us (0.979)
  local copies, waits for them, and re-layouts: 3.18 us -> 0.91 us
  waiting for transfers between devices: 3.93 us -> 5.78 us
    unnamed x10 -> x8, local copies, waits for them, and re-layouts: 3.18 us -> 0.91 us
    all_to_all x1, waiting for transfers between devices: 3.93 us -> 5.78 us  [on_device(): rows = lax.all_to_all(rows.reshape(16, 16, 128), 'tm', 0, 0, tiled=True)]
  transfers between devices with their start and end apart: 1 -> 1, of which waited for: 1 -> 1; matrix products, arithmetic and copies ran while one was open for 2% -> 1% of each run, Pallas kernels for 3% -> 3%
where the time goes in v5:
time: 88.5 us; the launch traced here: 88.2 us
  blocking collectives  60.2 us (68%)
  Pallas kernels  10.5 us (12%)
  starting transfers between devices  9.98 us (11%)
  waiting for transfers between devices  5.78 us (7%)
  local copies, waits for them, and re-layouts  0.91 us (1%)
    all_to_all x1, blocking collectives, on_device(): lax.all_to_all(message.reshape(256, 4, 128), BOTH, 0, 0, tiled=True)  29.5 us
    all_to_all x1, blocking collectives, on_device(): spectrum = lax.all_to_all(columns, BOTH, 0, 0, tiled=True)  18.1 us
    all_to_all x1, blocking collectives, on_device(): lax.all_to_all(finished.reshape(16, 16, 128), 'tm', 0, 0, tiled=True)  12.5 us
    pallas_call x6, Pallas kernels, call(): pl.pallas_call(kernel, out_shape=out_shape, in_specs=in_specs, out_specs=...  10.5 us
    all_to_all x1, starting transfers between devices, on_device(): rows = lax.all_to_all(rows.reshape(16, 16, 128), 'tm', 0, 0, tiled=True)  9.98 us
    all_to_all x1, waiting for transfers between devices, on_device(): rows = lax.all_to_all(rows.reshape(16, 16, 128), 'tm', 0, 0, tiled=True)  5.78 us
  transfers between devices with their start and end apart: 1, of which 1 were waited for; matrix products, arithmetic and copies ran while one was open for 1% of the time, Pallas kernels for 3%

profile of v5, /device:TPU:1, one launch (start us, length us, event | category | flops | bytes accessed | tf_op | source)
XLA Modules:
  0.0 88.2 jit_solution(8738824460144557245)
XLA Ops:
  0.0 0.0 copy-start
  0.0 0.9 %copy-done = f32[2,64,256]{2,1,0:T(8,128)S(1)} copy-done((f32[2,64,256]{2,1,0:T(8,128)S(1)}, f32[2,64,256]{2,1,0:T(8,128)}, u32[]{:S(2)}) %copy-start) | copy-done | bytes 131096
  0.9 0.7 shard_map.100
  1.6 10.0 %all-to-all-start = ((f32[16,16,128]{2,1,0:T(8,128)}), f32[16,16,128]{2,1,0:T(8,128)S(1)}, u32[]{:S(2)}, u32[]{:S(2)}) async-start(f32[16,16,128]{2,1,0:T(8,128)} %bitcast), calls=%async_computation | async-start | bytes 262144 | tf_op jit(solution)/shard_map/all_to_all | solution.py:552
  11.6 0.8 add_bitcast_fusion.packed
  12.4 0.0 copy-start.1
  12.4 2.5 %shard_map.101 = (bf16[2560,256]{1,0:T(8,128)(2,1)S(1)}, f32[2136,128]{1,0:T(8,128)S(1)}) custom-call(f32[106,128]{1,0:T(8,128)S(1)} %add_bitcast_fusion.packed), custom_call_target="tpu_custom_call" | custom-call | flops 4000000000 | bytes 54272 | tf_op jit(solution)/shard_map/pallas_call | solution.py:465
  14.9 5.8 %all-to-all-done = f32[16,16,128]{2,1,0:T(8,128)S(1)} async-done(((f32[16,16,128]{2,1,0:T(8,128)}), f32[16,16,128]{2,1,0:T(8,128)S(1)}, u32[]{:S(2)}, u32[]{:S(2)}) %all-to-all-start) | async-done | bytes 131104 | tf_op jit(solution)/shard_map/all_to_all | solution.py:552
  20.7 0.0 copy-done.1
  20.7 1.5 %shard_map.102 = f32[1024,128]{1,0:T(8,128)S(1)} custom-call(f32[256,128]{1,0:T(8,128)S(1)} %bitcast.18, bf16[2560,256]{1,0:T(8,128)(2,1)S(1)} %get-tuple-element.7.tables, f32[2136,128]{1,0:T(8,128)S(1)} %get-tuple-element.8.later, bf16[512,768]{1,0:T(8,128)(2,1)S(1)} %copy-done.1), custom_call_target="tpu_custom_call" | custom-call | flops 1500000000 | bytes 3321856 | tf_op jit(solution)/shard_map/pallas_call | solution.py:465
  22.2 29.5 %all_to_all.26 = f32[256,4,128]{2,1,0:T(4,128)S(1)} all-to-all(f32[256,4,128]{2,1,0:T(4,128)S(1)} %bitcast.16), channel_id=1, replica_groups=mesh['lat'=16,'tm'=16] {'lat','tm'}, dimensions={0} | all-to-all | bytes 1048576 | tf_op jit(solution)/shard_map/all_to_all | solution.py:564
  51.8 0.0 copy-start.2
  51.8 0.0 copy-start.3
  51.8 2.9 %shard_map.103 = f32[256,128]{1,0:T(8,128)S(1)} custom-call(f32[1024,128]{1,0:T(8,128)S(1)} %bitcast.15, bf16[512,768]{1,0:T(8,128)(2,1)S(1)} %copy-done.1, bf16[2560,256]{1,0:T(8,128)(2,1)S(1)} %get-tuple-element.7.tables, f32[2136,128]{1,0:T(8,128)S(1)} %get-tuple-element.8.later), custom_call_target="tpu_custom_call" | custom-call | flops 3000000000 | bytes 3715072 | tf_op jit(solution)/shard_map/pallas_call | solution.py:465
  54.6 18.1 %all_to_all.27 = f32[256,1,128]{2,1,0:T(1,128)S(1)} all-to-all(f32[256,1,128]{2,1,0:T(1,128)S(1)} %bitcast.21), channel_id=1, replica_groups=mesh['lat'=16,'tm'=16] {'lat','tm'}, dimensions={0} | all-to-all | bytes 262144 | tf_op jit(solution)/shard_map/all_to_all | solution.py:569
  72.8 0.0 copy-done.2
  72.8 0.0 copy-done.3
  72.8 2.2 %shard_map.104 = f32[256,128]{1,0:T(8,128)S(1)} custom-call(f32[256,128]{1,0:T(8,128)S(1)} %bitcast.19, bf16[2560,256]{1,0:T(8,128)(2,1)S(1)} %get-tuple-element.7.tables, f32[2136,128]{1,0:T(8,128)S(1)} %get-tuple-element.8.later, bf16[1536,256]{1,0:T(8,128)(2,1)S(1)} %copy-done.2, f32[768,128]{1,0:T(8,128)S(1)} %copy-done.3), custom_call_target="tpu_custom_call" | custom-call | flops 2300000000 | bytes 3715072 | tf_op jit(solution)/shard_map/pallas_call | solution.py:465
  75.0 12.5 %all_to_all.28 = f32[16,16,128]{2,1,0:T(8,128)S(1)} all-to-all(f32[16,16,128]{2,1,0:T(8,128)S(1)} %bitcast.20), channel_id=1, replica_groups=mesh['lat'=16,'tm'=16] {'tm'}, dimensions={0} | all-to-all | bytes 262144 | tf_op jit(solution)/shard_map/all_to_all | solution.py:574
  87.5 0.7 shard_map.105
Async XLA Ops:
  0.0 0.9 %copy-start = (f32[2,64,256]{2,1,0:T(8,128)S(1)}, f32[2,64,256]{2,1,0:T(8,128)}, u32[]{:S(2)}) copy-start(f32[2,64,256]{2,1,0:T(8,128)} %field.1) | copy-start | bytes 393220
  1.6 19.1 %all-to-all-start = ((f32[16,16,128]{2,1,0:T(8,128)}), f32[16,16,128]{2,1,0:T(8,128)S(1)}, u32[]{:S(2)}, u32[]{:S(2)}) async-start(f32[16,16,128]{2,1,0:T(8,128)} %bitcast), calls=%async_computation | async-start | bytes 262144 | tf_op jit(solution)/shard_map/all_to_all | solution.py:552
  12.4 8.3 %copy-start.1 = (bf16[512,768]{1,0:T(8,128)(2,1)S(1)}, bf16[512,768]{1,0:T(8,128)(2,1)}, u32[]{:S(2)}) copy-start(bf16[512,768]{1,0:T(8,128)(2,1)} %constant.10.clone.ahead) | copy-start | bytes 2359300
  51.8 21.0 %copy-start.2 = (bf16[1536,256]{1,0:T(8,128)(2,1)S(1)}, bf16[1536,256]{1,0:T(8,128)(2,1)}, u32[]{:S(2)}) copy-start(bf16[1536,256]{1,0:T(8,128)(2,1)} %constant.11.clone.back) | copy-start | bytes 2359300
  51.8 21.0 %copy-start.3 = (f32[768,128]{1,0:T(8,128)S(1)}, f32[768,128]{1,0:T(8,128)}, u32[]{:S(2)}) copy-start(f32[768,128]{1,0:T(8,128)} %constant.12.clone.shift) | copy-start | bytes 1179652

commit v6 on v5

--- a/solution.py
+++ b/solution.py
@@ -80,7 +80,8 @@
 
 
 def quadrants(product, rows, cols):
-    return product[:rows, :cols] + (product[:rows, cols:] + product[rows:, :cols])
+    rest = product[:rows, cols:] + (product[rows:, :cols] + product[rows:, cols:])
+    return product[:rows, :cols] + rest
 
 
 def table_times(table, value):

time: 88.5 us -> 88.5 us (level)
  no operation moved by 1% of the time
where the time goes in v6:
time: 88.5 us; the launch traced here: 88.2 us
  blocking collectives  60.2 us (68%)
  Pallas kernels  10.5 us (12%)
  starting transfers between devices  9.98 us (11%)
  waiting for transfers between devices  5.78 us (7%)
  local copies, waits for them, and re-layouts  0.91 us (1%)
    all_to_all x1, blocking collectives, on_device(): lax.all_to_all(message.reshape(256, 4, 128), BOTH, 0, 0, tiled=True)  29.5 us
    all_to_all x1, blocking collectives, on_device(): spectrum = lax.all_to_all(columns, BOTH, 0, 0, tiled=True)  18.1 us
    all_to_all x1, blocking collectives, on_device(): lax.all_to_all(finished.reshape(16, 16, 128), 'tm', 0, 0, tiled=True)  12.5 us
    pallas_call x6, Pallas kernels, call(): pl.pallas_call(kernel, out_shape=out_shape, in_specs=in_specs, out_specs=...  10.5 us
    all_to_all x1, starting transfers between devices, on_device(): rows = lax.all_to_all(rows.reshape(16, 16, 128), 'tm', 0, 0, tiled=True)  9.98 us
    all_to_all x1, waiting for transfers between devices, on_device(): rows = lax.all_to_all(rows.reshape(16, 16, 128), 'tm', 0, 0, tiled=True)  5.78 us
  transfers between devices with their start and end apart: 1, of which 1 were waited for; matrix products, arithmetic and copies ran while one was open for 1% of the time, Pallas kernels for 3%

profile of v6, /device:TPU:1, one launch (start us, length us, event | category | flops | bytes accessed | tf_op | source)
XLA Modules:
  0.0 88.2 jit_solution(6244187872537858376)
XLA Ops:
  0.0 0.0 copy-start
  0.0 0.9 %copy-done = f32[2,64,256]{2,1,0:T(8,128)S(1)} copy-done((f32[2,64,256]{2,1,0:T(8,128)S(1)}, f32[2,64,256]{2,1,0:T(8,128)}, u32[]{:S(2)}) %copy-start) | copy-done | bytes 131096
  0.9 0.7 shard_map.100
  1.6 10.0 %all-to-all-start = ((f32[16,16,128]{2,1,0:T(8,128)}), f32[16,16,128]{2,1,0:T(8,128)S(1)}, u32[]{:S(2)}, u32[]{:S(2)}) async-start(f32[16,16,128]{2,1,0:T(8,128)} %bitcast), calls=%async_computation | async-start | bytes 262144 | tf_op jit(solution)/shard_map/all_to_all | solution.py:553
  11.6 0.8 add_bitcast_fusion.packed
  12.4 0.0 copy-start.1
  12.4 2.5 %shard_map.101 = (bf16[2560,256]{1,0:T(8,128)(2,1)S(1)}, f32[2136,128]{1,0:T(8,128)S(1)}) custom-call(f32[106,128]{1,0:T(8,128)S(1)} %add_bitcast_fusion.packed), custom_call_target="tpu_custom_call" | custom-call | flops 4000000000 | bytes 54272 | tf_op jit(solution)/shard_map/pallas_call | solution.py:466
  14.9 5.8 %all-to-all-done = f32[16,16,128]{2,1,0:T(8,128)S(1)} async-done(((f32[16,16,128]{2,1,0:T(8,128)}), f32[16,16,128]{2,1,0:T(8,128)S(1)}, u32[]{:S(2)}, u32[]{:S(2)}) %all-to-all-start) | async-done | bytes 131104 | tf_op jit(solution)/shard_map/all_to_all | solution.py:553
  20.7 0.0 copy-done.1
  20.7 1.5 %shard_map.102 = f32[1024,128]{1,0:T(8,128)S(1)} custom-call(f32[256,128]{1,0:T(8,128)S(1)} %bitcast.18, bf16[2560,256]{1,0:T(8,128)(2,1)S(1)} %get-tuple-element.7.tables, f32[2136,128]{1,0:T(8,128)S(1)} %get-tuple-element.8.later, bf16[512,768]{1,0:T(8,128)(2,1)S(1)} %copy-done.1), custom_call_target="tpu_custom_call" | custom-call | flops 1500000000 | bytes 3321856 | tf_op jit(solution)/shard_map/pallas_call | solution.py:466
  22.2 29.5 %all_to_all.26 = f32[256,4,128]{2,1,0:T(4,128)S(1)} all-to-all(f32[256,4,128]{2,1,0:T(4,128)S(1)} %bitcast.16), channel_id=1, replica_groups=mesh['lat'=16,'tm'=16] {'lat','tm'}, dimensions={0} | all-to-all | bytes 1048576 | tf_op jit(solution)/shard_map/all_to_all | solution.py:565
  51.8 0.0 copy-start.2
  51.8 0.0 copy-start.3
  51.8 2.9 %shard_map.103 = f32[256,128]{1,0:T(8,128)S(1)} custom-call(f32[1024,128]{1,0:T(8,128)S(1)} %bitcast.15, bf16[512,768]{1,0:T(8,128)(2,1)S(1)} %copy-done.1, bf16[2560,256]{1,0:T(8,128)(2,1)S(1)} %get-tuple-element.7.tables, f32[2136,128]{1,0:T(8,128)S(1)} %get-tuple-element.8.later), custom_call_target="tpu_custom_call" | custom-call | flops 3000000000 | bytes 3715072 | tf_op jit(solution)/shard_map/pallas_call | solution.py:466
  54.7 18.1 %all_to_all.27 = f32[256,1,128]{2,1,0:T(1,128)S(1)} all-to-all(f32[256,1,128]{2,1,0:T(1,128)S(1)} %bitcast.21), channel_id=1, replica_groups=mesh['lat'=16,'tm'=16] {'lat','tm'}, dimensions={0} | all-to-all | bytes 262144 | tf_op jit(solution)/shard_map/all_to_all | solution.py:570
  72.8 0.0 copy-done.2
  72.8 0.0 copy-done.3
  72.8 2.2 %shard_map.104 = f32[256,128]{1,0:T(8,128)S(1)} custom-call(f32[256,128]{1,0:T(8,128)S(1)} %bitcast.19, bf16[2560,256]{1,0:T(8,128)(2,1)S(1)} %get-tuple-element.7.tables, f32[2136,128]{1,0:T(8,128)S(1)} %get-tuple-element.8.later, bf16[1536,256]{1,0:T(8,128)(2,1)S(1)} %copy-done.2, f32[768,128]{1,0:T(8,128)S(1)} %copy-done.3), custom_call_target="tpu_custom_call" | custom-call | flops 2300000000 | bytes 3715072 | tf_op jit(solution)/shard_map/pallas_call | solution.py:466
  75.0 12.5 %all_to_all.28 = f32[16,16,128]{2,1,0:T(8,128)S(1)} all-to-all(f32[16,16,128]{2,1,0:T(8,128)S(1)} %bitcast.20), channel_id=1, replica_groups=mesh['lat'=16,'tm'=16] {'tm'}, dimensions={0} | all-to-all | bytes 262144 | tf_op jit(solution)/shard_map/all_to_all | solution.py:575
  87.5 0.7 shard_map.105
Async XLA Ops:
  0.0 0.9 %copy-start = (f32[2,64,256]{2,1,0:T(8,128)S(1)}, f32[2,64,256]{2,1,0:T(8,128)}, u32[]{:S(2)}) copy-start(f32[2,64,256]{2,1,0:T(8,128)} %field.1) | copy-start | bytes 393220
  1.6 19.1 %all-to-all-start = ((f32[16,16,128]{2,1,0:T(8,128)}), f32[16,16,128]{2,1,0:T(8,128)S(1)}, u32[]{:S(2)}, u32[]{:S(2)}) async-start(f32[16,16,128]{2,1,0:T(8,128)} %bitcast), calls=%async_computation | async-start | bytes 262144 | tf_op jit(solution)/shard_map/all_to_all | solution.py:553
  12.4 8.3 %copy-start.1 = (bf16[512,768]{1,0:T(8,128)(2,1)S(1)}, bf16[512,768]{1,0:T(8,128)(2,1)}, u32[]{:S(2)}) copy-start(bf16[512,768]{1,0:T(8,128)(2,1)} %constant.10.clone.ahead) | copy-start | bytes 2359300
  51.8 21.0 %copy-start.2 = (bf16[1536,256]{1,0:T(8,128)(2,1)S(1)}, bf16[1536,256]{1,0:T(8,128)(2,1)}, u32[]{:S(2)}) copy-start(bf16[1536,256]{1,0:T(8,128)(2,1)} %constant.11.clone.back) | copy-start | bytes 2359300
  51.8 21.0 %copy-start.3 = (f32[768,128]{1,0:T(8,128)S(1)}, f32[768,128]{1,0:T(8,128)}, u32[]{:S(2)}) copy-start(f32[768,128]{1,0:T(8,128)} %constant.12.clone.shift) | copy-start | bytes 1179652

commit v7 on v6

--- a/solution.py
+++ b/solution.py
@@ -328,7 +328,7 @@
         total = jnp.zeros((BINS, 128), F32)
         for w1 in range(16):
             start = (part * 16 + w1) * BINS
-            total = total + jnp.where(lane == w1, product[start : start + BINS], 0.0)
+            total = jnp.where(lane == w1, product[start : start + BINS], total)
         sums.append(total)
     return sums[0] + half_sign((BINS, 128)) * roll(sums[1], 64)
 
@@ -419,7 +419,8 @@
         half_sign((BINS, 128)) * roll(state, 64)
     )
     gather = (iota((128, 128), 0) // 16 == iota((128, 128), 1) // 16).astype(BF16)
-    spread = sum(dot_nt(gather, jnp.concatenate([part] * 16, 0)) for part in thirds(state))
+    spread = sum(dot_nt(gather, jnp.concatenate([part] * 4, 0)) for part in thirds(state))
+    spread = jnp.concatenate([spread] * 4, 1)
     couple_grid = jnp.concatenate([third[64 * k : 64 * k + 64] for k in range(4)], 1)
     k_re, k_im = couple_grid * spread[:64], couple_grid * spread[64:]
     left = jnp.concatenate(

time: 88.5 us -> 88.5 us (level)
  no operation moved by 1% of the time
where the time goes in v7:
time: 88.5 us; the launch traced here: 88.2 us
  blocking collectives  60.2 us (68%)
  Pallas kernels  10.5 us (12%)
  starting transfers between devices  9.98 us (11%)
  waiting for transfers between devices  5.78 us (7%)
  local copies, waits for them, and re-layouts  0.91 us (1%)
    all_to_all x1, blocking collectives, on_device(): lax.all_to_all(message.reshape(256, 4, 128), BOTH, 0, 0, tiled=True)  29.5 us
    all_to_all x1, blocking collectives, on_device(): spectrum = lax.all_to_all(columns, BOTH, 0, 0, tiled=True)  18.1 us
    all_to_all x1, blocking collectives, on_device(): lax.all_to_all(finished.reshape(16, 16, 128), 'tm', 0, 0, tiled=True)  12.5 us
    pallas_call x6, Pallas kernels, call(): pl.pallas_call(kernel, out_shape=out_shape, in_specs=in_specs, out_specs=...  10.5 us
    all_to_all x1, starting transfers between devices, on_device(): rows = lax.all_to_all(rows.reshape(16, 16, 128), 'tm', 0, 0, tiled=True)  9.98 us
    all_to_all x1, waiting for transfers between devices, on_device(): rows = lax.all_to_all(rows.reshape(16, 16, 128), 'tm', 0, 0, tiled=True)  5.78 us
  transfers between devices with their start and end apart: 1, of which 1 were waited for; matrix products, arithmetic and copies ran while one was open for 1% of the time, Pallas kernels for 3%

profile of v7, /device:TPU:1, one launch (start us, length us, event | category | flops | bytes accessed | tf_op | source)
XLA Modules:
  0.0 88.2 jit_solution(384408404257241297)
XLA Ops:
  0.0 0.0 copy-start
  0.0 0.9 %copy-done = f32[2,64,256]{2,1,0:T(8,128)S(1)} copy-done((f32[2,64,256]{2,1,0:T(8,128)S(1)}, f32[2,64,256]{2,1,0:T(8,128)}, u32[]{:S(2)}) %copy-start) | copy-done | bytes 131096
  0.9 0.7 shard_map.100
  1.6 10.0 %all-to-all-start = ((f32[16,16,128]{2,1,0:T(8,128)}), f32[16,16,128]{2,1,0:T(8,128)S(1)}, u32[]{:S(2)}, u32[]{:S(2)}) async-start(f32[16,16,128]{2,1,0:T(8,128)} %bitcast), calls=%async_computation | async-start | bytes 262144 | tf_op jit(solution)/shard_map/all_to_all | solution.py:554
  11.6 0.8 add_bitcast_fusion.packed
  12.4 0.0 copy-start.1
  12.4 2.5 %shard_map.101 = (bf16[2560,256]{1,0:T(8,128)(2,1)S(1)}, f32[2136,128]{1,0:T(8,128)S(1)}) custom-call(f32[106,128]{1,0:T(8,128)S(1)} %add_bitcast_fusion.packed), custom_call_target="tpu_custom_call" | custom-call | flops 4000000000 | bytes 54272 | tf_op jit(solution)/shard_map/pallas_call | solution.py:467
  14.9 5.8 %all-to-all-done = f32[16,16,128]{2,1,0:T(8,128)S(1)} async-done(((f32[16,16,128]{2,1,0:T(8,128)}), f32[16,16,128]{2,1,0:T(8,128)S(1)}, u32[]{:S(2)}, u32[]{:S(2)}) %all-to-all-start) | async-done | bytes 131104 | tf_op jit(solution)/shard_map/all_to_all | solution.py:554
  20.7 0.0 copy-done.1
  20.7 1.5 %shard_map.102 = f32[1024,128]{1,0:T(8,128)S(1)} custom-call(f32[256,128]{1,0:T(8,128)S(1)} %bitcast.18, bf16[2560,256]{1,0:T(8,128)(2,1)S(1)} %get-tuple-element.7.tables, f32[2136,128]{1,0:T(8,128)S(1)} %get-tuple-element.8.later, bf16[512,768]{1,0:T(8,128)(2,1)S(1)} %copy-done.1), custom_call_target="tpu_custom_call" | custom-call | flops 1500000000 | bytes 3321856 | tf_op jit(solution)/shard_map/pallas_call | solution.py:467
  22.2 29.5 %all_to_all.26 = f32[256,4,128]{2,1,0:T(4,128)S(1)} all-to-all(f32[256,4,128]{2,1,0:T(4,128)S(1)} %bitcast.16), channel_id=1, replica_groups=mesh['lat'=16,'tm'=16] {'lat','tm'}, dimensions={0} | all-to-all | bytes 1048576 | tf_op jit(solution)/shard_map/all_to_all | solution.py:566
  51.8 0.0 copy-start.2
  51.8 0.0 copy-start.3
  51.8 2.9 %shard_map.103 = f32[256,128]{1,0:T(8,128)S(1)} custom-call(f32[1024,128]{1,0:T(8,128)S(1)} %bitcast.15, bf16[512,768]{1,0:T(8,128)(2,1)S(1)} %copy-done.1, bf16[2560,256]{1,0:T(8,128)(2,1)S(1)} %get-tuple-element.7.tables, f32[2136,128]{1,0:T(8,128)S(1)} %get-tuple-element.8.later), custom_call_target="tpu_custom_call" | custom-call | flops 3000000000 | bytes 3715072 | tf_op jit(solution)/shard_map/pallas_call | solution.py:467
  54.6 18.1 %all_to_all.27 = f32[256,1,128]{2,1,0:T(1,128)S(1)} all-to-all(f32[256,1,128]{2,1,0:T(1,128)S(1)} %bitcast.21), channel_id=1, replica_groups=mesh['lat'=16,'tm'=16] {'lat','tm'}, dimensions={0} | all-to-all | bytes 262144 | tf_op jit(solution)/shard_map/all_to_all | solution.py:571
  72.8 0.0 copy-done.2
  72.8 0.0 copy-done.3
  72.8 2.2 %shard_map.104 = f32[256,128]{1,0:T(8,128)S(1)} custom-call(f32[256,128]{1,0:T(8,128)S(1)} %bitcast.19, bf16[2560,256]{1,0:T(8,128)(2,1)S(1)} %get-tuple-element.7.tables, f32[2136,128]{1,0:T(8,128)S(1)} %get-tuple-element.8.later, bf16[1536,256]{1,0:T(8,128)(2,1)S(1)} %copy-done.2, f32[768,128]{1,0:T(8,128)S(1)} %copy-done.3), custom_call_target="tpu_custom_call" | custom-call | flops 2300000000 | bytes 3715072 | tf_op jit(solution)/shard_map/pallas_call | solution.py:467
  75.0 12.5 %all_to_all.28 = f32[16,16,128]{2,1,0:T(8,128)S(1)} all-to-all(f32[16,16,128]{2,1,0:T(8,128)S(1)} %bitcast.20), channel_id=1, replica_groups=mesh['lat'=16,'tm'=16] {'tm'}, dimensions={0} | all-to-all | bytes 262144 | tf_op jit(solution)/shard_map/all_to_all | solution.py:576
  87.5 0.7 shard_map.105
Async XLA Ops:
  0.0 0.9 %copy-start = (f32[2,64,256]{2,1,0:T(8,128)S(1)}, f32[2,64,256]{2,1,0:T(8,128)}, u32[]{:S(2)}) copy-start(f32[2,64,256]{2,1,0:T(8,128)} %field.1) | copy-start | bytes 393220
  1.6 19.1 %all-to-all-start = ((f32[16,16,128]{2,1,0:T(8,128)}), f32[16,16,128]{2,1,0:T(8,128)S(1)}, u32[]{:S(2)}, u32[]{:S(2)}) async-start(f32[16,16,128]{2,1,0:T(8,128)} %bitcast), calls=%async_computation | async-start | bytes 262144 | tf_op jit(solution)/shard_map/all_to_all | solution.py:554
  12.4 8.3 %copy-start.1 = (bf16[512,768]{1,0:T(8,128)(2,1)S(1)}, bf16[512,768]{1,0:T(8,128)(2,1)}, u32[]{:S(2)}) copy-start(bf16[512,768]{1,0:T(8,128)(2,1)} %constant.10.clone.ahead) | copy-start | bytes 2359300
  51.8 21.0 %copy-start.2 = (bf16[1536,256]{1,0:T(8,128)(2,1)S(1)}, bf16[1536,256]{1,0:T(8,128)(2,1)}, u32[]{:S(2)}) copy-start(bf16[1536,256]{1,0:T(8,128)(2,1)} %constant.11.clone.back) | copy-start | bytes 2359300
  51.8 21.0 %copy-start.3 = (f32[768,128]{1,0:T(8,128)S(1)}, f32[768,128]{1,0:T(8,128)}, u32[]{:S(2)}) copy-start(f32[768,128]{1,0:T(8,128)} %constant.12.clone.shift) | copy-start | bytes 1179652
